TPU v7x, 32 devices: a whole 2x2x4 slice. The times are simulated.
32 devices in a mesh: feat: 8 (over z, core), dp: 4 (over y, x).
Axes of the slice: x: 2, y: 2, z: 4, core: 2. Of those that a mesh axis runs over, the one named last changes fastest.
Arguments:
- features: bfloat16 [4, 1024, 256], P('dp', 'feat'), may hold values from -6 to 6
- neigh_lists: int32 [4, 10, 128], P('dp'), may hold values from 0 to 255
- w1_self: bfloat16 [1024, 512], P('feat'), may hold values from -0.125 to 0.125
- w1_neigh: bfloat16 [1024, 512], P('feat'), may hold values from -0.125 to 0.125
- w2_self: bfloat16 [512, 512], replicated, may hold values from -0.1875 to 0.1875
- w2_neigh: bfloat16 [512, 512], replicated, may hold values from -0.1875 to 0.1875
- send_rows: int32 [4, 8, 4, 8], P('dp', 'feat'), may hold values from 0 to 15
- send_count: int32 [4, 8, 4], P('dp', 'feat'), may hold values from 1 to 8, as said below
- recv_target: int32 [4, 8, 4, 8], P('dp', 'feat'), may hold values from 0 to 15
- out_grad: bfloat16 [4, 8, 16, 512], P('dp', 'feat'), may hold values from -6 to 6
Outputs:
- layer_out: bfloat16 [4, 8, 16, 512], P('dp', 'feat')
- grad_w1_self: float32 [4, 1024, 512], P('dp', 'feat')
- grad_w1_neigh: float32 [4, 1024, 512], P('dp', 'feat')
Inputs may be any that keep to these rules, and one draw needn't show every extreme that they name: `send_count`: for each feat index one data index, drawn from the seed, receives 8 live slots from every data peer; every other count is at most 4. `recv_target`: slots at or beyond the sending device's count carry nothing.
All inputs are finite; a program needn't handle non-finite values.
Results may differ from a plain program's by a relative error of at most 0.0277.
Values may be sent and summed in bfloat16 or wider, within the bound.
No kernel may reach another device: no remote copies, remote signals or barrier semaphores. Data moves between devices by JAX's collectives and lax.ppermute only.
A program may use at most 64 MiB of HBM per device.

v0:
```python
import jax
import jax.numpy as jnp
from jax import lax
from jax.sharding import PartitionSpec as P

K1 = 10


def on_device(
    features,
    neigh_lists,
    w1_self,
    w1_neigh,
    w2_self,
    w2_neigh,
    send_rows,
    send_count,
    recv_target,
    out_grad,
):
    columns = features[0]
    neighbour_lists = neigh_lists[0]
    group_rows = neighbour_lists.shape[1]
    self_cols = columns[:, :group_rows]
    gathered = jnp.take(columns, neighbour_lists, axis=1)
    mean_cols = (jnp.sum(gathered, axis=1, dtype=jnp.float32) / K1).astype(jnp.bfloat16)
    feat_count = lax.axis_size("feat")
    rows_dev = group_rows // feat_count
    width = w1_self.shape[1]
    contract = (((0,), (0,)), ((), ()))
    part_self = self_cols
    part_mean = mean_cols
    term = lax.dot_general(part_self, w1_self, contract, preferred_element_type=jnp.float32)
    preact = lax.psum_scatter(
        term + lax.dot_general(part_mean, w1_neigh, contract, preferred_element_type=jnp.float32),
        "feat",
        scatter_dimension=0,
        tiled=True,
    )
    hidden = jnp.maximum(preact, 0.0).astype(jnp.bfloat16)
    dp_count = lax.axis_size("dp")
    rows_out = send_rows[0, 0]
    slot_count = rows_out.shape[1]
    outgoing = jnp.take(hidden, rows_out, axis=0)
    counts_out = send_count[0, 0].astype(jnp.bfloat16).reshape(dp_count, 1)
    incoming, counts_in = (
        lax.all_to_all(outgoing, "dp", split_axis=0, concat_axis=0, tiled=True),
        lax.all_to_all(counts_out, "dp", split_axis=0, concat_axis=0, tiled=True),
    )
    slot_ids = lax.broadcasted_iota(jnp.int32, (dp_count, slot_count), 1)
    usable = slot_ids < counts_in.astype(jnp.int32)
    targets = recv_target[0, 0]
    row_ids = lax.broadcasted_iota(jnp.int32, (rows_dev, dp_count * slot_count), 0)
    chosen = (row_ids == targets.reshape(1, -1)) & usable.reshape(1, -1)
    onehot = chosen.astype(jnp.bfloat16)
    neigh_sum = jnp.dot(
        onehot, incoming.reshape(dp_count * slot_count, width), preferred_element_type=jnp.float32
    )
    degree = jnp.sum(chosen.astype(jnp.float32), axis=1, keepdims=True)
    mean_two = ((hidden.astype(jnp.float32) + neigh_sum) / (1.0 + degree)).astype(jnp.bfloat16)
    layer_out = jnp.dot(hidden, w2_self, preferred_element_type=jnp.float32)
    layer_out = (
        layer_out + jnp.dot(mean_two, w2_neigh, preferred_element_type=jnp.float32)
    ).astype(jnp.bfloat16)
    upstream = out_grad[0, 0]
    transposed = (((1,), (1,)), ((), ()))
    grad_self = lax.dot_general(upstream, w2_self, transposed, preferred_element_type=jnp.float32)
    grad_mean = lax.dot_general(
        upstream, w2_neigh, transposed, preferred_element_type=jnp.float32
    ) / (1.0 + degree)
    returning = jnp.where(usable[..., None], jnp.take(grad_mean, targets, axis=0), 0.0)
    arrived = lax.all_to_all(
        returning.astype(jnp.bfloat16), "dp", split_axis=0, concat_axis=0, tiled=True
    ).astype(returning.dtype)
    own_table = (row_ids == rows_out.reshape(1, -1)).astype(jnp.float32)
    from_peers = jnp.dot(
        own_table, arrived.reshape(dp_count * slot_count, width), precision=lax.Precision.HIGHEST
    )
    grad_hidden = grad_self + grad_mean + from_peers
    grad_pre = jnp.where(preact > 0, grad_hidden, 0.0).astype(jnp.bfloat16)
    block_rows = lax.all_gather(grad_pre, "feat", axis=0, tiled=True)
    part_self = self_cols
    part_mean = mean_cols
    first = jnp.dot(part_self, block_rows, preferred_element_type=jnp.float32)
    second = jnp.dot(part_mean, block_rows, preferred_element_type=jnp.float32)
    return (layer_out[None, None], first[None], second[None])


def solution(mesh):
    in_specs = (
        P("dp", "feat", None),
        P("dp", None, None),
        P("feat", None),
        P("feat", None),
        P(),
        P(),
        P("dp", "feat", None, None),
        P("dp", "feat", None),
        P("dp", "feat", None, None),
        P("dp", "feat", None, None),
    )
    out_specs = (P("dp", "feat", None, None), P("dp", "feat", None), P("dp", "feat", None))
    return jax.shard_map(
        on_device, mesh=mesh, in_specs=in_specs, out_specs=out_specs, check_vma=False
    )
```

profile of v0, /device:TPU:0, one launch (start us, length us, event | category | flops | bytes accessed | tf_op | source)
XLA Modules:
  0.0 77.0 jit_solution(17144897814878926038)
XLA Ops:
  7.2 0.8 %fusion.21 = s32[10,128]{1,0:T(8,128)S(1)} fusion(s32[1,10,128]{2,0,1:T(1,128)} %param.11), kind=kLoop, calls=%fused_computation.45 | loop fusion | flops 3840 | bytes 10240 | tf_op jit(solution)/shard_map/jit(_take)/jit(_where)/select_n | solution.py:25
  8.1 1.0 %copy.21 = bf16[1,128,256]{1,2,0:T(8,128)(2,1)S(1)} copy(bf16[1,128,256]{2,1,0:T(8,128)(2,1)} %param.10) | data formatting | bytes 131072 | tf_op args[0]
  9.2 2.8 %gather_fusion = bf16[1280,128]{1,0:T(8,128)(2,1)S(1)} fusion(bf16[128,256]{0,1:T(8,128)(2,1)S(1)} %bitcast.65, s32[2048]{0:T(1024)S(1)} %pad_clamp_fusion), kind=kCustom, calls=%fused_computation | custom fusion | bytes 660480 | tf_op jit(solution)/shard_map/jit(_take)/gather | solution.py:25
  12.0 0.2 convert_reduce_fusion
  12.3 0.7 copy-done.4
  12.9 0.9 %convolution_add_fusion = f32[128,512]{1,0:T(8,128)} fusion(f32[128,512]{1,0:T(8,128)S(1)} %fusion.13, bf16[128,512]{1,0:T(8,128)(2,1)S(1)} %copy-done.4, f32[128,128]{1,0:T(8,128)S(1)} %convert_reduce_fusion), kind=kOutput, calls=%fused_computation.3 | convolution fusion | flops 16875520 | bytes 720896 | tf_op jit(solution)/shard_map/dot_general | solution.py:35
  13.8 0.6 copy-done.9
  14.5 0.7 copy.22
  15.2 5.3 %all-to-all-start = ((bf16[4,1,1]{2,1,0:T(2,128)(2,1)}), bf16[4,1,1]{2,1,0:T(2,128)(2,1)S(1)}, u32[]{:S(2)}, u32[]{:S(2)}) async-start(bf16[4,1,1]{2,1,0:T(2,128)(2,1)} %copy.22), calls=%async_computation.1 | async-start | bytes 4096 | tf_op jit(solution)/shard_map/all_to_all | solution.py:48
  20.5 0.7 copy-done.7
  21.5 3.5 %all-to-all-done = bf16[4,1,1]{2,1,0:T(2,128)(2,1)S(1)} async-done(((bf16[4,1,1]{2,1,0:T(2,128)(2,1)}), bf16[4,1,1]{2,1,0:T(2,128)(2,1)S(1)}, u32[]{:S(2)}, u32[]{:S(2)}) %all-to-all-start) | async-done | bytes 40 | tf_op jit(solution)/shard_map/all_to_all | solution.py:48
  25.5 0.2 convolution_divide_fusion
  25.7 0.6 gather_fusion.2
  26.4 0.7 fusion.7
  27.1 3.3 %all-to-all-start.2 = ((bf16[4,8,512]{2,1,0:T(8,128)(2,1)}), bf16[4,8,512]{2,1,0:T(8,128)(2,1)S(1)}, u32[]{:S(2)}, u32[]{:S(2)}) async-start(bf16[4,8,512]{2,1,0:T(8,128)(2,1)} %fusion.7), calls=%async_computation.3 | async-start | bytes 65536 | tf_op jit(solution)/shard_map/all_to_all | solution.py:72
  30.6 16.5 %reduce-scatter.2.cloned.1.call-done = f32[16,512]{1,0:T(8,128)} async-done(((f32[128,512]{1,0:T(8,128)}), f32[16,512]{1,0:T(8,128)}) %reduce-scatter.2.cloned.1.call-update) | async-done | bytes 32784 | tf_op jit(solution)/shard_map/reduce_scatter | solution.py:34
  47.1 0.8 maximum_convert_fusion
  48.1 0.6 gather_fusion.1
  48.7 0.7 bitcast_select_fusion.1
  49.4 3.8 %all-to-all-start.1 = ((bf16[4,8,512]{2,1,0:T(8,128)(2,1)}), bf16[4,8,512]{2,1,0:T(8,128)(2,1)S(1)}, u32[]{:S(2)}, u32[]{:S(2)}) async-start(bf16[4,8,512]{2,1,0:T(8,128)(2,1)} %bitcast_select_fusion.1), calls=%async_computation.2 | async-start | bytes 65536 | tf_op jit(solution)/shard_map/all_to_all | solution.py:47
  53.3 13.9 %all_gather.3 = bf16[128,512]{1,0:T(8,128)(2,1)S(1)} all-gather(bf16[16,512]{1,0:T(8,128)(2,1)S(1)} %fusion.3), channel_id=1, replica_groups=mesh['feat'=8,'dp'=4] {'feat'}, dimensions={0}, use_global_device_ids=true | all-gather | bytes 147456 | tf_op jit(solution)/shard_map/all_gather | solution.py:81
  67.3 0.9 %convolution_bitcast_fusion = f32[1,128,512]{2,1,0:T(8,128)} fusion(bf16[128,512]{1,0:T(8,128)(2,1)S(1)} %all_gather.3, f32[128,128]{1,0:T(8,128)S(1)} %convert_reduce_fusion), kind=kOutput, calls=%fused_computation.4 | convolution fusion | flops 16809984 | bytes 458752 | tf_op jit(solution)/shard_map/dot_general | solution.py:85
  68.4 0.8 %copy.23 = f32[1,128,512]{2,1,0:T(8,128)} copy(f32[1,128,512]{1,2,0:T(8,128)S(1)} %convolution_bitcast_fusion.1) | data formatting | bytes 524288
  69.2 0.9 %fusion.5 = bf16[1,1,16,512]{3,2,1,0:T(8,128)(2,1)} fusion(f32[16,512]{1,0:T(8,128)S(1)} %fusion.29, bf16[512,512]{1,0:T(8,128)(2,1)S(1)} %copy-done.1, bf16[4,8,512]{2,1,0:T(8,128)(2,1)S(1)} %all-to-all-done.1, bf16[16,512]{1,0:T(8,128)(2,1)S(1)} %maximum_convert_fusion, f32[16]{0:T(128)S(1)} %broadcast_add_fusion, s32[32]{0:T(128)S(1)} %eq.20, ...), kind=kOutput, calls=%fused_computation.16 | convolution fusion | flops 8963072 | bytes 622816 | tf_op jit(solution)/shard_map/dot_general | solution.py:63
  (44 shorter events, 1.8 us)
Async XLA Ops:
  7.2 23.2 %copy-start = (bf16[512,512]{1,0:T(8,128)(2,1)S(1)}, bf16[512,512]{1,0:T(8,128)(2,1)}, u32[]{:S(2)}) copy-start(bf16[512,512]{1,0:T(8,128)(2,1)} %param.14) | copy-start | bytes 1572868
  7.2 0.9 %copy-start.6 = (s32[1,10,128]{2,0,1:T(1,128)S(1)}, s32[1,10,128]{2,0,1:T(1,128)}, u32[]{:S(2)}) copy-start(s32[1,10,128]{2,0,1:T(1,128)} %param.11) | copy-start | bytes 15364
  7.2 1.8 %copy-start.3 = (bf16[128,512]{1,0:T(8,128)(2,1)S(1)}, bf16[128,512]{1,0:T(8,128)(2,1)}, u32[]{:S(2)}) copy-start(bf16[128,512]{1,0:T(8,128)(2,1)} %param.12) | copy-start | bytes 393220
  7.2 39.9 %reduce-scatter.2.cloned.1.call-start = ((), (), s32[]{:S(2)}) async-start(), calls=%async_computation.4 | async-start | bytes 294912 | tf_op jit(solution)/shard_map/reduce_scatter | solution.py:34
  12.0 0.9 %copy-start.4 = (bf16[128,512]{1,0:T(8,128)(2,1)S(1)}, bf16[128,512]{1,0:T(8,128)(2,1)}, u32[]{:S(2)}) copy-start(bf16[128,512]{1,0:T(8,128)(2,1)} %param.13) | copy-start | bytes 393220
  12.9 12.6 %copy-start.1 = (bf16[512,512]{1,0:T(8,128)(2,1)S(1)}, bf16[512,512]{1,0:T(8,128)(2,1)}, u32[]{:S(2)}) copy-start(bf16[512,512]{1,0:T(8,128)(2,1)} %param.15) | copy-start | bytes 1572868
  13.8 0.7 copy-start.9
  15.2 5.3 %copy-start.8 = (s32[1,1,4,8]{3,2,1,0:T(4,128)S(1)}, s32[1,1,4,8]{3,2,1,0:T(4,128)}, u32[]{:S(2)}) copy-start(s32[1,1,4,8]{3,2,1,0:T(4,128)} %param.16) | copy-start | bytes 388
  15.2 9.9 %all-to-all-start = ((bf16[4,1,1]{2,1,0:T(2,128)(2,1)}), bf16[4,1,1]{2,1,0:T(2,128)(2,1)S(1)}, u32[]{:S(2)}, u32[]{:S(2)}) async-start(bf16[4,1,1]{2,1,0:T(2,128)(2,1)} %copy.22), calls=%async_computation.1 | async-start | bytes 4096 | tf_op jit(solution)/shard_map/all_to_all | solution.py:48
  20.5 0.7 copy-start.7
  21.2 4.3 %copy-start.5 = (bf16[1,1,16,512]{3,2,1,0:T(8,128)(2,1)S(1)}, bf16[1,1,16,512]{3,2,1,0:T(8,128)(2,1)}, u32[]{:S(2)}) copy-start(bf16[1,1,16,512]{3,2,1,0:T(8,128)(2,1)} %param.19) | copy-start | bytes 49156
  27.1 22.3 %all-to-all-start.2 = ((bf16[4,8,512]{2,1,0:T(8,128)(2,1)}), bf16[4,8,512]{2,1,0:T(8,128)(2,1)S(1)}, u32[]{:S(2)}, u32[]{:S(2)}) async-start(bf16[4,8,512]{2,1,0:T(8,128)(2,1)} %fusion.7), calls=%async_computation.3 | async-start | bytes 65536 | tf_op jit(solution)/shard_map/all_to_all | solution.py:72
  49.4 3.8 %copy-start.2 = (f32[16,512]{1,0:T(8,128)S(1)}, f32[16,512]{1,0:T(8,128)}, u32[]{:S(2)}) copy-start(f32[16,512]{1,0:T(8,128)} %reduce-scatter.2.cloned.1.call-done) | copy-start | bytes 98308
  49.4 19.9 %all-to-all-start.1 = ((bf16[4,8,512]{2,1,0:T(8,128)(2,1)}), bf16[4,8,512]{2,1,0:T(8,128)(2,1)S(1)}, u32[]{:S(2)}, u32[]{:S(2)}) async-start(bf16[4,8,512]{2,1,0:T(8,128)(2,1)} %bitcast_select_fusion.1), calls=%async_computation.2 | async-start | bytes 65536 | tf_op jit(solution)/shard_map/all_to_all | solution.py:47
Sparse Core Ops, SparseCore 0:
  14.0 33.1 reduce-scatter.1
where the time goes:
time: 77.5 us; the launch traced here: 77 us
  waiting for transfers between devices  20.1 us (26%)
  between operations  14.2 us (18%)
  blocking collectives  13.9 us (18%)
  starting transfers between devices  12.4 us (16%)
  local copies, waits for them, and re-layouts  8.95 us (12%)
  matrix products  3.8 us (5%)
  other arithmetic  3.58 us (5%)
    reduce_scatter x1, waiting for transfers between devices, on_device(): lax.psum_scatter(term + lax.dot_general(part_mean, w1_neigh, contract, pr...  16.5 us
    all_gather x1, blocking collectives, on_device(): block_rows = lax.all_gather(grad_pre, 'feat', axis=0, tiled=True)  13.9 us
    all_to_all x1, starting transfers between devices, on_device(): lax.all_to_all(counts_out, 'dp', split_axis=0, concat_axis=0, tiled=True)  5.29 us
    all_to_all x1, starting transfers between devices, on_device(): lax.all_to_all(outgoing, 'dp', split_axis=0, concat_axis=0, tiled=True)  3.81 us
    unnamed x22, local copies, waits for them, and re-layouts  3.77 us
    all_to_all x1, waiting for transfers between devices, on_device(): lax.all_to_all(counts_out, 'dp', split_axis=0, concat_axis=0, tiled=True)  3.51 us
    all_to_all x1, starting transfers between devices, on_device(): lax.all_to_all(returning.astype(jnp.bfloat16), 'dp', split_axis=0, concat...  3.26 us
    gather x1, local copies, waits for them, and re-layouts, on_device(): gathered = jnp.take(columns, neighbour_lists, axis=1)  2.81 us
  transfers between devices with their start and end apart: 4, of which 2 were waited for; matrix products, arithmetic and copies ran while one was open for 10% of the time, Pallas kernels for 0%

commit v1 on v0

v1 whole, which is shorter than its diff:
```python
import functools

import jax
import jax.numpy as jnp
from jax import lax
from jax.experimental import pallas as pl
from jax.experimental.pallas import tpu as pltpu
from jax.sharding import PartitionSpec as P

K1 = 10
HIDDEN_COST = 3 * 10**8
OWN_COST = 10**8
BACKWARD_COST = 10**10
INDEX_COST = 10**8
F32 = jnp.float32
BF16 = jnp.bfloat16
NT = (((1,), (1,)), ((), ()))
TN = (((0,), (0,)), ((), ()))
VMEM = pl.BlockSpec(memory_space=pltpu.VMEM)
PARAMS = pltpu.CompilerParams(vmem_limit_bytes=12 * 1024 * 1024)


def iota(shape, dim):
    return lax.broadcasted_iota(jnp.int32, shape, dim)


def table_lanes(peers, slots):
    return -(-3 * peers * slots // 128) * 128


def first_layer_kernel(
    feat_hbm, lists_hbm, w1s_hbm, w1n_hbm, rows_hbm, counts_hbm, targets_hbm, og_hbm, w2s_hbm, w2n_hbm,
    keep_ref, send_ref, mean_ref, aux_ref, w2s_ref, w2n_ref,
    feat_ref, lists_ref, w1_ref, rows_ref, counts_ref, targets_ref, og_ref, both_ref, part_ref, sems,
):
    i = pl.program_id(0)
    depth = feat_ref.shape[1]
    pairs = (
        (lists_hbm, lists_ref), (feat_hbm, feat_ref),
        (w1s_hbm, w1_ref.at[0:depth]), (w1n_hbm, w1_ref.at[depth : 2 * depth]),
        (targets_hbm, targets_ref), (rows_hbm, rows_ref), (counts_hbm, counts_ref), (og_hbm, og_ref),
        (w2s_hbm, w2s_ref), (w2n_hbm, w2n_ref),
    )
    copies = [pltpu.make_async_copy(src, dst, sems.at[n]) for n, (src, dst) in enumerate(pairs)]

    def wait(first, last):
        @pl.when(i == 0)
        def _():
            for copy in copies[first:last]:
                copy.wait()

    @pl.when(i == 0)
    def _():
        for copy in copies:
            copy.start()

    core = lax.axis_index("feat") % 2
    nodes = feat_ref.shape[2]
    tile, width = part_ref.shape
    rows_dev = og_ref.shape[2]
    step = min(nodes, 256)
    at_tile = pl.ds(pl.multiple_of(i * tile, tile), tile)
    wait(0, 1)
    hits = []
    for start in range(0, nodes, step):
        ids = iota((step, tile), 0) + start
        times = jnp.zeros((step, tile), F32)
        for k in range(K1):
            times = times + (ids == lists_ref[k, :, at_tile]).astype(F32)
        hits.append(times.astype(BF16))
    wait(1, 2)
    total = jnp.zeros((depth, tile), F32)
    for n, times in enumerate(hits):
        total = total + jnp.dot(
            feat_ref[0, :, n * step : (n + 1) * step], times, preferred_element_type=F32
        )
    mean = (total / K1).astype(BF16)
    mean_ref[...] = mean
    both_ref[0:depth, :] = feat_ref[0, :, at_tile]
    both_ref[depth:, :] = mean
    wait(2, 4)
    part_ref[...] = lax.dot_general(both_ref[...], w1_ref[...], TN, preferred_element_type=F32)
    for z in range(keep_ref.shape[0]):
        for ref, which in ((keep_ref, core), (send_ref, 1 - core)):
            at = pl.multiple_of((2 * z + which) * rows_dev, rows_dev)
            ref[z] = part_ref[pl.ds(at, rows_dev), :]

    @pl.when(i == 0)
    def _():
        for copy in copies[4:]:
            copy.wait()
        peers, slots = rows_ref.shape[2], rows_ref.shape[3]
        lanes = aux_ref.shape[1] - width
        which = iota((slots, lanes), 1) // (peers * slots)
        same_slot = iota((slots, lanes), 1) % slots == iota((slots, lanes), 0)

        def tiled(ref, n):
            spread = (same_slot & (which == n)).astype(BF16)
            return jnp.dot(ref[0, 0].astype(BF16), spread, preferred_element_type=F32)

        eye = iota((peers, peers), 0) == iota((peers, peers), 1)
        column = jnp.sum(jnp.where(eye, counts_ref[0], 0), axis=1, keepdims=True)
        lane = iota((peers, lanes), 1)
        live = (lane // (peers * slots) == 2) & (lane % slots < column)
        tables = tiled(targets_ref, 0) + tiled(rows_ref, 1) + live.astype(F32)
        if peers < rows_dev:
            tables = jnp.concatenate([tables, jnp.zeros((rows_dev - peers, lanes), F32)], axis=0)
        aux_ref[:, :width] = og_ref[0, 0]
        aux_ref[:, width:] = tables.astype(BF16)


def first_layer(features, lists, w1s, w1n, rows, counts, targets, og, w2s, w2n):
    depth = features.shape[1]
    group, width = lists.shape[2], w1s.shape[1]
    lists = lists.reshape(lists.shape[1], 1, group)
    rows_dev = og.shape[2]
    tile = min(group, 128)
    chips = group // (2 * rows_dev)
    tile_chips = tile // (2 * rows_dev)
    aux = (rows_dev, width + table_lanes(*rows.shape[2:]))
    args = (features, lists, w1s, w1n, rows, counts, targets, og, w2s, w2n)
    args = tuple(pltpu.with_memory_space_constraint(a, pltpu.HBM) for a in args)
    half = jax.ShapeDtypeStruct((chips, rows_dev, width), F32)
    half_spec = pl.BlockSpec((tile_chips, rows_dev, width), lambda i: (i, 0, 0))
    whole = lambda shape: pl.BlockSpec(shape, lambda i: (0,) * len(shape))
    scratch = [features, lists, jax.ShapeDtypeStruct((2 * depth, width), BF16), rows, counts, targets, og]
    return pl.pallas_call(
        first_layer_kernel,
        grid=(group // tile,),
        in_specs=[pl.BlockSpec(memory_space=pltpu.HBM)] * len(args),
        out_specs=[
            half_spec, half_spec,
            pl.BlockSpec((depth, tile), lambda i: (0, i)),
            whole(aux), whole(w2s.shape), whole(w2n.shape),
        ],
        out_shape=[
            half, half,
            jax.ShapeDtypeStruct((depth, group), BF16),
            jax.ShapeDtypeStruct(aux, BF16),
            jax.ShapeDtypeStruct(w2s.shape, BF16),
            jax.ShapeDtypeStruct(w2n.shape, BF16),
        ],
        scratch_shapes=[pltpu.VMEM(a.shape, a.dtype) for a in scratch]
        + [pltpu.VMEM((2 * depth, tile), BF16), pltpu.VMEM((tile, width), F32)]
        + [pltpu.SemaphoreType.DMA((len(args),))],
        name="first_layer", compiler_params=PARAMS,
    )(*args)


def call(kernel, name, args, out_shape, cost=0):
    return pl.pallas_call(
        kernel,
        in_specs=[VMEM] * len(args),
        out_specs=[VMEM] * len(out_shape),
        out_shape=[jax.ShapeDtypeStruct(shape, dtype) for shape, dtype in out_shape],
        name=name, compiler_params=PARAMS,
        cost_estimate=pl.CostEstimate(flops=cost, bytes_accessed=0, transcendentals=0),
    )(*args)


def pair_sum_kernel(keep_ref, got_ref, near_ref, far_ref):
    z = lax.axis_index("feat") // 2
    for s in range(keep_ref.shape[0]):
        at = lax.bitwise_xor(z, s)
        (far_ref if s % 2 else near_ref)[s // 2] = keep_ref[at] + got_ref[at]


def pair_sum(keep, got):
    half = ((keep.shape[0] // 2,) + keep.shape[1:], F32)
    return call(pair_sum_kernel, "pair_sum", (keep, got), [half, half])


def fold_kernel(near_ref, got_ref, *outs):
    for s in range(near_ref.shape[0]):
        outs[s % len(outs)][s // len(outs)] = near_ref[s] + got_ref[s]


def fold(near, got, parts):
    out = ((near.shape[0] // parts,) + near.shape[1:], F32)
    return call(fold_kernel, "fold", (near, got), [out] * parts)


def join_kernel(a_ref, b_ref, out_ref):
    count = out_ref.shape[0] // 2
    out_ref[:count] = a_ref[:count]
    out_ref[count:] = b_ref[:count]


def join(a, b, cost=0):
    count = a.shape[0]
    return call(join_kernel, "join", (a, b), [((2 * count,) + a.shape[1:], a.dtype)], cost)[0]


def place(scratch, near, far, size, me):
    count = near.shape[0] // size
    for s in range(2 * count):
        ref, at = (near, s) if s < count else (far, s - count)
        to = pl.multiple_of(lax.bitwise_xor(me, s) * size, size)
        scratch[pl.ds(to, size), :] = ref[at * size : (at + 1) * size, :]


def near_kernel(near_ref, w2s_ref, w2n_ref, self_ref, near_grad_ref):
    rows, width = self_ref.shape
    self_ref[...] = lax.dot_general(near_ref[:rows, :width], w2s_ref[...], NT, preferred_element_type=F32)
    near_grad_ref[...] = lax.dot_general(near_ref[:, :width], w2n_ref[...], NT, preferred_element_type=F32)


def backward_near(near, w2s, w2n, rows_dev):
    width = w2s.shape[0]
    shapes = [((rows_dev, width), F32), ((near.shape[0], width), F32)]
    return call(near_kernel, "backward_near", (near, w2s, w2n), shapes)


def backward_kernel(
    peers, slots, near_ref, far_ref, self_ref, near_grad_ref, w2n_ref, grad_ref, table_ref, degree_ref,
    tables, grads,
):
    me = lax.axis_index("dp")
    rows, width = self_ref.shape
    place(tables, near_ref.at[:, width:], far_ref.at[:, width:], rows, me)
    far_grad = lax.dot_general(far_ref[:, :width], w2n_ref[...], NT, preferred_element_type=F32)
    place(grads, near_grad_ref, far_grad, rows, me)
    lanes = peers * slots

    def table(d, which):
        return tables[d * rows : (d + 1) * rows, which * lanes : (which + 1) * lanes].astype(F32)

    block_of = iota((rows, lanes), 1) // slots
    diagonal = iota((rows, lanes), 0) == block_of
    mine = iota((rows, lanes), 0) == me

    def pick(where, x):
        return jnp.sum(jnp.where(where, x, 0.0), axis=0, keepdims=True)

    def crossed(which):
        return sum(jnp.where(block_of == d, table(d, which), 0.0) for d in range(peers))

    def own(which):
        return sum(jnp.where(me == d, table(d, which), 0.0) for d in range(peers))

    live_in = crossed(2)
    target_there = pick(mine, crossed(0))
    row_there = pick(mine, crossed(1))
    own_target, own_row, own_live = [pick(diagonal, own(which)) for which in range(3)]
    own_live_in = pick(mine, live_in)

    local = iota((rows, lanes), 0).astype(F32)
    every = iota((peers * rows, lanes), 0)
    same = every // rows == iota((peers * rows, lanes), 1) // slots
    every_local = (every % rows).astype(F32)

    back = jnp.where(local == own_row, own_live, 0.0).astype(BF16)
    there = jnp.where(same & (every_local == target_there), 1.0, 0.0).astype(BF16)
    back_table = lax.dot_general(back, there, NT, preferred_element_type=F32)
    into = jnp.where(local == own_target, own_live_in, 0.0)
    origin = jnp.where(same & (every_local == row_there), 1.0, 0.0).astype(BF16)
    table_ref[...] = lax.dot_general(into.astype(BF16), origin, NT, preferred_element_type=F32).astype(BF16)
    degree_ref[...] = jnp.broadcast_to(jnp.sum(into, axis=1, keepdims=True), degree_ref.shape)

    own_columns = iota(back_table.shape, 1) - me * rows
    back_table = back_table + (own_columns == iota(back_table.shape, 0)).astype(F32)
    degrees = []
    for e in range(peers):
        hit = jnp.where(local == pick(diagonal, table(e, 0)), live_in[e : e + 1, :], 0.0)
        degrees.append(jnp.sum(hit, axis=1, keepdims=True))
    grad_mean = grads[...] / (1.0 + jnp.concatenate(degrees, axis=0))
    high = grad_mean.astype(BF16)
    low = (grad_mean - high.astype(F32)).astype(BF16)
    back_table = back_table.astype(BF16)
    grad_hidden = self_ref[...] + jnp.dot(back_table, high, preferred_element_type=F32)
    grad_hidden = grad_hidden + jnp.dot(back_table, low, preferred_element_type=F32)
    grad_ref[...] = grad_hidden.astype(BF16)


def backward(near, far, w2s, w2n, peers, slots, rows_dev):
    width = w2s.shape[0]
    grad_self, near_grad = backward_near(near, w2s, w2n, rows_dev)
    return pl.pallas_call(
        functools.partial(backward_kernel, peers, slots),
        in_specs=[VMEM] * 5,
        out_specs=[VMEM] * 3,
        out_shape=[
            jax.ShapeDtypeStruct((rows_dev, width), BF16),
            jax.ShapeDtypeStruct((rows_dev, peers * rows_dev), BF16),
            jax.ShapeDtypeStruct((rows_dev, 128), F32),
        ],
        scratch_shapes=[
            pltpu.VMEM((peers * rows_dev, near.shape[1] - width), BF16),
            pltpu.VMEM((peers * rows_dev, width), F32),
        ],
        name="second_backward", compiler_params=PARAMS,
        cost_estimate=pl.CostEstimate(flops=BACKWARD_COST, bytes_accessed=0, transcendentals=0),
    )(near, far, grad_self, near_grad, w2n)


def hidden_kernel(total_ref, got_ref, grad_ref, grad_far_ref, hidden_ref, grads_ref):
    for s, ref in enumerate((grad_ref, grad_far_ref)):
        preact = total_ref[s] + got_ref[1 - s]
        grads_ref[s] = jnp.where(preact > 0, ref[...], jnp.zeros_like(ref))
        if s == 0:
            hidden_ref[...] = jnp.maximum(preact, 0.0).astype(BF16)


def hidden_and_grads(total, got, grad, grad_far):
    return call(
        hidden_kernel, "hidden", (total, got, grad, grad_far), [(grad.shape, BF16), (total.shape, BF16)]
    )


def own_part_kernel(hidden_ref, w2s_ref, out_ref):
    out_ref[...] = jnp.dot(hidden_ref[...], w2s_ref[...], preferred_element_type=F32)


def own_part(hidden, w2s):
    out = ((hidden.shape[0], w2s.shape[1]), F32)
    return call(own_part_kernel, "own_part", (hidden, w2s), [out], OWN_COST)[0]


def outputs_kernel(codes, near_ref, far_ref, table_ref, degree_ref, own_ref, w2n_ref, *refs):
    grad_refs, (feat_ref, mean_ref, out_hbm, self_hbm, neigh_hbm) = refs[:-11], refs[-11:-6]
    out_ref, self_ref, neigh_ref, grad_scratch, hidden_scratch, sems = refs[-6:]
    pairs = ((self_ref, self_hbm), (neigh_ref, neigh_hbm), (out_ref, out_hbm))
    copies = [pltpu.make_async_copy(src, dst, sems.at[n]) for n, (src, dst) in enumerate(pairs)]
    rows = table_ref.shape[0]
    group = mean_ref.shape[1]
    me = lax.axis_index("feat")
    for ref, code_list in zip(grad_refs, codes):
        for n, code in enumerate(code_list):
            to = pl.multiple_of(lax.bitwise_xor(me, code) * rows, rows)
            grad_scratch[pl.ds(to, rows), :] = ref[n]
    grad_pre = grad_scratch[...]
    self_ref[0] = jnp.dot(feat_ref[0, :, :group], grad_pre, preferred_element_type=F32)
    copies[0].start()
    neigh_ref[0] = jnp.dot(mean_ref[...], grad_pre, preferred_element_type=F32)
    copies[1].start()

    place(hidden_scratch, near_ref, far_ref, rows, lax.axis_index("dp"))
    neigh_sum = jnp.dot(table_ref[...], hidden_scratch[...], preferred_element_type=F32)
    mean_two = ((near_ref[0:rows, :].astype(F32) + neigh_sum) / (1.0 + degree_ref[:, 0:1])).astype(BF16)
    out = own_ref[...] + jnp.dot(mean_two, w2n_ref[...], preferred_element_type=F32)
    out_ref[0, 0] = out.astype(BF16)
    copies[2].start()
    for copy in copies:
        copy.wait()


def outputs(near, far, table, degree, own, w2n, grads, codes, features, mean):
    group, width = mean.shape[1], grads[0].shape[2]
    grad = jax.ShapeDtypeStruct((1, mean.shape[0], width), F32)
    out = jax.ShapeDtypeStruct((1, 1) + own.shape, BF16)
    return pl.pallas_call(
        functools.partial(outputs_kernel, codes),
        in_specs=[VMEM] * (len(grads) + 8),
        out_specs=[pl.BlockSpec(memory_space=pltpu.HBM)] * 3,
        out_shape=[out, grad, grad],
        scratch_shapes=[pltpu.VMEM(a.shape, a.dtype) for a in (out, grad, grad)]
        + [pltpu.VMEM((group, width), BF16), pltpu.VMEM((table.shape[1], near.shape[1]), BF16)]
        + [pltpu.SemaphoreType.DMA((3,))],
        name="outputs", compiler_params=PARAMS,
    )(near, far, table, degree, own, w2n, *grads, features, mean)


def swap(x, axis, bits):
    return lax.ppermute(x, axis, [(i, i ^ bits) for i in range(lax.axis_size(axis))])


def far_half(near, axis):
    bits = 2
    while 2 * bits < lax.axis_size(axis):
        near = join(near, swap(near, axis, bits))
        bits *= 2
    return near, swap(near, axis, bits)


def sum_over_chips(near, far, chips):
    bit = 1
    while 4 * bit < chips:
        near, far = fold(near, swap(far, "feat", 2 * bit), 2)
        bit *= 2
    total = fold(near, swap(far, "feat", 2 * bit), 1)[0]
    return total, swap(total, "feat", chips)


def on_device(features, neigh_lists, w1_self, w1_neigh, w2_self, w2_neigh, send_rows, send_count, recv_target, out_grad):
    chips, peers = lax.axis_size("feat") // 2, lax.axis_size("dp")
    rows_dev, slots = out_grad.shape[2], send_rows.shape[3]
    keep, send, mean, aux, w2_self, w2_neigh = first_layer(
        features, neigh_lists, w1_self, w1_neigh, send_rows, send_count, recv_target, out_grad, w2_self, w2_neigh
    )
    near, far = pair_sum(keep, swap(send, "feat", 1))
    total, got = sum_over_chips(near, far, chips)
    aux_near, aux_far = far_half(join(aux, swap(aux, "dp", 1), INDEX_COST), "dp")
    grad, table, degree = backward(aux_near, aux_far, w2_self, w2_neigh, peers, slots, rows_dev)
    hidden, grads = hidden_and_grads(total, got, grad, swap(grad, "feat", chips))
    codes, bit = [0, chips // 2], chips // 4
    while bit > 1:
        grads = join(grads, swap(grads, "feat", 2 * bit))
        codes, bit = codes + [code ^ bit for code in codes], bit // 2
    grads = [grads, swap(grads, "feat", 2)]
    grads = grads + [swap(x, "feat", 1) for x in grads]
    codes = [[2 * code ^ flip for code in codes] for flip in (0, 2, 1, 3)]
    near, far = far_half(join(hidden, swap(hidden, "dp", 1), cost=HIDDEN_COST), "dp")
    own = own_part(hidden, w2_self)
    return outputs(near, far, table, degree, own, w2_neigh, grads, codes, features, mean)


def solution(mesh):
    in_specs = (
        P("dp", "feat", None),
        P("dp", None, None),
        P("feat", None),
        P("feat", None),
        P(),
        P(),
        P("dp", "feat", None, None),
        P("dp", "feat", None),
        P("dp", "feat", None, None),
        P("dp", "feat", None, None),
    )
    out_specs = (P("dp", "feat", None, None), P("dp", "feat", None), P("dp", "feat", None))
    return jax.shard_map(
        on_device, mesh=mesh, in_specs=in_specs, out_specs=out_specs, check_vma=False
    )
```

time: 77.5 us -> 26.5 us (0.34)
  waiting for transfers between devices: 20.1 us -> 6.05 us
  blocking collectives: 13.9 us -> 0 us
  between operations: 14.2 us -> 0.67 us
  local copies, waits for them, and re-layouts: 8.95 us -> 0.01 us
  matrix products: 3.8 us -> 0 us
  Pallas kernels: 0 us -> 3.73 us
  other arithmetic: 3.58 us -> 0 us
  starting transfers between devices: 12.4 us -> 15.8 us
    reduce_scatter x1 -> x0, waiting for transfers between devices: 16.5 us -> none  [on_device(): lax.psum_scatter(term + lax.dot_general(part_mean, w1_neigh, contract, pr...]
    ppermute x0 -> x11, starting transfers between devices: none -> 15.8 us  [swap(): lax.ppermute(x, axis, [(i, i ^ bits) for i in range(lax.axis_size(axis))])]
    all_gather x1 -> x0, blocking collectives: 13.9 us -> none  [on_device(): block_rows = lax.all_gather(grad_pre, 'feat', axis=0, tiled=True)]
    all_to_all x3 -> x0, starting transfers between devices: 12.4 us -> none  [the longest x1 5.29 us: on_device(): lax.all_to_all(counts_out, 'dp', split_axis=0, concat_axis=0, tiled=True)]
    ppermute x0 -> x11, waiting for transfers between devices: none -> 6.05 us  [swap(): lax.ppermute(x, axis, [(i, i ^ bits) for i in range(lax.axis_size(axis))])]
    gather x3 -> x0, local copies, waits for them, and re-layouts: 4.07 us -> none  [the longest x1 2.81 us: on_device(): gathered = jnp.take(columns, neighbour_lists, axis=1)]
    dot_general x9 -> x0, matrix products: 3.8 us -> none  [the longest x1 0.91 us: on_device(): second = jnp.dot(part_mean, block_rows, preferred_element_type=jnp.float32)]
    unnamed x22 -> x2, local copies, waits for them, and re-layouts: 3.77 us -> 0.01 us
  transfers between devices with their start and end apart: 4 -> 11, of which waited for: 2 -> 5; matrix products, arithmetic and copies ran while one was open for 10% -> 0% of each run, Pallas kernels for 0% -> 4%
where the time goes in v1:
time: 26.5 us; the launch traced here: 26.3 us
  starting transfers between devices  15.8 us (60%)
  waiting for transfers between devices  6.05 us (23%)
  Pallas kernels  3.73 us (14%)
  between operations  0.67 us (3%)
    ppermute x11, starting transfers between devices, swap(): lax.ppermute(x, axis, [(i, i ^ bits) for i in range(lax.axis_size(axis))])  15.8 us
    ppermute x11, waiting for transfers between devices, swap(): lax.ppermute(x, axis, [(i, i ^ bits) for i in range(lax.axis_size(axis))])  6.05 us
    pallas_call x1, Pallas kernels, first_layer(): pl.pallas_call(first_layer_kernel, grid=(group // tile,), in_specs=[pl.Bl...  1.67 us
    pallas_call x1, Pallas kernels, outputs(): pl.pallas_call(functools.partial(outputs_kernel, codes), in_specs=[VMEM]...  1.03 us
    pallas_call x7, Pallas kernels, call(): pl.pallas_call(kernel, in_specs=[VMEM] * len(args), out_specs=[VMEM] * le...  0.59 us
  transfers between devices with their start and end apart: 11, of which 5 were waited for; matrix products, arithmetic and copies ran while one was open for 0% of the time, Pallas kernels for 4%

profile of v1, /device:TPU:0, one launch (start us, length us, event | category | flops | bytes accessed | tf_op | source)
XLA Modules:
  0.0 26.3 jit_solution(13829357176416822348)
XLA Ops:
  0.6 1.7 %first_layer.1 = (f32[4,16,512]{2,1,0:T(8,128)S(1)}, f32[4,16,512]{2,1,0:T(8,128)S(1)}, bf16[128,128]{1,0:T(8,128)(2,1)S(1)}, bf16[16,640]{1,0:T(8,128)(2,1)S(1)...) custom-call(bf16[1,128,256]{2,1,0:T(8,128)(2,1)} %refs_4_.1, s32[10,1,128]{2,1,0:T(1,128)} %bitcast.1, ...), custom_call_target="tpu_custom_call" | custom-call | tf_op jit(solution)/shard_map/first_layer/pallas_call | solution.py:127
  2.3 0.5 %collective-permute-start = (f32[4,16,512]{2,1,0:T(8,128)S(1)}, f32[4,16,512]{2,1,0:T(8,128)S(1)}, u32[]{:S(2)}, u32[]{:S(2)}) collective-permute-start(f32[4,16,512]{2,1,0:T(8,128)S(1)} %get-tuple-element.19), channel_id=1, source_target_pairs={{0,4},{4,0},{8,12},{12,8},{16,20},{20,16},{24,28},{28,24},{1,5},{5... | collective-permute-start | bytes 393224 | tf_op jit(solution)/shard_map/ppermute | solution.py:364
  2.8 2.6 %collective-permute-start.3 = (bf16[16,640]{1,0:T(8,128)(2,1)S(1)}, bf16[16,640]{1,0:T(8,128)(2,1)S(1)}, u32[]{:S(2)}, u32[]{:S(2)}) collective-permute-start(bf16[16,640]{1,0:T(8,128)(2,1)S(1)} %get-tuple-element.22.a_ref), channel_id=1, source_target_pairs={{0,1},{1,0},{2,3},{3,2},{4,5},{5,4},{6,7},{7,6},{8,9},{9,8},{10,11... | collective-permute-start | bytes 61448 | tf_op jit(solution)/shard_map/ppermute | solution.py:364
  5.4 1.6 %collective-permute-start.1 = (f32[2,16,512]{2,1,0:T(8,128)S(1)}, f32[2,16,512]{2,1,0:T(8,128)S(1)}, u32[]{:S(2)}, u32[]{:S(2)}) collective-permute-start(f32[2,16,512]{2,1,0:T(8,128)S(1)} %get-tuple-element.21), channel_id=1, source_target_pairs={{0,8},{4,12},{8,0},{12,4},{16,24},{20,28},{24,16},{28,20},{1,9},{5... | collective-permute-start | bytes 196616 | tf_op jit(solution)/shard_map/ppermute | solution.py:364
  7.1 0.1 collective-permute-done.3.b_ref
  7.2 2.0 %collective-permute-start.4 = (bf16[32,640]{1,0:T(8,128)(2,1)S(1)}, bf16[32,640]{1,0:T(8,128)(2,1)S(1)}, u32[]{:S(2)}, u32[]{:S(2)}) collective-permute-start(bf16[32,640]{1,0:T(8,128)(2,1)S(1)} %join.2.near_ref), channel_id=1, source_target_pairs={{0,2},{1,3},{2,0},{3,1},{4,6},{5,7},{6,4},{7,5},{8,10},{9,11},{10,... | collective-permute-start | bytes 122888 | tf_op jit(solution)/shard_map/ppermute | solution.py:364
  9.2 0.4 %backward_near.1 = (f32[16,512]{1,0:T(8,128)S(1)}, f32[32,512]{1,0:T(8,128)S(1)}) custom-call(bf16[32,640]{1,0:T(8,128)(2,1)S(1)} %join.2.near_ref, bf16[512,512]{1,0:T(8,128)(2,1)S(1)} %get-tuple-element.23.w2s_ref, bf16[512,512]{1,0:T(8,128)(2,1)S(1)} %get-tuple-element.24.w2n_ref), custom_call_target="tpu_custom_call" | custom-call | tf_op jit(solution)/shard_map/backward_near/pallas_call | solution.py:151
  9.6 0.2 collective-permute-done.1.got_ref
  9.8 2.7 %collective-permute-start.2 = (f32[2,16,512]{2,1,0:T(8,128)S(1)}, f32[2,16,512]{2,1,0:T(8,128)S(1)}, u32[]{:S(2)}, u32[]{:S(2)}) collective-permute-start(f32[2,16,512]{2,1,0:T(8,128)S(1)} %fold.1.total_ref), channel_id=1, source_target_pairs={{0,16},{4,20},{8,24},{12,28},{16,0},{20,4},{24,8},{28,12},{1,17},{... | collective-permute-start | bytes 196616 | tf_op jit(solution)/shard_map/ppermute | solution.py:364
  12.4 0.0 collective-permute-done.4.far_ref
  12.4 0.4 %second_backward.1 = (bf16[16,512]{1,0:T(8,128)(2,1)S(1)}, bf16[16,64]{1,0:T(8,128)(2,1)S(1)}, f32[16,128]{1,0:T(8,128)S(1)}) custom-call(bf16[32,640]{1,0:T(8,128)(2,1)S(1)} %join.2.near_ref, bf16[32,640]{1,0:T(8,128)(2,1)S(1)} %collective-permute-done.4.far_ref, f32[16,512]{1,0:T(8,128)S(1)} %get-tuple-element.25.self_ref, ...), custom_call_target="tpu_custom_call" | custom-call | flops 10000000000 | tf_op jit(solution)/shard_map/second_backward/pallas_call | solution.py:278
  12.9 1.9 %collective-permute-start.5 = (bf16[16,512]{1,0:T(8,128)(2,1)S(1)}, bf16[16,512]{1,0:T(8,128)(2,1)S(1)}, u32[]{:S(2)}, u32[]{:S(2)}) collective-permute-start(bf16[16,512]{1,0:T(8,128)(2,1)S(1)} %get-tuple-element.27.grad_ref), channel_id=1, source_target_pairs={{0,16},{4,20},{8,24},{12,28},{16,0},{20,4},{24,8},{28,12},{1,17},{... | collective-permute-start | bytes 49160 | tf_op jit(solution)/shard_map/ppermute | solution.py:364
  14.7 2.8 %collective-permute-done.5.grad_far_ref = bf16[16,512]{1,0:T(8,128)(2,1)S(1)} collective-permute-done((bf16[16,512]{1,0:T(8,128)(2,1)S(1)}, bf16[16,512]{1,0:T(8,128)(2,1)S(1)}, u32[]{:S(2)}, u32[]{:S(2)}) %collective-permute-start.5) | collective-permute-done | bytes 16416 | tf_op jit(solution)/shard_map/ppermute | solution.py:364
  17.5 1.4 %collective-permute-start.6 = (bf16[16,512]{1,0:T(8,128)(2,1)S(1)}, bf16[16,512]{1,0:T(8,128)(2,1)S(1)}, u32[]{:S(2)}, u32[]{:S(2)}) collective-permute-start(bf16[16,512]{1,0:T(8,128)(2,1)S(1)} %get-tuple-element.28.a_ref.hidden_ref), channel_id=1, source_target_pairs={{0,1},{1,0},{2,3},{3,2},{4,5},{5,4},{6,7},{7,6},{8,9},{9,8},{10,11... | collective-permute-start | bytes 49160 | tf_op jit(solution)/shard_map/ppermute | solution.py:364
  18.9 1.6 %collective-permute-start.8 = (bf16[2,16,512]{2,1,0:T(8,128)(2,1)S(1)}, bf16[2,16,512]{2,1,0:T(8,128)(2,1)S(1)}, u32[]{:S(2)}, u32[]{:S(2)}) collective-permute-start(bf16[2,16,512]{2,1,0:T(8,128)(2,1)S(1)} %get-tuple-element.31.refs_0_), channel_id=1, source_target_pairs={{0,8},{4,12},{8,0},{12,4},{16,24},{20,28},{24,16},{28,20},{1,9},{5... | collective-permute-start | bytes 98312 | tf_op jit(solution)/shard_map/ppermute | solution.py:364
  20.5 0.0 collective-permute-start.9
  20.5 0.8 %collective-permute-done.6.b_ref = bf16[16,512]{1,0:T(8,128)(2,1)S(1)} collective-permute-done((bf16[16,512]{1,0:T(8,128)(2,1)S(1)}, bf16[16,512]{1,0:T(8,128)(2,1)S(1)}, u32[]{:S(2)}, u32[]{:S(2)}) %collective-permute-start.6) | collective-permute-done | bytes 16416 | tf_op jit(solution)/shard_map/ppermute | solution.py:364
  21.3 1.5 %collective-permute-start.7 = (bf16[32,512]{1,0:T(8,128)(2,1)S(1)}, bf16[32,512]{1,0:T(8,128)(2,1)S(1)}, u32[]{:S(2)}, u32[]{:S(2)}) collective-permute-start(bf16[32,512]{1,0:T(8,128)(2,1)S(1)} %join.3.near_ref), channel_id=1, source_target_pairs={{0,2},{1,3},{2,0},{3,1},{4,6},{5,7},{6,4},{7,5},{8,10},{9,11},{10,... | collective-permute-start | bytes 98312 | tf_op jit(solution)/shard_map/ppermute | solution.py:364
  22.9 0.0 collective-permute-done.8.refs_1_
  22.9 0.0 collective-permute-start.10
  22.9 0.2 own_part.1.own_ref
  23.0 0.0 collective-permute-done.9.refs_2_
  23.0 2.2 %collective-permute-done.7.far_ref = bf16[32,512]{1,0:T(8,128)(2,1)S(1)} collective-permute-done((bf16[32,512]{1,0:T(8,128)(2,1)S(1)}, bf16[32,512]{1,0:T(8,128)(2,1)S(1)}, u32[]{:S(2)}, u32[]{:S(2)}) %collective-permute-start.7) | collective-permute-done | bytes 32800 | tf_op jit(solution)/shard_map/ppermute | solution.py:364
  25.3 1.0 %outputs.1 = (bf16[1,1,16,512]{3,2,1,0:T(8,128)(2,1)}, f32[1,128,512]{2,1,0:T(8,128)}, f32[1,128,512]{2,1,0:T(8,128)}) custom-call(bf16[32,512]{1,0:T(8,128)(2,1)S(1)} %join.3.near_ref, bf16[32,512]{1,0:T(8,128)(2,1)S(1)} %collective-permute-done.7.far_ref, bf16[16,64]{1,0:T(8,128)(2,1)S(1)} %get-tuple-element.29.table_ref, ...), custom_call_target="tpu_custom_call" | custom-call | tf_op jit(solution)/shard_map/outputs/pallas_call | solution.py:351
  (10 shorter events, 0.1 us)
Async XLA Ops:
  2.3 3.1 %collective-permute-start = (f32[4,16,512]{2,1,0:T(8,128)S(1)}, f32[4,16,512]{2,1,0:T(8,128)S(1)}, u32[]{:S(2)}, u32[]{:S(2)}) collective-permute-start(f32[4,16,512]{2,1,0:T(8,128)S(1)} %get-tuple-element.19), channel_id=1, source_target_pairs={{0,4},{4,0},{8,12},{12,8},{16,20},{20,16},{24,28},{28,24},{1,5},{5... | collective-permute-start | bytes 393224 | tf_op jit(solution)/shard_map/ppermute | solution.py:364
  2.8 4.3 %collective-permute-start.3 = (bf16[16,640]{1,0:T(8,128)(2,1)S(1)}, bf16[16,640]{1,0:T(8,128)(2,1)S(1)}, u32[]{:S(2)}, u32[]{:S(2)}) collective-permute-start(bf16[16,640]{1,0:T(8,128)(2,1)S(1)} %get-tuple-element.22.a_ref), channel_id=1, source_target_pairs={{0,1},{1,0},{2,3},{3,2},{4,5},{5,4},{6,7},{7,6},{8,9},{9,8},{10,11... | collective-permute-start | bytes 61448 | tf_op jit(solution)/shard_map/ppermute | solution.py:364
  5.4 4.3 %collective-permute-start.1 = (f32[2,16,512]{2,1,0:T(8,128)S(1)}, f32[2,16,512]{2,1,0:T(8,128)S(1)}, u32[]{:S(2)}, u32[]{:S(2)}) collective-permute-start(f32[2,16,512]{2,1,0:T(8,128)S(1)} %get-tuple-element.21), channel_id=1, source_target_pairs={{0,8},{4,12},{8,0},{12,4},{16,24},{20,28},{24,16},{28,20},{1,9},{5... | collective-permute-start | bytes 196616 | tf_op jit(solution)/shard_map/ppermute | solution.py:364
  7.2 5.3 %collective-permute-start.4 = (bf16[32,640]{1,0:T(8,128)(2,1)S(1)}, bf16[32,640]{1,0:T(8,128)(2,1)S(1)}, u32[]{:S(2)}, u32[]{:S(2)}) collective-permute-start(bf16[32,640]{1,0:T(8,128)(2,1)S(1)} %join.2.near_ref), channel_id=1, source_target_pairs={{0,2},{1,3},{2,0},{3,1},{4,6},{5,7},{6,4},{7,5},{8,10},{9,11},{10,... | collective-permute-start | bytes 122888 | tf_op jit(solution)/shard_map/ppermute | solution.py:364
  9.8 7.7 %collective-permute-start.2 = (f32[2,16,512]{2,1,0:T(8,128)S(1)}, f32[2,16,512]{2,1,0:T(8,128)S(1)}, u32[]{:S(2)}, u32[]{:S(2)}) collective-permute-start(f32[2,16,512]{2,1,0:T(8,128)S(1)} %fold.1.total_ref), channel_id=1, source_target_pairs={{0,16},{4,20},{8,24},{12,28},{16,0},{20,4},{24,8},{28,12},{1,17},{... | collective-permute-start | bytes 196616 | tf_op jit(solution)/shard_map/ppermute | solution.py:364
  12.9 4.6 %collective-permute-start.5 = (bf16[16,512]{1,0:T(8,128)(2,1)S(1)}, bf16[16,512]{1,0:T(8,128)(2,1)S(1)}, u32[]{:S(2)}, u32[]{:S(2)}) collective-permute-start(bf16[16,512]{1,0:T(8,128)(2,1)S(1)} %get-tuple-element.27.grad_ref), channel_id=1, source_target_pairs={{0,16},{4,20},{8,24},{12,28},{16,0},{20,4},{24,8},{28,12},{1,17},{... | collective-permute-start | bytes 49160 | tf_op jit(solution)/shard_map/ppermute | solution.py:364
  17.5 3.8 %collective-permute-start.6 = (bf16[16,512]{1,0:T(8,128)(2,1)S(1)}, bf16[16,512]{1,0:T(8,128)(2,1)S(1)}, u32[]{:S(2)}, u32[]{:S(2)}) collective-permute-start(bf16[16,512]{1,0:T(8,128)(2,1)S(1)} %get-tuple-element.28.a_ref.hidden_ref), channel_id=1, source_target_pairs={{0,1},{1,0},{2,3},{3,2},{4,5},{5,4},{6,7},{7,6},{8,9},{9,8},{10,11... | collective-permute-start | bytes 49160 | tf_op jit(solution)/shard_map/ppermute | solution.py:364
  18.9 3.9 %collective-permute-start.8 = (bf16[2,16,512]{2,1,0:T(8,128)(2,1)S(1)}, bf16[2,16,512]{2,1,0:T(8,128)(2,1)S(1)}, u32[]{:S(2)}, u32[]{:S(2)}) collective-permute-start(bf16[2,16,512]{2,1,0:T(8,128)(2,1)S(1)} %get-tuple-element.31.refs_0_), channel_id=1, source_target_pairs={{0,8},{4,12},{8,0},{12,4},{16,24},{20,28},{24,16},{28,20},{1,9},{5... | collective-permute-start | bytes 98312 | tf_op jit(solution)/shard_map/ppermute | solution.py:364
  20.5 2.5 %collective-permute-start.9 = (bf16[2,16,512]{2,1,0:T(8,128)(2,1)S(1)}, bf16[2,16,512]{2,1,0:T(8,128)(2,1)S(1)}, u32[]{:S(2)}, u32[]{:S(2)}) collective-permute-start(bf16[2,16,512]{2,1,0:T(8,128)(2,1)S(1)} %get-tuple-element.31.refs_0_), channel_id=1, source_target_pairs={{0,4},{4,0},{8,12},{12,8},{16,20},{20,16},{24,28},{28,24},{1,5},{5... | collective-permute-start | bytes 98312 | tf_op jit(solution)/shard_map/ppermute | solution.py:364
  21.3 3.9 %copy-start = (bf16[1,128,256]{2,1,0:T(8,128)(2,1)S(1)}, bf16[1,128,256]{2,1,0:T(8,128)(2,1)}, u32[]{:S(2)}) copy-start(bf16[1,128,256]{2,1,0:T(8,128)(2,1)} %refs_4_.1) | copy-start | bytes 196612
  21.3 3.9 %collective-permute-start.7 = (bf16[32,512]{1,0:T(8,128)(2,1)S(1)}, bf16[32,512]{1,0:T(8,128)(2,1)S(1)}, u32[]{:S(2)}, u32[]{:S(2)}) collective-permute-start(bf16[32,512]{1,0:T(8,128)(2,1)S(1)} %join.3.near_ref), channel_id=1, source_target_pairs={{0,2},{1,3},{2,0},{3,1},{4,6},{5,7},{6,4},{7,5},{8,10},{9,11},{10,... | collective-permute-start | bytes 98312 | tf_op jit(solution)/shard_map/ppermute | solution.py:364
  22.9 2.4 %collective-permute-start.10 = (bf16[2,16,512]{2,1,0:T(8,128)(2,1)S(1)}, bf16[2,16,512]{2,1,0:T(8,128)(2,1)S(1)}, u32[]{:S(2)}, u32[]{:S(2)}) collective-permute-start(bf16[2,16,512]{2,1,0:T(8,128)(2,1)S(1)} %collective-permute-done.8.refs_1_), channel_id=1, source_target_pairs={{0,4},{4,0},{8,12},{12,8},{16,20},{20,16},{24,28},{28,24},{1,5},{5... | collective-permute-start | bytes 98312 | tf_op jit(solution)/shard_map/ppermute | solution.py:364

commit v2 on v1

v2 whole, which is shorter than its diff:
```python
import functools

import jax
import jax.numpy as jnp
from jax import lax
from jax.experimental import pallas as pl
from jax.experimental.pallas import tpu as pltpu
from jax.sharding import PartitionSpec as P

K1 = 10
HIDDEN_COST = 3 * 10**8
PREACT_COST = 4 * 10**8
OWN_COST = 10**8
BACKWARD_COST = 0
INDEX_COST = 10**9
F32 = jnp.float32
BF16 = jnp.bfloat16
NT = (((1,), (1,)), ((), ()))
TN = (((0,), (0,)), ((), ()))
VMEM = pl.BlockSpec(memory_space=pltpu.VMEM)
PARAMS = pltpu.CompilerParams(vmem_limit_bytes=12 * 1024 * 1024)


def iota(shape, dim):
    return lax.broadcasted_iota(jnp.int32, shape, dim)


def table_lanes(peers, slots):
    return -(-3 * peers * slots // 128) * 128


def first_layer_kernel(
    tiles, feat_hbm, lists_hbm, w1s_hbm, w1n_hbm, rows_hbm, counts_hbm, targets_hbm, og_hbm,
    keep_ref, send_ref, both_ref, aux_ref,
    feat_ref, lists_ref, w1_ref, rows_ref, counts_ref, targets_ref, og_ref, part_ref, sems,
):
    i = pl.program_id(0) if tiles > 1 else 0
    depth = feat_ref.shape[1]
    pairs = (
        (lists_hbm, lists_ref), (feat_hbm, feat_ref),
        (w1s_hbm, w1_ref.at[0:depth]), (w1n_hbm, w1_ref.at[depth : 2 * depth]),
        (targets_hbm, targets_ref), (rows_hbm, rows_ref), (counts_hbm, counts_ref), (og_hbm, og_ref),
    )
    copies = [pltpu.make_async_copy(src, dst, sems.at[n]) for n, (src, dst) in enumerate(pairs)]

    def once(step):
        if tiles > 1:
            pl.when(i == 0)(step)
        else:
            step()

    def wait(first, last):
        @once
        def _():
            for copy in copies[first:last]:
                copy.wait()

    @once
    def _():
        for copy in copies:
            copy.start()

    me = lax.axis_index("feat")
    core = me % 2
    nodes = feat_ref.shape[2]
    tile, width = part_ref.shape
    rows_dev = og_ref.shape[2]
    step = min(nodes, 256)
    at_tile = pl.ds(pl.multiple_of(i * tile, tile), tile) if tiles > 1 else slice(0, tile)
    wait(0, 1)
    hits = []
    for start in range(0, nodes, step):
        ids = iota((step, tile), 0) + start
        times = jnp.zeros((step, tile), F32)
        for k in range(K1):
            times = times + (ids == lists_ref[k, :, at_tile]).astype(F32)
        hits.append(times.astype(BF16))

    @once
    def _():
        for copy in copies[4:8]:
            copy.wait()
        peers, slots = rows_ref.shape[2], rows_ref.shape[3]
        lanes = aux_ref.shape[1] - width
        which = iota((slots, lanes), 1) // (peers * slots)
        same_slot = iota((slots, lanes), 1) % slots == iota((slots, lanes), 0)

        def tiled(ref, n):
            spread = (same_slot & (which == n)).astype(BF16)
            return jnp.dot(ref[0, 0].astype(BF16), spread, preferred_element_type=F32)

        eye = iota((peers, peers), 0) == iota((peers, peers), 1)
        column = jnp.sum(jnp.where(eye, counts_ref[0], 0), axis=1, keepdims=True)
        lane = iota((peers, lanes), 1)
        live = (lane // (peers * slots) == 2) & (lane % slots < column)
        tables = tiled(targets_ref, 0) + tiled(rows_ref, 1) + live.astype(F32)
        if peers < rows_dev:
            tables = jnp.concatenate([tables, jnp.zeros((rows_dev - peers, lanes), F32)], axis=0)
        aux_ref[:, :width] = og_ref[0, 0]
        aux_ref[:, width:] = tables.astype(BF16)

    wait(1, 2)
    total = jnp.zeros((depth, tile), F32)
    for n, times in enumerate(hits):
        total = total + jnp.dot(
            feat_ref[0, :, n * step : (n + 1) * step], times, preferred_element_type=F32
        )
    both_ref[0:depth, :] = feat_ref[0, :, at_tile]
    both_ref[depth:, :] = (total / K1).astype(BF16)
    wait(2, 4)
    part_ref[...] = lax.dot_general(both_ref[...], w1_ref[...], TN, preferred_element_type=F32)
    for z in range(keep_ref.shape[0]):
        kept = jnp.where(i * keep_ref.shape[0] + z == me // 2, core, 1 - core)
        for ref, which in ((keep_ref, kept), (send_ref, 1 - kept)):
            at = pl.multiple_of((2 * z + which) * rows_dev, rows_dev)
            ref[z] = part_ref[pl.ds(at, rows_dev), :]


def first_layer(features, lists, w1s, w1n, rows, counts, targets, og):
    depth = features.shape[1]
    group, width = lists.shape[2], w1s.shape[1]
    lists = lists.reshape(lists.shape[1], 1, group)
    rows_dev = og.shape[2]
    tile = min(group, 128)
    chips = group // (2 * rows_dev)
    tile_chips = tile // (2 * rows_dev)
    aux = (rows_dev, width + table_lanes(*rows.shape[2:]))
    args = (features, lists, w1s, w1n, rows, counts, targets, og)
    args = tuple(pltpu.with_memory_space_constraint(a, pltpu.HBM) for a in args)
    half = jax.ShapeDtypeStruct((chips, rows_dev, width), F32)
    half_spec = pl.BlockSpec((tile_chips, rows_dev, width), lambda i: (i, 0, 0))
    whole = lambda shape: pl.BlockSpec(shape, lambda i: (0,) * len(shape))
    scratch = [features, lists, jax.ShapeDtypeStruct((2 * depth, width), BF16), rows, counts, targets, og]
    return pl.pallas_call(
        functools.partial(first_layer_kernel, group // tile),
        grid=(group // tile,),
        in_specs=[pl.BlockSpec(memory_space=pltpu.HBM)] * len(args),
        out_specs=[
            half_spec, half_spec,
            pl.BlockSpec((2 * depth, tile), lambda i: (0, i)),
            whole(aux),
        ],
        out_shape=[
            half, half,
            jax.ShapeDtypeStruct((2 * depth, group), BF16),
            jax.ShapeDtypeStruct(aux, BF16),
        ],
        scratch_shapes=[pltpu.VMEM(a.shape, a.dtype) for a in scratch]
        + [pltpu.VMEM((tile, width), F32)]
        + [pltpu.SemaphoreType.DMA((len(args),))],
        name="first_layer", compiler_params=PARAMS,
    )(*args)


def call(kernel, name, args, out_shape, cost=0):
    return pl.pallas_call(
        kernel,
        in_specs=[VMEM] * len(args),
        out_specs=[VMEM] * len(out_shape),
        out_shape=[jax.ShapeDtypeStruct(shape, dtype) for shape, dtype in out_shape],
        name=name, compiler_params=PARAMS,
        cost_estimate=pl.CostEstimate(flops=cost, bytes_accessed=0, transcendentals=0),
    )(*args)


def reverse(n, levels):
    return sum(((n >> k) & 1) << (levels - 1 - k) for k in range(levels))


def code_of(n, levels, core):
    return jnp.where(core == 0, n, reverse(n, levels))


def levels_of(count):
    return count.bit_length() - 1


def pair_sum_kernel(keep_ref, got_ref, *outs):
    z = lax.axis_index("feat") // 2
    for s, ref in enumerate(outs):
        at = lax.bitwise_xor(z, s)
        ref[...] = keep_ref[at] + got_ref[at]


def pair_sum(keep, got):
    return call(pair_sum_kernel, "pair_sum", (keep, got), [(keep.shape[1:], F32)] * keep.shape[0])


def preact_kernel(*refs):
    refs[-1][...] = sum(ref[...] for ref in refs[:-1])


def preact_sum(parts):
    return call(preact_kernel, "preact", parts, [(parts[0].shape, F32)], PREACT_COST)[0]


def join_kernel(a_ref, b_ref, *refs):
    out_ref = refs[-1]
    count = a_ref.shape[0]
    out_ref[:count] = a_ref[...]
    out_ref[count:] = b_ref[...]


def join(a, b, cost=0, after=()):
    return call(join_kernel, "join", (a, b, *after), [((2 * a.shape[0],) + a.shape[1:], a.dtype)], cost)[0]


def place(scratch, near, far, size, me):
    count = near.shape[0] // size
    core = lax.axis_index("feat") % 2
    for s in range(2 * count):
        ref, at = (near, s) if s < count else (far, s - count)
        code = code_of(s, levels_of(2 * count), core)
        to = pl.multiple_of(lax.bitwise_xor(me, code) * size, size)
        scratch[pl.ds(to, size), :] = ref[at * size : (at + 1) * size, :]


def near_kernel(near_ref, w2s_hbm, w2n_hbm, self_ref, near_grad_ref, w2s_ref, w2n_ref, sems):
    pairs = ((w2s_hbm, w2s_ref), (w2n_hbm, w2n_ref))
    copies = [pltpu.make_async_copy(src, dst, sems.at[n]) for n, (src, dst) in enumerate(pairs)]
    for copy in copies:
        copy.start()
    rows, width = self_ref.shape
    copies[0].wait()
    self_ref[...] = lax.dot_general(near_ref[:rows, :width], w2s_ref[...], NT, preferred_element_type=F32)
    copies[1].wait()
    near_grad_ref[...] = lax.dot_general(near_ref[:, :width], w2n_ref[...], NT, preferred_element_type=F32)


def backward_near(near, w2s, w2n, rows_dev):
    width = w2s.shape[0]
    hbm = pl.BlockSpec(memory_space=pltpu.HBM)
    shapes = [((rows_dev, width), F32), ((near.shape[0], width), F32), (w2s.shape, BF16), (w2n.shape, BF16)]
    return pl.pallas_call(
        near_kernel,
        in_specs=[VMEM, hbm, hbm],
        out_specs=[VMEM] * 4,
        out_shape=[jax.ShapeDtypeStruct(shape, dtype) for shape, dtype in shapes],
        scratch_shapes=[pltpu.SemaphoreType.DMA((2,))],
        name="backward_near", compiler_params=PARAMS,
        cost_estimate=pl.CostEstimate(flops=0, bytes_accessed=0, transcendentals=0),
    )(near, *[pltpu.with_memory_space_constraint(w, pltpu.HBM) for w in (w2s, w2n)])


def backward_kernel(
    peers, slots, near_ref, far_ref, self_ref, near_grad_ref, w2n_ref, grad_ref, table_ref, degree_ref,
    tables, grads,
):
    me = lax.axis_index("dp")
    rows, width = self_ref.shape
    place(tables, near_ref.at[:, width:], far_ref.at[:, width:], rows, me)
    far_grad = lax.dot_general(far_ref[:, :width], w2n_ref[...], NT, preferred_element_type=F32)
    place(grads, near_grad_ref, far_grad, rows, me)
    lanes = peers * slots

    def table(d, which):
        return tables[d * rows : (d + 1) * rows, which * lanes : (which + 1) * lanes].astype(F32)

    block_of = iota((rows, lanes), 1) // slots
    diagonal = iota((rows, lanes), 0) == block_of
    mine = iota((rows, lanes), 0) == me

    def pick(where, x):
        return jnp.sum(jnp.where(where, x, 0.0), axis=0, keepdims=True)

    def crossed(which):
        return sum(jnp.where(block_of == d, table(d, which), 0.0) for d in range(peers))

    def own(which):
        return sum(jnp.where(me == d, table(d, which), 0.0) for d in range(peers))

    live_in = crossed(2)
    target_there = pick(mine, crossed(0))
    row_there = pick(mine, crossed(1))
    own_target, own_row, own_live = [pick(diagonal, own(which)) for which in range(3)]
    own_live_in = pick(mine, live_in)

    local = iota((rows, lanes), 0).astype(F32)
    every = iota((peers * rows, lanes), 0)
    same = every // rows == iota((peers * rows, lanes), 1) // slots
    every_local = (every % rows).astype(F32)

    back = jnp.where(local == own_row, own_live, 0.0).astype(BF16)
    there = jnp.where(same & (every_local == target_there), 1.0, 0.0).astype(BF16)
    back_table = lax.dot_general(back, there, NT, preferred_element_type=F32)
    into = jnp.where(local == own_target, own_live_in, 0.0)
    origin = jnp.where(same & (every_local == row_there), 1.0, 0.0).astype(BF16)
    table_ref[...] = lax.dot_general(into.astype(BF16), origin, NT, preferred_element_type=F32).astype(BF16)
    degree_ref[...] = jnp.broadcast_to(jnp.sum(into, axis=1, keepdims=True), degree_ref.shape)

    own_columns = iota(back_table.shape, 1) - me * rows
    back_table = back_table + (own_columns == iota(back_table.shape, 0)).astype(F32)
    degrees = []
    for e in range(peers):
        hit = jnp.where(local == pick(diagonal, table(e, 0)), live_in[e : e + 1, :], 0.0)
        degrees.append(jnp.sum(hit, axis=1, keepdims=True))
    grad_mean = grads[...] / (1.0 + jnp.concatenate(degrees, axis=0))
    high = grad_mean.astype(BF16)
    low = (grad_mean - high.astype(F32)).astype(BF16)
    back_table = back_table.astype(BF16)
    grad_hidden = self_ref[...] + jnp.dot(back_table, high, preferred_element_type=F32)
    grad_hidden = grad_hidden + jnp.dot(back_table, low, preferred_element_type=F32)
    grad_ref[...] = grad_hidden.astype(BF16)


def backward(near, far, w2s, w2n, peers, slots, rows_dev):
    width = w2s.shape[0]
    grad_self, near_grad, w2s, w2n = backward_near(near, w2s, w2n, rows_dev)
    grad, table, degree = pl.pallas_call(
        functools.partial(backward_kernel, peers, slots),
        in_specs=[VMEM] * 5,
        out_specs=[VMEM] * 3,
        out_shape=[
            jax.ShapeDtypeStruct((rows_dev, width), BF16),
            jax.ShapeDtypeStruct((rows_dev, peers * rows_dev), BF16),
            jax.ShapeDtypeStruct((rows_dev, 128), F32),
        ],
        scratch_shapes=[
            pltpu.VMEM((peers * rows_dev, near.shape[1] - width), BF16),
            pltpu.VMEM((peers * rows_dev, width), F32),
        ],
        name="second_backward", compiler_params=PARAMS,
        cost_estimate=pl.CostEstimate(flops=BACKWARD_COST, bytes_accessed=0, transcendentals=0),
    )(near, far, grad_self, near_grad, w2n)
    return grad, table, degree, w2s, w2n


def hidden_kernel(preact_ref, grad_ref, hidden_ref, grads_ref):
    preact = preact_ref[...]
    hidden_ref[...] = jnp.maximum(preact, 0.0).astype(BF16)
    grads_ref[0] = jnp.where(preact > 0, grad_ref[...], jnp.zeros_like(grad_ref))


def hidden_and_grads(preact, grad):
    return call(hidden_kernel, "hidden", (preact, grad), [(grad.shape, BF16), ((1,) + grad.shape, BF16)])


def own_part_kernel(hidden_ref, w2s_ref, out_ref):
    out_ref[...] = jnp.dot(hidden_ref[...], w2s_ref[...], preferred_element_type=F32)


def own_part(hidden, w2s):
    out = ((hidden.shape[0], w2s.shape[1]), F32)
    return call(own_part_kernel, "own_part", (hidden, w2s), [out], OWN_COST)[0]


def outputs_kernel(codes, near_ref, far_ref, table_ref, degree_ref, own_ref, w2n_ref, *refs):
    grad_refs, (both_ref, out_hbm, self_hbm, neigh_hbm) = refs[:-10], refs[-10:-6]
    out_ref, self_ref, neigh_ref, grad_scratch, hidden_scratch, sems = refs[-6:]
    depth = both_ref.shape[0] // 2
    half = depth // 2 if depth % 32 == 0 else depth
    pieces = [(ref, hbm, n, at) for n, (ref, hbm) in enumerate(((self_ref, self_hbm), (neigh_ref, neigh_hbm)))
              for at in range(0, depth, half)]
    pairs = [(ref.at[0, pl.ds(at, half)], hbm.at[0, pl.ds(at, half)]) for ref, hbm, _, at in pieces]
    pairs.append((out_ref, out_hbm))
    copies = [pltpu.make_async_copy(src, dst, sems.at[n]) for n, (src, dst) in enumerate(pairs)]
    rows = table_ref.shape[0]
    me = lax.axis_index("feat")
    for ref, code_list in zip(grad_refs, codes):
        for n, code in enumerate(code_list):
            to = pl.multiple_of(lax.bitwise_xor(me, code) * rows, rows)
            grad_scratch[pl.ds(to, rows), :] = ref[n]
    grad_pre = grad_scratch[...]
    for (ref, _, n, at), copy in zip(pieces, copies):
        columns = both_ref[n * depth + at : n * depth + at + half, :]
        ref[0, at : at + half] = jnp.dot(columns, grad_pre, preferred_element_type=F32)
        copy.start()

    width = hidden_scratch.shape[1]
    place(hidden_scratch, near_ref.at[:, :width], far_ref.at[:, :width], rows, lax.axis_index("dp"))
    neigh_sum = jnp.dot(table_ref[...], hidden_scratch[...], preferred_element_type=F32)
    mean_two = ((near_ref[0:rows, :width].astype(F32) + neigh_sum) / (1.0 + degree_ref[:, 0:1])).astype(BF16)
    out = own_ref[...] + jnp.dot(mean_two, w2n_ref[...], preferred_element_type=F32)
    out_ref[0, 0] = out.astype(BF16)
    copies[-1].start()
    for copy in copies:
        copy.wait()


def outputs(near, far, table, degree, own, w2n, grads, codes, both):
    group, width = both.shape[1], grads[0].shape[2]
    grad = jax.ShapeDtypeStruct((1, both.shape[0] // 2, width), F32)
    out = jax.ShapeDtypeStruct((1, 1) + own.shape, BF16)
    return pl.pallas_call(
        functools.partial(outputs_kernel, codes),
        in_specs=[VMEM] * (len(grads) + 7),
        out_specs=[pl.BlockSpec(memory_space=pltpu.HBM)] * 3,
        out_shape=[out, grad, grad],
        scratch_shapes=[pltpu.VMEM(a.shape, a.dtype) for a in (out, grad, grad)]
        + [pltpu.VMEM((group, width), BF16), pltpu.VMEM((table.shape[1], w2n.shape[0]), BF16)]
        + [pltpu.SemaphoreType.DMA((5,))],
        name="outputs", compiler_params=PARAMS,
    )(near, far, table, degree, own, w2n, *grads, both)


def swap_cores(x):
    return lax.ppermute(x, "feat", [(i, i ^ 1) for i in range(lax.axis_size("feat"))])


def swap_chips(x, bits):
    return lax.ppermute(x, "feat", [(i, i ^ (2 * bits + 1)) for i in range(lax.axis_size("feat"))])


def swap_peers(x, level):
    feats, peers = lax.axis_size("feat"), lax.axis_size("dp")
    bits = 1 << level, 1 << (levels_of(peers) - 1 - level)
    pairs = [(f * peers + d, f * peers + (d ^ bits[f % 2])) for f in range(feats) for d in range(peers)]
    return lax.ppermute(x, ("feat", "dp"), pairs)


def gather_peers(x, cost, after):
    levels = levels_of(lax.axis_size("dp"))
    for level in range(levels - 1):
        x = join(x, swap_peers(x, level), cost, after)
    return x, swap_peers(x, levels - 1)


def on_device(features, neigh_lists, w1_self, w1_neigh, w2_self, w2_neigh, send_rows, send_count, recv_target, out_grad):
    chips, peers = lax.axis_size("feat") // 2, lax.axis_size("dp")
    rows_dev, slots = out_grad.shape[2], send_rows.shape[3]
    keep, send, both, aux = first_layer(
        features, neigh_lists, w1_self, w1_neigh, send_rows, send_count, recv_target, out_grad
    )
    parts = list(pair_sum(keep, swap_cores(send)))
    far = [swap_chips(parts[s], s) for s in range(chips - 1, 0, -1)]
    aux_near, aux_far = gather_peers(aux, INDEX_COST, parts[:1])
    grad, table, degree, w2_self, w2_neigh = backward(
        aux_near, aux_far, w2_self, w2_neigh, peers, slots, rows_dev
    )
    hidden, grads = hidden_and_grads(preact_sum(parts[:1] + far), grad)
    pieces, codes, bits = [grads], [[0]], chips // 2
    while bits:
        pieces.append(swap_chips(grads, bits))
        codes.append([code ^ (2 * bits + 1) for known in codes for code in known])
        bits //= 2
        if bits:
            grads = join(grads, pieces[-1])
    near, far = gather_peers(hidden, HIDDEN_COST, (grads,))
    pieces = pieces + [swap_cores(x) for x in pieces]
    codes = codes + [[code ^ 1 for code in known] for known in codes]
    own = own_part(hidden, w2_self)
    return outputs(near, far, table, degree, own, w2_neigh, pieces, codes, both)


def solution(mesh):
    in_specs = (
        P("dp", "feat", None),
        P("dp", None, None),
        P("feat", None),
        P("feat", None),
        P(),
        P(),
        P("dp", "feat", None, None),
        P("dp", "feat", None),
        P("dp", "feat", None, None),
        P("dp", "feat", None, None),
    )
    out_specs = (P("dp", "feat", None, None), P("dp", "feat", None), P("dp", "feat", None))
    return jax.shard_map(
        on_device, mesh=mesh, in_specs=in_specs, out_specs=out_specs, check_vma=False
    )
```

time: 26.5 us -> 24.6 us (0.928)
  waiting for transfers between devices: 6.05 us -> 3.56 us
  Pallas kernels: 3.73 us -> 4.85 us
  starting transfers between devices: 15.8 us -> 15.2 us
    ppermute x11 -> x13, waiting for transfers between devices: 6.05 us -> 3.56 us  [the longest x5 2 us: swap_chips(): lax.ppermute(x, 'feat', [(i, i ^ 2 * bits + 1) for i in range(lax.axis_si...]
    pallas_call x1 -> x2, Pallas kernels: 1.67 us -> 3.14 us  [the longest x1 1.57 us: backward_near(): pl.pallas_call(near_kernel, in_specs=[VMEM, hbm, hbm], out_specs=[VMEM] *...]
    ppermute x11 -> x13, starting transfers between devices: 15.8 us -> 15.2 us  [the longest x4 7.18 us: swap_peers(): return lax.ppermute(x, ('feat', 'dp'), pairs)]
    pallas_call x7, Pallas kernels: 0.59 us -> 0.22 us  [call(): pl.pallas_call(kernel, in_specs=[VMEM] * len(args), out_specs=[VMEM] * le...]
  transfers between devices with their start and end apart: 11 -> 13, of which waited for: 5 -> 8; matrix products, arithmetic and copies ran while one was open for 0% -> 0% of each run, Pallas kernels for 4% -> 7%
where the time goes in v2:
time: 24.6 us; the launch traced here: 24.3 us
  starting transfers between devices  15.2 us (62%)
  Pallas kernels  4.85 us (20%)
  waiting for transfers between devices  3.56 us (14%)
  between operations  0.69 us (3%)
    ppermute x4, starting transfers between devices, swap_peers(): return lax.ppermute(x, ('feat', 'dp'), pairs)  7.18 us
    ppermute x5, starting transfers between devices, swap_chips(): lax.ppermute(x, 'feat', [(i, i ^ 2 * bits + 1) for i in range(lax.axis_si...  6.88 us
    ppermute x5, waiting for transfers between devices, swap_chips(): lax.ppermute(x, 'feat', [(i, i ^ 2 * bits + 1) for i in range(lax.axis_si...  2 us
    pallas_call x1, Pallas kernels, backward_near(): pl.pallas_call(near_kernel, in_specs=[VMEM, hbm, hbm], out_specs=[VMEM] *...  1.57 us
    pallas_call x1, Pallas kernels, first_layer(): pl.pallas_call(functools.partial(first_layer_kernel, group // tile), grid...  1.56 us
    ppermute x4, starting transfers between devices, swap_cores(): lax.ppermute(x, 'feat', [(i, i ^ 1) for i in range(lax.axis_size('feat'))])  1.15 us
    pallas_call x1, Pallas kernels, outputs(): pl.pallas_call(functools.partial(outputs_kernel, codes), in_specs=[VMEM]...  1.05 us
    ppermute x4, waiting for transfers between devices, swap_cores(): lax.ppermute(x, 'feat', [(i, i ^ 1) for i in range(lax.axis_size('feat'))])  0.9 us
  transfers between devices with their start and end apart: 13, of which 8 were waited for; matrix products, arithmetic and copies ran while one was open for 0% of the time, Pallas kernels for 7%

profile of v2, /device:TPU:0, one launch (start us, length us, event | category | flops | bytes accessed | tf_op | source)
XLA Modules:
  0.0 24.3 jit_solution(1230045843230524891)
XLA Ops:
  0.6 1.6 %first_layer.1 = (f32[4,16,512]{2,1,0:T(8,128)S(1)}, f32[4,16,512]{2,1,0:T(8,128)S(1)}, bf16[256,128]{1,0:T(8,128)(2,1)S(1)}, bf16[16,640]{1,0:T(8,128)(2,1)S(1)}) custom-call(bf16[1,128,256]{2,1,0:T(8,128)(2,1)} %feat_hbm.1, s32[10,1,128]{2,1,0:T(1,128)} %bitcast.1, bf16[128,512]{1,0:T(8,128)(2,1)} %w1s_hbm.1, bf16[128,512]{1,0:T(8,128)(2,1)} %w1n_hbm.1, ...), custom_call_target="tpu_custom_call" | custom-call | tf_op jit(solution)/shard_map/first_layer/pallas_call | solution.py:134
  2.2 0.5 %collective-permute-start = (f32[4,16,512]{2,1,0:T(8,128)S(1)}, f32[4,16,512]{2,1,0:T(8,128)S(1)}, u32[]{:S(2)}, u32[]{:S(2)}) collective-permute-start(f32[4,16,512]{2,1,0:T(8,128)S(1)} %get-tuple-element.21), channel_id=1, source_target_pairs={{0,4},{4,0},{8,12},{12,8},{16,20},{20,16},{24,28},{28,24},{1,5},{5... | collective-permute-start | bytes 393224 | tf_op jit(solution)/shard_map/ppermute | solution.py:397
  2.7 2.6 %collective-permute-start.4 = (bf16[16,640]{1,0:T(8,128)(2,1)S(1)}, bf16[16,640]{1,0:T(8,128)(2,1)S(1)}, u32[]{:S(2)}, u32[]{:S(2)}) collective-permute-start(bf16[16,640]{1,0:T(8,128)(2,1)S(1)} %get-tuple-element.26.a_ref), channel_id=1, source_target_pairs={{0,1},{1,0},{2,3},{3,2},{4,6},{5,7},{6,4},{7,5},{8,9},{9,8},{10,11... | collective-permute-start | bytes 61448 | tf_op jit(solution)/shard_map/ppermute | solution.py:408
  5.3 3.5 %collective-permute-start.1 = (f32[16,512]{1,0:T(8,128)S(1)}, f32[16,512]{1,0:T(8,128)S(1)}, u32[]{:S(2)}, u32[]{:S(2)}) collective-permute-start(f32[16,512]{1,0:T(8,128)S(1)} %get-tuple-element.23), channel_id=1, source_target_pairs={{0,28},{4,24},{8,20},{12,16},{16,12},{20,8},{24,4},{28,0},{1,29},{... | collective-permute-start | bytes 98312 | tf_op jit(solution)/shard_map/ppermute | solution.py:401
  8.8 0.6 %collective-permute-start.3 = (f32[16,512]{1,0:T(8,128)S(1)}, f32[16,512]{1,0:T(8,128)S(1)}, u32[]{:S(2)}, u32[]{:S(2)}) collective-permute-start(f32[16,512]{1,0:T(8,128)S(1)} %get-tuple-element.25), channel_id=1, source_target_pairs={{0,12},{4,8},{8,4},{12,0},{16,28},{20,24},{24,20},{28,16},{1,13},{... | collective-permute-start | bytes 98312 | tf_op jit(solution)/shard_map/ppermute | solution.py:401
  9.3 1.6 %collective-permute-start.5 = (bf16[32,640]{1,0:T(8,128)(2,1)S(1)}, bf16[32,640]{1,0:T(8,128)(2,1)S(1)}, u32[]{:S(2)}, u32[]{:S(2)}) collective-permute-start(bf16[32,640]{1,0:T(8,128)(2,1)S(1)} %join.3.near_ref), channel_id=1, source_target_pairs={{0,2},{1,3},{2,0},{3,1},{4,5},{5,4},{6,7},{7,6},{8,10},{9,11},{10,... | collective-permute-start | bytes 122888 | tf_op jit(solution)/shard_map/ppermute | solution.py:408
  10.9 1.6 %backward_near.1 = (f32[16,512]{1,0:T(8,128)S(1)}, f32[32,512]{1,0:T(8,128)S(1)}, bf16[512,512]{1,0:T(8,128)(2,1)S(1)}, bf16[512,512]{1,0:T(8,128)(2,1)S(1)}) custom-call(bf16[32,640]{1,0:T(8,128)(2,1)S(1)} %join.3.near_ref, bf16[512,512]{1,0:T(8,128)(2,1)} %w2s_hbm.1, bf16[512,512]{1,0:T(8,128)(2,1)} %w2n_hbm.1), custom_call_target="tpu_custom_call" | custom-call | tf_op jit(solution)/shard_map/backward_near/pallas_call | solution.py:234
  12.5 0.5 %collective-permute-done.2.refs_2_ = f32[16,512]{1,0:T(8,128)S(1)} collective-permute-done((f32[16,512]{1,0:T(8,128)S(1)}, f32[16,512]{1,0:T(8,128)S(1)}, u32[]{:S(2)}, u32[]{:S(2)}) %collective-permute-start.2) | collective-permute-done | bytes 32800 | tf_op jit(solution)/shard_map/ppermute | solution.py:401
  13.0 0.4 %collective-permute-done.5.far_ref = bf16[32,640]{1,0:T(8,128)(2,1)S(1)} collective-permute-done((bf16[32,640]{1,0:T(8,128)(2,1)S(1)}, bf16[32,640]{1,0:T(8,128)(2,1)S(1)}, u32[]{:S(2)}, u32[]{:S(2)}) %collective-permute-start.5) | collective-permute-done | bytes 40992 | tf_op jit(solution)/shard_map/ppermute | solution.py:408
  13.4 0.4 %second_backward.1 = (bf16[16,512]{1,0:T(8,128)(2,1)S(1)}, bf16[16,64]{1,0:T(8,128)(2,1)S(1)}, f32[16,128]{1,0:T(8,128)S(1)}) custom-call(bf16[32,640]{1,0:T(8,128)(2,1)S(1)} %join.3.near_ref, bf16[32,640]{1,0:T(8,128)(2,1)S(1)} %collective-permute-done.5.far_ref, f32[16,512]{1,0:T(8,128)S(1)} %get-tuple-element.27.self_ref, ...), custom_call_target="tpu_custom_call" | custom-call | tf_op jit(solution)/shard_map/second_backward/pallas_call | solution.py:309
  13.9 1.7 %collective-permute-start.7 = (bf16[1,16,512]{2,1,0:T(8,128)(2,1)S(1)}, bf16[1,16,512]{2,1,0:T(8,128)(2,1)S(1)}, u32[]{:S(2)}, u32[]{:S(2)}) collective-permute-start(bf16[1,16,512]{2,1,0:T(8,128)(2,1)S(1)} %get-tuple-element.32.a_ref.refs_0_), channel_id=1, source_target_pairs={{0,20},{4,16},{8,28},{12,24},{16,4},{20,0},{24,12},{28,8},{1,21},{... | collective-permute-start | bytes 49160 | tf_op jit(solution)/shard_map/ppermute | solution.py:401
  15.6 1.5 %collective-permute-start.6 = (bf16[16,512]{1,0:T(8,128)(2,1)S(1)}, bf16[16,512]{1,0:T(8,128)(2,1)S(1)}, u32[]{:S(2)}, u32[]{:S(2)}) collective-permute-start(bf16[16,512]{1,0:T(8,128)(2,1)S(1)} %get-tuple-element.31.a_ref.hidden_ref), channel_id=1, source_target_pairs={{0,1},{1,0},{2,3},{3,2},{4,6},{5,7},{6,4},{7,5},{8,9},{9,8},{10,11... | collective-permute-start | bytes 49160 | tf_op jit(solution)/shard_map/ppermute | solution.py:408
  17.1 0.9 %collective-permute-done.7.b_ref.refs_1_ = bf16[1,16,512]{2,1,0:T(8,128)(2,1)S(1)} collective-permute-done((bf16[1,16,512]{2,1,0:T(8,128)(2,1)S(1)}, bf16[1,16,512]{2,1,0:T(8,128)(2,1)S(1)}, u32[]{:S(2)}, u32[]{:S(2)}) %collective-permute-start.7) | collective-permute-done | bytes 16416 | tf_op jit(solution)/shard_map/ppermute | solution.py:401
  18.0 1.1 %collective-permute-start.9 = (bf16[2,16,512]{2,1,0:T(8,128)(2,1)S(1)}, bf16[2,16,512]{2,1,0:T(8,128)(2,1)S(1)}, u32[]{:S(2)}, u32[]{:S(2)}) collective-permute-start(bf16[2,16,512]{2,1,0:T(8,128)(2,1)S(1)} %join.4.refs_0_), channel_id=1, source_target_pairs={{0,12},{4,8},{8,4},{12,0},{16,28},{20,24},{24,20},{28,16},{1,13},{... | collective-permute-start | bytes 98312 | tf_op jit(solution)/shard_map/ppermute | solution.py:401
  19.2 0.2 collective-permute-done.6.b_ref
  19.3 1.5 %collective-permute-start.8 = (bf16[32,512]{1,0:T(8,128)(2,1)S(1)}, bf16[32,512]{1,0:T(8,128)(2,1)S(1)}, u32[]{:S(2)}, u32[]{:S(2)}) collective-permute-start(bf16[32,512]{1,0:T(8,128)(2,1)S(1)} %join.5.near_ref), channel_id=1, source_target_pairs={{0,2},{1,3},{2,0},{3,1},{4,5},{5,4},{6,7},{7,6},{8,10},{9,11},{10,... | collective-permute-start | bytes 98312 | tf_op jit(solution)/shard_map/ppermute | solution.py:408
  20.8 0.6 %collective-permute-done.9.refs_2_ = bf16[2,16,512]{2,1,0:T(8,128)(2,1)S(1)} collective-permute-done((bf16[2,16,512]{2,1,0:T(8,128)(2,1)S(1)}, bf16[2,16,512]{2,1,0:T(8,128)(2,1)S(1)}, u32[]{:S(2)}, u32[]{:S(2)}) %collective-permute-start.9) | collective-permute-done | bytes 32800 | tf_op jit(solution)/shard_map/ppermute | solution.py:401
  21.4 0.1 collective-permute-start.12
  21.6 0.4 %collective-permute-start.10 = (bf16[1,16,512]{2,1,0:T(8,128)(2,1)S(1)}, bf16[1,16,512]{2,1,0:T(8,128)(2,1)S(1)}, u32[]{:S(2)}, u32[]{:S(2)}) collective-permute-start(bf16[1,16,512]{2,1,0:T(8,128)(2,1)S(1)} %get-tuple-element.32.a_ref.refs_0_), channel_id=1, source_target_pairs={{0,4},{4,0},{8,12},{12,8},{16,20},{20,16},{24,28},{28,24},{1,5},{5... | collective-permute-start | bytes 49160 | tf_op jit(solution)/shard_map/ppermute | solution.py:397
  22.0 0.1 collective-permute-start.11
  22.1 0.2 own_part.1.own_ref
  22.2 0.6 %collective-permute-done.10.refs_3_ = bf16[1,16,512]{2,1,0:T(8,128)(2,1)S(1)} collective-permute-done((bf16[1,16,512]{2,1,0:T(8,128)(2,1)S(1)}, bf16[1,16,512]{2,1,0:T(8,128)(2,1)S(1)}, u32[]{:S(2)}, u32[]{:S(2)}) %collective-permute-start.10) | collective-permute-done | bytes 16416 | tf_op jit(solution)/shard_map/ppermute | solution.py:397
  22.8 0.3 %collective-permute-done.11.refs_4_ = bf16[1,16,512]{2,1,0:T(8,128)(2,1)S(1)} collective-permute-done((bf16[1,16,512]{2,1,0:T(8,128)(2,1)S(1)}, bf16[1,16,512]{2,1,0:T(8,128)(2,1)S(1)}, u32[]{:S(2)}, u32[]{:S(2)}) %collective-permute-start.11) | collective-permute-done | bytes 16416 | tf_op jit(solution)/shard_map/ppermute | solution.py:397
  23.3 1.1 %outputs.1 = (bf16[1,1,16,512]{3,2,1,0:T(8,128)(2,1)}, f32[1,128,512]{2,1,0:T(8,128)}, f32[1,128,512]{2,1,0:T(8,128)}) custom-call(bf16[32,512]{1,0:T(8,128)(2,1)S(1)} %join.5.near_ref, bf16[32,512]{1,0:T(8,128)(2,1)S(1)} %collective-permute-done.8.far_ref, bf16[16,64]{1,0:T(8,128)(2,1)S(1)} %get-tuple-element.33.table_ref, ...), custom_call_target="tpu_custom_call" | custom-call | tf_op jit(solution)/shard_map/outputs/pallas_call | solution.py:384
  (13 shorter events, 0.2 us)
Async XLA Ops:
  2.2 3.1 %collective-permute-start = (f32[4,16,512]{2,1,0:T(8,128)S(1)}, f32[4,16,512]{2,1,0:T(8,128)S(1)}, u32[]{:S(2)}, u32[]{:S(2)}) collective-permute-start(f32[4,16,512]{2,1,0:T(8,128)S(1)} %get-tuple-element.21), channel_id=1, source_target_pairs={{0,4},{4,0},{8,12},{12,8},{16,20},{20,16},{24,28},{28,24},{1,5},{5... | collective-permute-start | bytes 393224 | tf_op jit(solution)/shard_map/ppermute | solution.py:397
  2.7 6.6 %collective-permute-start.4 = (bf16[16,640]{1,0:T(8,128)(2,1)S(1)}, bf16[16,640]{1,0:T(8,128)(2,1)S(1)}, u32[]{:S(2)}, u32[]{:S(2)}) collective-permute-start(bf16[16,640]{1,0:T(8,128)(2,1)S(1)} %get-tuple-element.26.a_ref), channel_id=1, source_target_pairs={{0,1},{1,0},{2,3},{3,2},{4,6},{5,7},{6,4},{7,5},{8,9},{9,8},{10,11... | collective-permute-start | bytes 61448 | tf_op jit(solution)/shard_map/ppermute | solution.py:408
  5.3 7.2 %collective-permute-start.1 = (f32[16,512]{1,0:T(8,128)S(1)}, f32[16,512]{1,0:T(8,128)S(1)}, u32[]{:S(2)}, u32[]{:S(2)}) collective-permute-start(f32[16,512]{1,0:T(8,128)S(1)} %get-tuple-element.23), channel_id=1, source_target_pairs={{0,28},{4,24},{8,20},{12,16},{16,12},{20,8},{24,4},{28,0},{1,29},{... | collective-permute-start | bytes 98312 | tf_op jit(solution)/shard_map/ppermute | solution.py:401
  8.8 4.2 %collective-permute-start.2 = (f32[16,512]{1,0:T(8,128)S(1)}, f32[16,512]{1,0:T(8,128)S(1)}, u32[]{:S(2)}, u32[]{:S(2)}) collective-permute-start(f32[16,512]{1,0:T(8,128)S(1)} %get-tuple-element.24), channel_id=1, source_target_pairs={{0,20},{4,16},{8,28},{12,24},{16,4},{20,0},{24,12},{28,8},{1,21},{... | collective-permute-start | bytes 98312 | tf_op jit(solution)/shard_map/ppermute | solution.py:401
  8.8 4.2 %collective-permute-start.3 = (f32[16,512]{1,0:T(8,128)S(1)}, f32[16,512]{1,0:T(8,128)S(1)}, u32[]{:S(2)}, u32[]{:S(2)}) collective-permute-start(f32[16,512]{1,0:T(8,128)S(1)} %get-tuple-element.25), channel_id=1, source_target_pairs={{0,12},{4,8},{8,4},{12,0},{16,28},{20,24},{24,20},{28,16},{1,13},{... | collective-permute-start | bytes 98312 | tf_op jit(solution)/shard_map/ppermute | solution.py:401
  9.3 4.1 %collective-permute-start.5 = (bf16[32,640]{1,0:T(8,128)(2,1)S(1)}, bf16[32,640]{1,0:T(8,128)(2,1)S(1)}, u32[]{:S(2)}, u32[]{:S(2)}) collective-permute-start(bf16[32,640]{1,0:T(8,128)(2,1)S(1)} %join.3.near_ref), channel_id=1, source_target_pairs={{0,2},{1,3},{2,0},{3,1},{4,5},{5,4},{6,7},{7,6},{8,10},{9,11},{10,... | collective-permute-start | bytes 122888 | tf_op jit(solution)/shard_map/ppermute | solution.py:408
  13.9 4.2 %collective-permute-start.7 = (bf16[1,16,512]{2,1,0:T(8,128)(2,1)S(1)}, bf16[1,16,512]{2,1,0:T(8,128)(2,1)S(1)}, u32[]{:S(2)}, u32[]{:S(2)}) collective-permute-start(bf16[1,16,512]{2,1,0:T(8,128)(2,1)S(1)} %get-tuple-element.32.a_ref.refs_0_), channel_id=1, source_target_pairs={{0,20},{4,16},{8,28},{12,24},{16,4},{20,0},{24,12},{28,8},{1,21},{... | collective-permute-start | bytes 49160 | tf_op jit(solution)/shard_map/ppermute | solution.py:401
  15.6 3.7 %collective-permute-start.6 = (bf16[16,512]{1,0:T(8,128)(2,1)S(1)}, bf16[16,512]{1,0:T(8,128)(2,1)S(1)}, u32[]{:S(2)}, u32[]{:S(2)}) collective-permute-start(bf16[16,512]{1,0:T(8,128)(2,1)S(1)} %get-tuple-element.31.a_ref.hidden_ref), channel_id=1, source_target_pairs={{0,1},{1,0},{2,3},{3,2},{4,6},{5,7},{6,4},{7,5},{8,9},{9,8},{10,11... | collective-permute-start | bytes 49160 | tf_op jit(solution)/shard_map/ppermute | solution.py:408
  18.0 3.4 %collective-permute-start.9 = (bf16[2,16,512]{2,1,0:T(8,128)(2,1)S(1)}, bf16[2,16,512]{2,1,0:T(8,128)(2,1)S(1)}, u32[]{:S(2)}, u32[]{:S(2)}) collective-permute-start(bf16[2,16,512]{2,1,0:T(8,128)(2,1)S(1)} %join.4.refs_0_), channel_id=1, source_target_pairs={{0,12},{4,8},{8,4},{12,0},{16,28},{20,24},{24,20},{28,16},{1,13},{... | collective-permute-start | bytes 98312 | tf_op jit(solution)/shard_map/ppermute | solution.py:401
  19.3 3.9 %collective-permute-start.8 = (bf16[32,512]{1,0:T(8,128)(2,1)S(1)}, bf16[32,512]{1,0:T(8,128)(2,1)S(1)}, u32[]{:S(2)}, u32[]{:S(2)}) collective-permute-start(bf16[32,512]{1,0:T(8,128)(2,1)S(1)} %join.5.near_ref), channel_id=1, source_target_pairs={{0,2},{1,3},{2,0},{3,1},{4,5},{5,4},{6,7},{7,6},{8,10},{9,11},{10,... | collective-permute-start | bytes 98312 | tf_op jit(solution)/shard_map/ppermute | solution.py:408
  21.4 1.8 %collective-permute-start.12 = (bf16[2,16,512]{2,1,0:T(8,128)(2,1)S(1)}, bf16[2,16,512]{2,1,0:T(8,128)(2,1)S(1)}, u32[]{:S(2)}, u32[]{:S(2)}) collective-permute-start(bf16[2,16,512]{2,1,0:T(8,128)(2,1)S(1)} %collective-permute-done.9.refs_2_), channel_id=1, source_target_pairs={{0,4},{4,0},{8,12},{12,8},{16,20},{20,16},{24,28},{28,24},{1,5},{5... | collective-permute-start | bytes 98312 | tf_op jit(solution)/shard_map/ppermute | solution.py:397
  21.6 1.2 %collective-permute-start.10 = (bf16[1,16,512]{2,1,0:T(8,128)(2,1)S(1)}, bf16[1,16,512]{2,1,0:T(8,128)(2,1)S(1)}, u32[]{:S(2)}, u32[]{:S(2)}) collective-permute-start(bf16[1,16,512]{2,1,0:T(8,128)(2,1)S(1)} %get-tuple-element.32.a_ref.refs_0_), channel_id=1, source_target_pairs={{0,4},{4,0},{8,12},{12,8},{16,20},{20,16},{24,28},{28,24},{1,5},{5... | collective-permute-start | bytes 49160 | tf_op jit(solution)/shard_map/ppermute | solution.py:397
  22.0 1.2 %collective-permute-start.11 = (bf16[1,16,512]{2,1,0:T(8,128)(2,1)S(1)}, bf16[1,16,512]{2,1,0:T(8,128)(2,1)S(1)}, u32[]{:S(2)}, u32[]{:S(2)}) collective-permute-start(bf16[1,16,512]{2,1,0:T(8,128)(2,1)S(1)} %collective-permute-done.7.b_ref.refs_1_), channel_id=1, source_target_pairs={{0,4},{4,0},{8,12},{12,8},{16,20},{20,16},{24,28},{28,24},{1,5},{5... | collective-permute-start | bytes 49160 | tf_op jit(solution)/shard_map/ppermute | solution.py:397

commit v3 on v2

--- a/solution.py
+++ b/solution.py
@@ -205,16 +205,6 @@
     return call(join_kernel, "join", (a, b, *after), [((2 * a.shape[0],) + a.shape[1:], a.dtype)], cost)[0]
 
 
-def place(scratch, near, far, size, me):
-    count = near.shape[0] // size
-    core = lax.axis_index("feat") % 2
-    for s in range(2 * count):
-        ref, at = (near, s) if s < count else (far, s - count)
-        code = code_of(s, levels_of(2 * count), core)
-        to = pl.multiple_of(lax.bitwise_xor(me, code) * size, size)
-        scratch[pl.ds(to, size), :] = ref[at * size : (at + 1) * size, :]
-
-
 def near_kernel(near_ref, w2s_hbm, w2n_hbm, self_ref, near_grad_ref, w2s_ref, w2n_ref, sems):
     pairs = ((w2s_hbm, w2s_ref), (w2n_hbm, w2n_ref))
     copies = [pltpu.make_async_copy(src, dst, sems.at[n]) for n, (src, dst) in enumerate(pairs)]
@@ -243,41 +233,41 @@
 
 
 def backward_kernel(
-    peers, slots, near_ref, far_ref, self_ref, near_grad_ref, w2n_ref, grad_ref, table_ref, degree_ref,
-    tables, grads,
+    peers, slots, near_ref, far_ref, self_ref, near_grad_ref, w2n_ref, grad_ref, table_ref, degree_ref
 ):
-    me = lax.axis_index("dp")
+    me, core = lax.axis_index("dp"), lax.axis_index("feat") % 2
     rows, width = self_ref.shape
-    place(tables, near_ref.at[:, width:], far_ref.at[:, width:], rows, me)
+    lanes = peers * slots
     far_grad = lax.dot_general(far_ref[:, :width], w2n_ref[...], NT, preferred_element_type=F32)
-    place(grads, near_grad_ref, far_grad, rows, me)
-    lanes = peers * slots
-
-    def table(d, which):
-        return tables[d * rows : (d + 1) * rows, which * lanes : (which + 1) * lanes].astype(F32)
+    grads = jnp.concatenate([near_grad_ref[...], far_grad], axis=0)
+    peer = [lax.bitwise_xor(me, code_of(s, levels_of(peers), core)) for s in range(peers)]
+
+    def table(s, which):
+        ref, at = (near_ref, s) if s < peers // 2 else (far_ref, s - peers // 2)
+        at_lanes = slice(width + which * lanes, width + (which + 1) * lanes)
+        return ref[at * rows : (at + 1) * rows, at_lanes].astype(F32)
 
     block_of = iota((rows, lanes), 1) // slots
-    diagonal = iota((rows, lanes), 0) == block_of
-    mine = iota((rows, lanes), 0) == me
+    row_of = iota((rows, lanes), 0)
+    diagonal = row_of == block_of
 
     def pick(where, x):
         return jnp.sum(jnp.where(where, x, 0.0), axis=0, keepdims=True)
 
     def crossed(which):
-        return sum(jnp.where(block_of == d, table(d, which), 0.0) for d in range(peers))
-
-    def own(which):
-        return sum(jnp.where(me == d, table(d, which), 0.0) for d in range(peers))
+        return sum(jnp.where(block_of == peer[s], table(s, which), 0.0) for s in range(peers))
 
     live_in = crossed(2)
+    mine = row_of == me
     target_there = pick(mine, crossed(0))
     row_there = pick(mine, crossed(1))
-    own_target, own_row, own_live = [pick(diagonal, own(which)) for which in range(3)]
+    own_target, own_row, own_live = [pick(diagonal, table(0, which)) for which in range(3)]
     own_live_in = pick(mine, live_in)
 
-    local = iota((rows, lanes), 0).astype(F32)
+    local = row_of.astype(F32)
     every = iota((peers * rows, lanes), 0)
-    same = every // rows == iota((peers * rows, lanes), 1) // slots
+    peer_of = sum(jnp.where(every // rows == s, peer[s], 0) for s in range(peers))
+    same = peer_of == iota((peers * rows, lanes), 1) // slots
     every_local = (every % rows).astype(F32)
 
     back = jnp.where(local == own_row, own_live, 0.0).astype(BF16)
@@ -288,13 +278,12 @@
     table_ref[...] = lax.dot_general(into.astype(BF16), origin, NT, preferred_element_type=F32).astype(BF16)
     degree_ref[...] = jnp.broadcast_to(jnp.sum(into, axis=1, keepdims=True), degree_ref.shape)
 
-    own_columns = iota(back_table.shape, 1) - me * rows
-    back_table = back_table + (own_columns == iota(back_table.shape, 0)).astype(F32)
+    back_table = back_table + (iota(back_table.shape, 1) == iota(back_table.shape, 0)).astype(F32)
     degrees = []
-    for e in range(peers):
-        hit = jnp.where(local == pick(diagonal, table(e, 0)), live_in[e : e + 1, :], 0.0)
+    for s in range(peers):
+        hit = jnp.where(local == pick(diagonal, table(s, 0)), pick(row_of == peer[s], live_in), 0.0)
         degrees.append(jnp.sum(hit, axis=1, keepdims=True))
-    grad_mean = grads[...] / (1.0 + jnp.concatenate(degrees, axis=0))
+    grad_mean = grads / (1.0 + jnp.concatenate(degrees, axis=0))
     high = grad_mean.astype(BF16)
     low = (grad_mean - high.astype(F32)).astype(BF16)
     back_table = back_table.astype(BF16)
@@ -315,10 +304,6 @@
             jax.ShapeDtypeStruct((rows_dev, peers * rows_dev), BF16),
             jax.ShapeDtypeStruct((rows_dev, 128), F32),
         ],
-        scratch_shapes=[
-            pltpu.VMEM((peers * rows_dev, near.shape[1] - width), BF16),
-            pltpu.VMEM((peers * rows_dev, width), F32),
-        ],
         name="second_backward", compiler_params=PARAMS,
         cost_estimate=pl.CostEstimate(flops=BACKWARD_COST, bytes_accessed=0, transcendentals=0),
     )(near, far, grad_self, near_grad, w2n)
@@ -345,8 +330,8 @@
 
 
 def outputs_kernel(codes, near_ref, far_ref, table_ref, degree_ref, own_ref, w2n_ref, *refs):
-    grad_refs, (both_ref, out_hbm, self_hbm, neigh_hbm) = refs[:-10], refs[-10:-6]
-    out_ref, self_ref, neigh_ref, grad_scratch, hidden_scratch, sems = refs[-6:]
+    grad_refs, (both_ref, out_hbm, self_hbm, neigh_hbm) = refs[:-9], refs[-9:-5]
+    out_ref, self_ref, neigh_ref, grad_scratch, sems = refs[-5:]
     depth = both_ref.shape[0] // 2
     half = depth // 2 if depth % 32 == 0 else depth
     pieces = [(ref, hbm, n, at) for n, (ref, hbm) in enumerate(((self_ref, self_hbm), (neigh_ref, neigh_hbm)))
@@ -366,10 +351,10 @@
         ref[0, at : at + half] = jnp.dot(columns, grad_pre, preferred_element_type=F32)
         copy.start()
 
-    width = hidden_scratch.shape[1]
-    place(hidden_scratch, near_ref.at[:, :width], far_ref.at[:, :width], rows, lax.axis_index("dp"))
-    neigh_sum = jnp.dot(table_ref[...], hidden_scratch[...], preferred_element_type=F32)
-    mean_two = ((near_ref[0:rows, :width].astype(F32) + neigh_sum) / (1.0 + degree_ref[:, 0:1])).astype(BF16)
+    count = near_ref.shape[0]
+    neigh_sum = jnp.dot(table_ref[:, :count], near_ref[...], preferred_element_type=F32)
+    neigh_sum = neigh_sum + jnp.dot(table_ref[:, count:], far_ref[...], preferred_element_type=F32)
+    mean_two = ((near_ref[0:rows, :].astype(F32) + neigh_sum) / (1.0 + degree_ref[:, 0:1])).astype(BF16)
     out = own_ref[...] + jnp.dot(mean_two, w2n_ref[...], preferred_element_type=F32)
     out_ref[0, 0] = out.astype(BF16)
     copies[-1].start()
@@ -387,8 +372,7 @@
         out_specs=[pl.BlockSpec(memory_space=pltpu.HBM)] * 3,
         out_shape=[out, grad, grad],
         scratch_shapes=[pltpu.VMEM(a.shape, a.dtype) for a in (out, grad, grad)]
-        + [pltpu.VMEM((group, width), BF16), pltpu.VMEM((table.shape[1], w2n.shape[0]), BF16)]
-        + [pltpu.SemaphoreType.DMA((5,))],
+        + [pltpu.VMEM((group, width), BF16), pltpu.SemaphoreType.DMA((5,))],
         name="outputs", compiler_params=PARAMS,
     )(near, far, table, degree, own, w2n, *grads, both)
 
@@ -422,7 +406,8 @@
         features, neigh_lists, w1_self, w1_neigh, send_rows, send_count, recv_target, out_grad
     )
     parts = list(pair_sum(keep, swap_cores(send)))
-    far = [swap_chips(parts[s], s) for s in range(chips - 1, 0, -1)]
+    order = [chips // 2] + [s for s in range(chips - 1, 0, -1) if s != chips // 2]
+    far = [swap_chips(parts[s], s) for s in order]
     aux_near, aux_far = gather_peers(aux, INDEX_COST, parts[:1])
     grad, table, degree, w2_self, w2_neigh = backward(
         aux_near, aux_far, w2_self, w2_neigh, peers, slots, rows_dev

time: 24.6 us -> 24.3 us (0.988)
  starting transfers between devices: 15.2 us -> 14.4 us
  waiting for transfers between devices: 3.56 us -> 4.04 us
    ppermute x5, starting transfers between devices: 6.88 us -> 5.86 us  [swap_chips(): lax.ppermute(x, 'feat', [(i, i ^ 2 * bits + 1) for i in range(lax.axis_si...]
    ppermute x5, waiting for transfers between devices: 2 us -> 2.47 us  [swap_chips(): lax.ppermute(x, 'feat', [(i, i ^ 2 * bits + 1) for i in range(lax.axis_si...]
  transfers between devices with their start and end apart: 13 -> 13, of which waited for: 8 -> 7; matrix products, arithmetic and copies ran while one was open for 0% -> 0% of each run, Pallas kernels for 7% -> 7%
where the time goes in v3:
time: 24.3 us; the launch traced here: 24 us
  starting transfers between devices  14.4 us (59%)
  Pallas kernels  4.83 us (20%)
  waiting for transfers between devices  4.04 us (17%)
  between operations  0.69 us (3%)
    ppermute x4, starting transfers between devices, swap_peers(): return lax.ppermute(x, ('feat', 'dp'), pairs)  7.22 us
    ppermute x5, starting transfers between devices, swap_chips(): lax.ppermute(x, 'feat', [(i, i ^ 2 * bits + 1) for i in range(lax.axis_si...  5.86 us
    ppermute x5, waiting for transfers between devices, swap_chips(): lax.ppermute(x, 'feat', [(i, i ^ 2 * bits + 1) for i in range(lax.axis_si...  2.47 us
    pallas_call x1, Pallas kernels, backward_near(): pl.pallas_call(near_kernel, in_specs=[VMEM, hbm, hbm], out_specs=[VMEM] *...  1.57 us
    pallas_call x1, Pallas kernels, first_layer(): pl.pallas_call(functools.partial(first_layer_kernel, group // tile), grid...  1.56 us
    ppermute x4, starting transfers between devices, swap_cores(): lax.ppermute(x, 'feat', [(i, i ^ 1) for i in range(lax.axis_size('feat'))])  1.36 us
    pallas_call x1, Pallas kernels, outputs(): pl.pallas_call(functools.partial(outputs_kernel, codes), in_specs=[VMEM]...  1.05 us
    ppermute x4, waiting for transfers between devices, swap_peers(): return lax.ppermute(x, ('feat', 'dp'), pairs)  0.89 us
  transfers between devices with their start and end apart: 13, of which 7 were waited for; matrix products, arithmetic and copies ran while one was open for 0% of the time, Pallas kernels for 7%

profile of v3, /device:TPU:0, one launch (start us, length us, event | category | flops | bytes accessed | tf_op | source)
XLA Modules:
  0.0 24.0 jit_solution(2849018227130615059)
XLA Ops:
  0.6 1.6 %first_layer.1 = (f32[4,16,512]{2,1,0:T(8,128)S(1)}, f32[4,16,512]{2,1,0:T(8,128)S(1)}, bf16[256,128]{1,0:T(8,128)(2,1)S(1)}, bf16[16,640]{1,0:T(8,128)(2,1)S(1)}) custom-call(bf16[1,128,256]{2,1,0:T(8,128)(2,1)} %feat_hbm.1, s32[10,1,128]{2,1,0:T(1,128)} %bitcast.1, bf16[128,512]{1,0:T(8,128)(2,1)} %w1s_hbm.1, bf16[128,512]{1,0:T(8,128)(2,1)} %w1n_hbm.1, ...), custom_call_target="tpu_custom_call" | custom-call | tf_op jit(solution)/shard_map/first_layer/pallas_call | solution.py:134
  2.2 0.5 %collective-permute-start = (f32[4,16,512]{2,1,0:T(8,128)S(1)}, f32[4,16,512]{2,1,0:T(8,128)S(1)}, u32[]{:S(2)}, u32[]{:S(2)}) collective-permute-start(f32[4,16,512]{2,1,0:T(8,128)S(1)} %get-tuple-element.21), channel_id=1, source_target_pairs={{0,4},{4,0},{8,12},{12,8},{16,20},{20,16},{24,28},{28,24},{1,5},{5... | collective-permute-start | bytes 393224 | tf_op jit(solution)/shard_map/ppermute | solution.py:381
  2.7 2.6 %collective-permute-start.4 = (bf16[16,640]{1,0:T(8,128)(2,1)S(1)}, bf16[16,640]{1,0:T(8,128)(2,1)S(1)}, u32[]{:S(2)}, u32[]{:S(2)}) collective-permute-start(bf16[16,640]{1,0:T(8,128)(2,1)S(1)} %get-tuple-element.26.a_ref), channel_id=1, source_target_pairs={{0,1},{1,0},{2,3},{3,2},{4,6},{5,7},{6,4},{7,5},{8,9},{9,8},{10,11... | collective-permute-start | bytes 61448 | tf_op jit(solution)/shard_map/ppermute | solution.py:392
  5.3 2.4 %collective-permute-start.1 = (f32[16,512]{1,0:T(8,128)S(1)}, f32[16,512]{1,0:T(8,128)S(1)}, u32[]{:S(2)}, u32[]{:S(2)}) collective-permute-start(f32[16,512]{1,0:T(8,128)S(1)} %get-tuple-element.23), channel_id=1, source_target_pairs={{0,20},{4,16},{8,28},{12,24},{16,4},{20,0},{24,12},{28,8},{1,21},{... | collective-permute-start | bytes 98312 | tf_op jit(solution)/shard_map/ppermute | solution.py:385
  7.7 1.3 %collective-permute-start.2 = (f32[16,512]{1,0:T(8,128)S(1)}, f32[16,512]{1,0:T(8,128)S(1)}, u32[]{:S(2)}, u32[]{:S(2)}) collective-permute-start(f32[16,512]{1,0:T(8,128)S(1)} %get-tuple-element.24), channel_id=1, source_target_pairs={{0,28},{4,24},{8,20},{12,16},{16,12},{20,8},{24,4},{28,0},{1,29},{... | collective-permute-start | bytes 98312 | tf_op jit(solution)/shard_map/ppermute | solution.py:385
  9.0 0.2 collective-permute-start.3
  9.3 1.6 %collective-permute-start.5 = (bf16[32,640]{1,0:T(8,128)(2,1)S(1)}, bf16[32,640]{1,0:T(8,128)(2,1)S(1)}, u32[]{:S(2)}, u32[]{:S(2)}) collective-permute-start(bf16[32,640]{1,0:T(8,128)(2,1)S(1)} %join.3.near_ref), channel_id=1, source_target_pairs={{0,2},{1,3},{2,0},{3,1},{4,5},{5,4},{6,7},{7,6},{8,10},{9,11},{10,... | collective-permute-start | bytes 122888 | tf_op jit(solution)/shard_map/ppermute | solution.py:392
  10.8 1.6 %backward_near.1 = (f32[16,512]{1,0:T(8,128)S(1)}, f32[32,512]{1,0:T(8,128)S(1)}, bf16[512,512]{1,0:T(8,128)(2,1)S(1)}, bf16[512,512]{1,0:T(8,128)(2,1)S(1)}) custom-call(bf16[32,640]{1,0:T(8,128)(2,1)S(1)} %join.3.near_ref, bf16[512,512]{1,0:T(8,128)(2,1)} %w2s_hbm.1, bf16[512,512]{1,0:T(8,128)(2,1)} %w2n_hbm.1), custom_call_target="tpu_custom_call" | custom-call | tf_op jit(solution)/shard_map/backward_near/pallas_call | solution.py:224
  12.4 0.6 %collective-permute-done.2.refs_2_ = f32[16,512]{1,0:T(8,128)S(1)} collective-permute-done((f32[16,512]{1,0:T(8,128)S(1)}, f32[16,512]{1,0:T(8,128)S(1)}, u32[]{:S(2)}, u32[]{:S(2)}) %collective-permute-start.2) | collective-permute-done | bytes 32800 | tf_op jit(solution)/shard_map/ppermute | solution.py:385
  13.0 0.3 %collective-permute-done.5.far_ref = bf16[32,640]{1,0:T(8,128)(2,1)S(1)} collective-permute-done((bf16[32,640]{1,0:T(8,128)(2,1)S(1)}, bf16[32,640]{1,0:T(8,128)(2,1)S(1)}, u32[]{:S(2)}, u32[]{:S(2)}) %collective-permute-start.5) | collective-permute-done | bytes 40992 | tf_op jit(solution)/shard_map/ppermute | solution.py:392
  13.3 0.4 %second_backward.1 = (bf16[16,512]{1,0:T(8,128)(2,1)S(1)}, bf16[16,64]{1,0:T(8,128)(2,1)S(1)}, f32[16,128]{1,0:T(8,128)S(1)}) custom-call(bf16[32,640]{1,0:T(8,128)(2,1)S(1)} %join.3.near_ref, bf16[32,640]{1,0:T(8,128)(2,1)S(1)} %collective-permute-done.5.far_ref, f32[16,512]{1,0:T(8,128)S(1)} %get-tuple-element.27.self_ref, ...), custom_call_target="tpu_custom_call" | custom-call | tf_op jit(solution)/shard_map/second_backward/pallas_call | solution.py:298
  13.8 1.4 %collective-permute-start.7 = (bf16[1,16,512]{2,1,0:T(8,128)(2,1)S(1)}, bf16[1,16,512]{2,1,0:T(8,128)(2,1)S(1)}, u32[]{:S(2)}, u32[]{:S(2)}) collective-permute-start(bf16[1,16,512]{2,1,0:T(8,128)(2,1)S(1)} %get-tuple-element.32.a_ref.refs_0_), channel_id=1, source_target_pairs={{0,20},{4,16},{8,28},{12,24},{16,4},{20,0},{24,12},{28,8},{1,21},{... | collective-permute-start | bytes 49160 | tf_op jit(solution)/shard_map/ppermute | solution.py:385
  15.2 1.3 %collective-permute-start.6 = (bf16[16,512]{1,0:T(8,128)(2,1)S(1)}, bf16[16,512]{1,0:T(8,128)(2,1)S(1)}, u32[]{:S(2)}, u32[]{:S(2)}) collective-permute-start(bf16[16,512]{1,0:T(8,128)(2,1)S(1)} %get-tuple-element.31.a_ref.hidden_ref), channel_id=1, source_target_pairs={{0,1},{1,0},{2,3},{3,2},{4,6},{5,7},{6,4},{7,5},{8,9},{9,8},{10,11... | collective-permute-start | bytes 49160 | tf_op jit(solution)/shard_map/ppermute | solution.py:392
  16.5 1.4 %collective-permute-done.7.b_ref.refs_1_ = bf16[1,16,512]{2,1,0:T(8,128)(2,1)S(1)} collective-permute-done((bf16[1,16,512]{2,1,0:T(8,128)(2,1)S(1)}, bf16[1,16,512]{2,1,0:T(8,128)(2,1)S(1)}, u32[]{:S(2)}, u32[]{:S(2)}) %collective-permute-start.7) | collective-permute-done | bytes 16416 | tf_op jit(solution)/shard_map/ppermute | solution.py:385
  17.9 0.5 %collective-permute-start.9 = (bf16[2,16,512]{2,1,0:T(8,128)(2,1)S(1)}, bf16[2,16,512]{2,1,0:T(8,128)(2,1)S(1)}, u32[]{:S(2)}, u32[]{:S(2)}) collective-permute-start(bf16[2,16,512]{2,1,0:T(8,128)(2,1)S(1)} %join.4.refs_0_), channel_id=1, source_target_pairs={{0,12},{4,8},{8,4},{12,0},{16,28},{20,24},{24,20},{28,16},{1,13},{... | collective-permute-start | bytes 98312 | tf_op jit(solution)/shard_map/ppermute | solution.py:385
  18.4 0.6 %collective-permute-done.6.b_ref = bf16[16,512]{1,0:T(8,128)(2,1)S(1)} collective-permute-done((bf16[16,512]{1,0:T(8,128)(2,1)S(1)}, bf16[16,512]{1,0:T(8,128)(2,1)S(1)}, u32[]{:S(2)}, u32[]{:S(2)}) %collective-permute-start.6) | collective-permute-done | bytes 16416 | tf_op jit(solution)/shard_map/ppermute | solution.py:392
  19.0 1.8 %collective-permute-start.8 = (bf16[32,512]{1,0:T(8,128)(2,1)S(1)}, bf16[32,512]{1,0:T(8,128)(2,1)S(1)}, u32[]{:S(2)}, u32[]{:S(2)}) collective-permute-start(bf16[32,512]{1,0:T(8,128)(2,1)S(1)} %join.5.near_ref), channel_id=1, source_target_pairs={{0,2},{1,3},{2,0},{3,1},{4,5},{5,4},{6,7},{7,6},{8,10},{9,11},{10,... | collective-permute-start | bytes 98312 | tf_op jit(solution)/shard_map/ppermute | solution.py:392
  20.8 0.5 %collective-permute-done.9.refs_2_ = bf16[2,16,512]{2,1,0:T(8,128)(2,1)S(1)} collective-permute-done((bf16[2,16,512]{2,1,0:T(8,128)(2,1)S(1)}, bf16[2,16,512]{2,1,0:T(8,128)(2,1)S(1)}, u32[]{:S(2)}, u32[]{:S(2)}) %collective-permute-start.9) | collective-permute-done | bytes 32800 | tf_op jit(solution)/shard_map/ppermute | solution.py:385
  21.3 0.3 %collective-permute-start.12 = (bf16[2,16,512]{2,1,0:T(8,128)(2,1)S(1)}, bf16[2,16,512]{2,1,0:T(8,128)(2,1)S(1)}, u32[]{:S(2)}, u32[]{:S(2)}) collective-permute-start(bf16[2,16,512]{2,1,0:T(8,128)(2,1)S(1)} %collective-permute-done.9.refs_2_), channel_id=1, source_target_pairs={{0,4},{4,0},{8,12},{12,8},{16,20},{20,16},{24,28},{28,24},{1,5},{5... | collective-permute-start | bytes 98312 | tf_op jit(solution)/shard_map/ppermute | solution.py:381
  21.6 0.2 collective-permute-start.10
  21.8 0.3 %collective-permute-start.11 = (bf16[1,16,512]{2,1,0:T(8,128)(2,1)S(1)}, bf16[1,16,512]{2,1,0:T(8,128)(2,1)S(1)}, u32[]{:S(2)}, u32[]{:S(2)}) collective-permute-start(bf16[1,16,512]{2,1,0:T(8,128)(2,1)S(1)} %collective-permute-done.7.b_ref.refs_1_), channel_id=1, source_target_pairs={{0,4},{4,0},{8,12},{12,8},{16,20},{20,16},{24,28},{28,24},{1,5},{5... | collective-permute-start | bytes 49160 | tf_op jit(solution)/shard_map/ppermute | solution.py:381
  22.3 0.5 %collective-permute-done.10.refs_3_ = bf16[1,16,512]{2,1,0:T(8,128)(2,1)S(1)} collective-permute-done((bf16[1,16,512]{2,1,0:T(8,128)(2,1)S(1)}, bf16[1,16,512]{2,1,0:T(8,128)(2,1)S(1)}, u32[]{:S(2)}, u32[]{:S(2)}) %collective-permute-start.10) | collective-permute-done | bytes 16416 | tf_op jit(solution)/shard_map/ppermute | solution.py:381
  22.8 0.2 collective-permute-done.11.refs_4_
  23.0 1.1 %outputs.1 = (bf16[1,1,16,512]{3,2,1,0:T(8,128)(2,1)}, f32[1,128,512]{2,1,0:T(8,128)}, f32[1,128,512]{2,1,0:T(8,128)}) custom-call(bf16[32,512]{1,0:T(8,128)(2,1)S(1)} %join.5.near_ref, bf16[32,512]{1,0:T(8,128)(2,1)S(1)} %collective-permute-done.8.far_ref, bf16[16,64]{1,0:T(8,128)(2,1)S(1)} %get-tuple-element.33.table_ref, ...), custom_call_target="tpu_custom_call" | custom-call | tf_op jit(solution)/shard_map/outputs/pallas_call | solution.py:369
  (13 shorter events, 0.2 us)
Async XLA Ops:
  2.2 3.1 %collective-permute-start = (f32[4,16,512]{2,1,0:T(8,128)S(1)}, f32[4,16,512]{2,1,0:T(8,128)S(1)}, u32[]{:S(2)}, u32[]{:S(2)}) collective-permute-start(f32[4,16,512]{2,1,0:T(8,128)S(1)} %get-tuple-element.21), channel_id=1, source_target_pairs={{0,4},{4,0},{8,12},{12,8},{16,20},{20,16},{24,28},{28,24},{1,5},{5... | collective-permute-start | bytes 393224 | tf_op jit(solution)/shard_map/ppermute | solution.py:381
  2.7 6.5 %collective-permute-start.4 = (bf16[16,640]{1,0:T(8,128)(2,1)S(1)}, bf16[16,640]{1,0:T(8,128)(2,1)S(1)}, u32[]{:S(2)}, u32[]{:S(2)}) collective-permute-start(bf16[16,640]{1,0:T(8,128)(2,1)S(1)} %get-tuple-element.26.a_ref), channel_id=1, source_target_pairs={{0,1},{1,0},{2,3},{3,2},{4,6},{5,7},{6,4},{7,5},{8,9},{9,8},{10,11... | collective-permute-start | bytes 61448 | tf_op jit(solution)/shard_map/ppermute | solution.py:392
  5.3 7.1 %collective-permute-start.1 = (f32[16,512]{1,0:T(8,128)S(1)}, f32[16,512]{1,0:T(8,128)S(1)}, u32[]{:S(2)}, u32[]{:S(2)}) collective-permute-start(f32[16,512]{1,0:T(8,128)S(1)} %get-tuple-element.23), channel_id=1, source_target_pairs={{0,20},{4,16},{8,28},{12,24},{16,4},{20,0},{24,12},{28,8},{1,21},{... | collective-permute-start | bytes 98312 | tf_op jit(solution)/shard_map/ppermute | solution.py:385
  7.7 5.3 %collective-permute-start.2 = (f32[16,512]{1,0:T(8,128)S(1)}, f32[16,512]{1,0:T(8,128)S(1)}, u32[]{:S(2)}, u32[]{:S(2)}) collective-permute-start(f32[16,512]{1,0:T(8,128)S(1)} %get-tuple-element.24), channel_id=1, source_target_pairs={{0,28},{4,24},{8,20},{12,16},{16,12},{20,8},{24,4},{28,0},{1,29},{... | collective-permute-start | bytes 98312 | tf_op jit(solution)/shard_map/ppermute | solution.py:385
  9.0 4.0 %collective-permute-start.3 = (f32[16,512]{1,0:T(8,128)S(1)}, f32[16,512]{1,0:T(8,128)S(1)}, u32[]{:S(2)}, u32[]{:S(2)}) collective-permute-start(f32[16,512]{1,0:T(8,128)S(1)} %get-tuple-element.25), channel_id=1, source_target_pairs={{0,12},{4,8},{8,4},{12,0},{16,28},{20,24},{24,20},{28,16},{1,13},{... | collective-permute-start | bytes 98312 | tf_op jit(solution)/shard_map/ppermute | solution.py:385
  9.3 4.1 %collective-permute-start.5 = (bf16[32,640]{1,0:T(8,128)(2,1)S(1)}, bf16[32,640]{1,0:T(8,128)(2,1)S(1)}, u32[]{:S(2)}, u32[]{:S(2)}) collective-permute-start(bf16[32,640]{1,0:T(8,128)(2,1)S(1)} %join.3.near_ref), channel_id=1, source_target_pairs={{0,2},{1,3},{2,0},{3,1},{4,5},{5,4},{6,7},{7,6},{8,10},{9,11},{10,... | collective-permute-start | bytes 122888 | tf_op jit(solution)/shard_map/ppermute | solution.py:392
  13.8 4.1 %collective-permute-start.7 = (bf16[1,16,512]{2,1,0:T(8,128)(2,1)S(1)}, bf16[1,16,512]{2,1,0:T(8,128)(2,1)S(1)}, u32[]{:S(2)}, u32[]{:S(2)}) collective-permute-start(bf16[1,16,512]{2,1,0:T(8,128)(2,1)S(1)} %get-tuple-element.32.a_ref.refs_0_), channel_id=1, source_target_pairs={{0,20},{4,16},{8,28},{12,24},{16,4},{20,0},{24,12},{28,8},{1,21},{... | collective-permute-start | bytes 49160 | tf_op jit(solution)/shard_map/ppermute | solution.py:385
  15.2 3.7 %collective-permute-start.6 = (bf16[16,512]{1,0:T(8,128)(2,1)S(1)}, bf16[16,512]{1,0:T(8,128)(2,1)S(1)}, u32[]{:S(2)}, u32[]{:S(2)}) collective-permute-start(bf16[16,512]{1,0:T(8,128)(2,1)S(1)} %get-tuple-element.31.a_ref.hidden_ref), channel_id=1, source_target_pairs={{0,1},{1,0},{2,3},{3,2},{4,6},{5,7},{6,4},{7,5},{8,9},{9,8},{10,11... | collective-permute-start | bytes 49160 | tf_op jit(solution)/shard_map/ppermute | solution.py:392
  17.9 3.3 %collective-permute-start.9 = (bf16[2,16,512]{2,1,0:T(8,128)(2,1)S(1)}, bf16[2,16,512]{2,1,0:T(8,128)(2,1)S(1)}, u32[]{:S(2)}, u32[]{:S(2)}) collective-permute-start(bf16[2,16,512]{2,1,0:T(8,128)(2,1)S(1)} %join.4.refs_0_), channel_id=1, source_target_pairs={{0,12},{4,8},{8,4},{12,0},{16,28},{20,24},{24,20},{28,16},{1,13},{... | collective-permute-start | bytes 98312 | tf_op jit(solution)/shard_map/ppermute | solution.py:385
  19.0 4.0 %collective-permute-start.8 = (bf16[32,512]{1,0:T(8,128)(2,1)S(1)}, bf16[32,512]{1,0:T(8,128)(2,1)S(1)}, u32[]{:S(2)}, u32[]{:S(2)}) collective-permute-start(bf16[32,512]{1,0:T(8,128)(2,1)S(1)} %join.5.near_ref), channel_id=1, source_target_pairs={{0,2},{1,3},{2,0},{3,1},{4,5},{5,4},{6,7},{7,6},{8,10},{9,11},{10,... | collective-permute-start | bytes 98312 | tf_op jit(solution)/shard_map/ppermute | solution.py:392
  21.3 1.7 %collective-permute-start.12 = (bf16[2,16,512]{2,1,0:T(8,128)(2,1)S(1)}, bf16[2,16,512]{2,1,0:T(8,128)(2,1)S(1)}, u32[]{:S(2)}, u32[]{:S(2)}) collective-permute-start(bf16[2,16,512]{2,1,0:T(8,128)(2,1)S(1)} %collective-permute-done.9.refs_2_), channel_id=1, source_target_pairs={{0,4},{4,0},{8,12},{12,8},{16,20},{20,16},{24,28},{28,24},{1,5},{5... | collective-permute-start | bytes 98312 | tf_op jit(solution)/shard_map/ppermute | solution.py:381
  21.6 1.2 %collective-permute-start.10 = (bf16[1,16,512]{2,1,0:T(8,128)(2,1)S(1)}, bf16[1,16,512]{2,1,0:T(8,128)(2,1)S(1)}, u32[]{:S(2)}, u32[]{:S(2)}) collective-permute-start(bf16[1,16,512]{2,1,0:T(8,128)(2,1)S(1)} %get-tuple-element.32.a_ref.refs_0_), channel_id=1, source_target_pairs={{0,4},{4,0},{8,12},{12,8},{16,20},{20,16},{24,28},{28,24},{1,5},{5... | collective-permute-start | bytes 49160 | tf_op jit(solution)/shard_map/ppermute | solution.py:381
  21.8 1.2 %collective-permute-start.11 = (bf16[1,16,512]{2,1,0:T(8,128)(2,1)S(1)}, bf16[1,16,512]{2,1,0:T(8,128)(2,1)S(1)}, u32[]{:S(2)}, u32[]{:S(2)}) collective-permute-start(bf16[1,16,512]{2,1,0:T(8,128)(2,1)S(1)} %collective-permute-done.7.b_ref.refs_1_), channel_id=1, source_target_pairs={{0,4},{4,0},{8,12},{12,8},{16,20},{20,16},{24,28},{28,24},{1,5},{5... | collective-permute-start | bytes 49160 | tf_op jit(solution)/shard_map/ppermute | solution.py:381

commit v4 on v3

--- a/solution.py
+++ b/solution.py
@@ -11,6 +11,7 @@
 HIDDEN_COST = 3 * 10**8
 PREACT_COST = 4 * 10**8
 OWN_COST = 10**8
+MEAN_COST = 10**8
 BACKWARD_COST = 0
 INDEX_COST = 10**9
 F32 = jnp.float32
@@ -329,7 +330,19 @@
     return call(own_part_kernel, "own_part", (hidden, w2s), [out], OWN_COST)[0]
 
 
-def outputs_kernel(codes, near_ref, far_ref, table_ref, degree_ref, own_ref, w2n_ref, *refs):
+def neigh_sum_kernel(near_ref, far_ref, table_ref, degree_ref, out_ref):
+    rows, count = table_ref.shape[0], near_ref.shape[0]
+    neigh_sum = jnp.dot(table_ref[:, :count], near_ref[...], preferred_element_type=F32)
+    neigh_sum = neigh_sum + jnp.dot(table_ref[:, count:], far_ref[...], preferred_element_type=F32)
+    out_ref[...] = ((near_ref[0:rows, :].astype(F32) + neigh_sum) / (1.0 + degree_ref[:, 0:1])).astype(BF16)
+
+
+def mean_two(near, far, table, degree):
+    out = ((table.shape[0], near.shape[1]), BF16)
+    return call(neigh_sum_kernel, "mean_two", (near, far, table, degree), [out], MEAN_COST)[0]
+
+
+def outputs_kernel(codes, mean_two_ref, own_ref, w2n_ref, *refs):
     grad_refs, (both_ref, out_hbm, self_hbm, neigh_hbm) = refs[:-9], refs[-9:-5]
     out_ref, self_ref, neigh_ref, grad_scratch, sems = refs[-5:]
     depth = both_ref.shape[0] // 2
@@ -339,7 +352,7 @@
     pairs = [(ref.at[0, pl.ds(at, half)], hbm.at[0, pl.ds(at, half)]) for ref, hbm, _, at in pieces]
     pairs.append((out_ref, out_hbm))
     copies = [pltpu.make_async_copy(src, dst, sems.at[n]) for n, (src, dst) in enumerate(pairs)]
-    rows = table_ref.shape[0]
+    rows = mean_two_ref.shape[0]
     me = lax.axis_index("feat")
     for ref, code_list in zip(grad_refs, codes):
         for n, code in enumerate(code_list):
@@ -351,30 +364,26 @@
         ref[0, at : at + half] = jnp.dot(columns, grad_pre, preferred_element_type=F32)
         copy.start()
 
-    count = near_ref.shape[0]
-    neigh_sum = jnp.dot(table_ref[:, :count], near_ref[...], preferred_element_type=F32)
-    neigh_sum = neigh_sum + jnp.dot(table_ref[:, count:], far_ref[...], preferred_element_type=F32)
-    mean_two = ((near_ref[0:rows, :].astype(F32) + neigh_sum) / (1.0 + degree_ref[:, 0:1])).astype(BF16)
-    out = own_ref[...] + jnp.dot(mean_two, w2n_ref[...], preferred_element_type=F32)
+    out = own_ref[...] + jnp.dot(mean_two_ref[...], w2n_ref[...], preferred_element_type=F32)
     out_ref[0, 0] = out.astype(BF16)
     copies[-1].start()
     for copy in copies:
         copy.wait()
 
 
-def outputs(near, far, table, degree, own, w2n, grads, codes, both):
+def outputs(mean, own, w2n, grads, codes, both):
     group, width = both.shape[1], grads[0].shape[2]
     grad = jax.ShapeDtypeStruct((1, both.shape[0] // 2, width), F32)
     out = jax.ShapeDtypeStruct((1, 1) + own.shape, BF16)
     return pl.pallas_call(
         functools.partial(outputs_kernel, codes),
-        in_specs=[VMEM] * (len(grads) + 7),
+        in_specs=[VMEM] * (len(grads) + 4),
         out_specs=[pl.BlockSpec(memory_space=pltpu.HBM)] * 3,
         out_shape=[out, grad, grad],
         scratch_shapes=[pltpu.VMEM(a.shape, a.dtype) for a in (out, grad, grad)]
         + [pltpu.VMEM((group, width), BF16), pltpu.SemaphoreType.DMA((5,))],
         name="outputs", compiler_params=PARAMS,
-    )(near, far, table, degree, own, w2n, *grads, both)
+    )(mean, own, w2n, *grads, both)
 
 
 def swap_cores(x):
@@ -413,18 +422,16 @@
         aux_near, aux_far, w2_self, w2_neigh, peers, slots, rows_dev
     )
     hidden, grads = hidden_and_grads(preact_sum(parts[:1] + far), grad)
-    pieces, codes, bits = [grads], [[0]], chips // 2
-    while bits:
-        pieces.append(swap_chips(grads, bits))
-        codes.append([code ^ (2 * bits + 1) for known in codes for code in known])
-        bits //= 2
-        if bits:
-            grads = join(grads, pieces[-1])
+    codes, bits = [0], chips // 2
+    while bits > 1:
+        grads = join(grads, swap_chips(grads, bits))
+        codes, bits = codes + [code ^ (2 * bits + 1) for code in codes], bits // 2
     near, far = gather_peers(hidden, HIDDEN_COST, (grads,))
-    pieces = pieces + [swap_cores(x) for x in pieces]
-    codes = codes + [[code ^ 1 for code in known] for known in codes]
-    own = own_part(hidden, w2_self)
-    return outputs(near, far, table, degree, own, w2_neigh, pieces, codes, both)
+    grads = [grads, swap_chips(grads, 1)]
+    grads = grads + [swap_cores(x) for x in grads]
+    codes = [[code ^ flip for code in codes] for flip in (0, 3, 1, 2)]
+    mean = mean_two(near, far, table, degree)
+    return outputs(mean, own_part(hidden, w2_self), w2_neigh, grads, codes, both)
 
 
 def solution(mesh):

time: 24.3 us -> 24.4 us (level)
  starting transfers between devices: 14.4 us -> 14 us
  waiting for transfers between devices: 4.04 us -> 4.39 us
    ppermute x4, waiting for transfers between devices: 0.89 us -> 2.01 us  [swap_peers(): return lax.ppermute(x, ('feat', 'dp'), pairs)]
    ppermute x4 -> x3, waiting for transfers between devices: 0.68 us -> 0.01 us  [swap_cores(): lax.ppermute(x, 'feat', [(i, i ^ 1) for i in range(lax.axis_size('feat'))])]
    ppermute x4 -> x3, starting transfers between devices: 1.36 us -> 0.95 us  [swap_cores(): lax.ppermute(x, 'feat', [(i, i ^ 1) for i in range(lax.axis_size('feat'))])]
  transfers between devices with their start and end apart: 13 -> 12, of which waited for: 7 -> 6; matrix products, arithmetic and copies ran while one was open for 0% -> 0% of each run, Pallas kernels for 7% -> 8%
where the time goes in v4:
time: 24.4 us; the launch traced here: 24.1 us
  starting transfers between devices  14 us (57%)
  Pallas kernels  4.98 us (20%)
  waiting for transfers between devices  4.39 us (18%)
  between operations  0.69 us (3%)
    ppermute x4, starting transfers between devices, swap_peers(): return lax.ppermute(x, ('feat', 'dp'), pairs)  7.22 us
    ppermute x5, starting transfers between devices, swap_chips(): lax.ppermute(x, 'feat', [(i, i ^ 2 * bits + 1) for i in range(lax.axis_si...  5.86 us
    ppermute x5, waiting for transfers between devices, swap_chips(): lax.ppermute(x, 'feat', [(i, i ^ 2 * bits + 1) for i in range(lax.axis_si...  2.37 us
    ppermute x4, waiting for transfers between devices, swap_peers(): return lax.ppermute(x, ('feat', 'dp'), pairs)  2.01 us
    pallas_call x1, Pallas kernels, backward_near(): pl.pallas_call(near_kernel, in_specs=[VMEM, hbm, hbm], out_specs=[VMEM] *...  1.57 us
    pallas_call x1, Pallas kernels, first_layer(): pl.pallas_call(functools.partial(first_layer_kernel, group // tile), grid...  1.56 us
    pallas_call x1, Pallas kernels, outputs(): pl.pallas_call(functools.partial(outputs_kernel, codes), in_specs=[VMEM]...  1.02 us
    ppermute x3, starting transfers between devices, swap_cores(): lax.ppermute(x, 'feat', [(i, i ^ 1) for i in range(lax.axis_size('feat'))])  0.95 us
  transfers between devices with their start and end apart: 12, of which 6 were waited for; matrix products, arithmetic and copies ran while one was open for 0% of the time, Pallas kernels for 8%

profile of v4, /device:TPU:0, one launch (start us, length us, event | category | flops | bytes accessed | tf_op | source)
XLA Modules:
  0.0 24.1 jit_solution(5798196182277528813)
XLA Ops:
  0.6 1.6 %first_layer.1 = (f32[4,16,512]{2,1,0:T(8,128)S(1)}, f32[4,16,512]{2,1,0:T(8,128)S(1)}, bf16[256,128]{1,0:T(8,128)(2,1)S(1)}, bf16[16,640]{1,0:T(8,128)(2,1)S(1)}) custom-call(bf16[1,128,256]{2,1,0:T(8,128)(2,1)} %feat_hbm.1, s32[10,1,128]{2,1,0:T(1,128)} %bitcast.1, bf16[128,512]{1,0:T(8,128)(2,1)} %w1s_hbm.1, bf16[128,512]{1,0:T(8,128)(2,1)} %w1n_hbm.1, ...), custom_call_target="tpu_custom_call" | custom-call | tf_op jit(solution)/shard_map/first_layer/pallas_call | solution.py:135
  2.2 0.5 %collective-permute-start = (f32[4,16,512]{2,1,0:T(8,128)S(1)}, f32[4,16,512]{2,1,0:T(8,128)S(1)}, u32[]{:S(2)}, u32[]{:S(2)}) collective-permute-start(f32[4,16,512]{2,1,0:T(8,128)S(1)} %get-tuple-element.21), channel_id=1, source_target_pairs={{0,4},{4,0},{8,12},{12,8},{16,20},{20,16},{24,28},{28,24},{1,5},{5... | collective-permute-start | bytes 393224 | tf_op jit(solution)/shard_map/ppermute | solution.py:390
  2.7 2.6 %collective-permute-start.4 = (bf16[16,640]{1,0:T(8,128)(2,1)S(1)}, bf16[16,640]{1,0:T(8,128)(2,1)S(1)}, u32[]{:S(2)}, u32[]{:S(2)}) collective-permute-start(bf16[16,640]{1,0:T(8,128)(2,1)S(1)} %get-tuple-element.26.a_ref), channel_id=1, source_target_pairs={{0,1},{1,0},{2,3},{3,2},{4,6},{5,7},{6,4},{7,5},{8,9},{9,8},{10,11... | collective-permute-start | bytes 61448 | tf_op jit(solution)/shard_map/ppermute | solution.py:401
  5.3 2.4 %collective-permute-start.1 = (f32[16,512]{1,0:T(8,128)S(1)}, f32[16,512]{1,0:T(8,128)S(1)}, u32[]{:S(2)}, u32[]{:S(2)}) collective-permute-start(f32[16,512]{1,0:T(8,128)S(1)} %get-tuple-element.23), channel_id=1, source_target_pairs={{0,20},{4,16},{8,28},{12,24},{16,4},{20,0},{24,12},{28,8},{1,21},{... | collective-permute-start | bytes 98312 | tf_op jit(solution)/shard_map/ppermute | solution.py:394
  7.7 1.3 %collective-permute-start.2 = (f32[16,512]{1,0:T(8,128)S(1)}, f32[16,512]{1,0:T(8,128)S(1)}, u32[]{:S(2)}, u32[]{:S(2)}) collective-permute-start(f32[16,512]{1,0:T(8,128)S(1)} %get-tuple-element.24), channel_id=1, source_target_pairs={{0,28},{4,24},{8,20},{12,16},{16,12},{20,8},{24,4},{28,0},{1,29},{... | collective-permute-start | bytes 98312 | tf_op jit(solution)/shard_map/ppermute | solution.py:394
  9.0 0.2 collective-permute-start.3
  9.3 1.6 %collective-permute-start.5 = (bf16[32,640]{1,0:T(8,128)(2,1)S(1)}, bf16[32,640]{1,0:T(8,128)(2,1)S(1)}, u32[]{:S(2)}, u32[]{:S(2)}) collective-permute-start(bf16[32,640]{1,0:T(8,128)(2,1)S(1)} %join.3.near_ref), channel_id=1, source_target_pairs={{0,2},{1,3},{2,0},{3,1},{4,5},{5,4},{6,7},{7,6},{8,10},{9,11},{10,... | collective-permute-start | bytes 122888 | tf_op jit(solution)/shard_map/ppermute | solution.py:401
  10.8 1.6 %backward_near.1 = (f32[16,512]{1,0:T(8,128)S(1)}, f32[32,512]{1,0:T(8,128)S(1)}, bf16[512,512]{1,0:T(8,128)(2,1)S(1)}, bf16[512,512]{1,0:T(8,128)(2,1)S(1)}) custom-call(bf16[32,640]{1,0:T(8,128)(2,1)S(1)} %join.3.near_ref, bf16[512,512]{1,0:T(8,128)(2,1)} %w2s_hbm.1, bf16[512,512]{1,0:T(8,128)(2,1)} %w2n_hbm.1), custom_call_target="tpu_custom_call" | custom-call | tf_op jit(solution)/shard_map/backward_near/pallas_call | solution.py:225
  12.4 0.6 %collective-permute-done.2.refs_2_ = f32[16,512]{1,0:T(8,128)S(1)} collective-permute-done((f32[16,512]{1,0:T(8,128)S(1)}, f32[16,512]{1,0:T(8,128)S(1)}, u32[]{:S(2)}, u32[]{:S(2)}) %collective-permute-start.2) | collective-permute-done | bytes 32800 | tf_op jit(solution)/shard_map/ppermute | solution.py:394
  13.0 0.3 %collective-permute-done.5.far_ref = bf16[32,640]{1,0:T(8,128)(2,1)S(1)} collective-permute-done((bf16[32,640]{1,0:T(8,128)(2,1)S(1)}, bf16[32,640]{1,0:T(8,128)(2,1)S(1)}, u32[]{:S(2)}, u32[]{:S(2)}) %collective-permute-start.5) | collective-permute-done | bytes 40992 | tf_op jit(solution)/shard_map/ppermute | solution.py:401
  13.3 0.4 %second_backward.1 = (bf16[16,512]{1,0:T(8,128)(2,1)S(1)}, bf16[16,64]{1,0:T(8,128)(2,1)S(1)}, f32[16,128]{1,0:T(8,128)S(1)}) custom-call(bf16[32,640]{1,0:T(8,128)(2,1)S(1)} %join.3.near_ref, bf16[32,640]{1,0:T(8,128)(2,1)S(1)} %collective-permute-done.5.far_ref, f32[16,512]{1,0:T(8,128)S(1)} %get-tuple-element.27.self_ref, ...), custom_call_target="tpu_custom_call" | custom-call | tf_op jit(solution)/shard_map/second_backward/pallas_call | solution.py:299
  13.8 1.4 %collective-permute-start.7 = (bf16[1,16,512]{2,1,0:T(8,128)(2,1)S(1)}, bf16[1,16,512]{2,1,0:T(8,128)(2,1)S(1)}, u32[]{:S(2)}, u32[]{:S(2)}) collective-permute-start(bf16[1,16,512]{2,1,0:T(8,128)(2,1)S(1)} %get-tuple-element.32.a_ref), channel_id=1, source_target_pairs={{0,20},{4,16},{8,28},{12,24},{16,4},{20,0},{24,12},{28,8},{1,21},{... | collective-permute-start | bytes 49160 | tf_op jit(solution)/shard_map/ppermute | solution.py:394
  15.2 1.3 %collective-permute-start.6 = (bf16[16,512]{1,0:T(8,128)(2,1)S(1)}, bf16[16,512]{1,0:T(8,128)(2,1)S(1)}, u32[]{:S(2)}, u32[]{:S(2)}) collective-permute-start(bf16[16,512]{1,0:T(8,128)(2,1)S(1)} %get-tuple-element.31.a_ref.hidden_ref), channel_id=1, source_target_pairs={{0,1},{1,0},{2,3},{3,2},{4,6},{5,7},{6,4},{7,5},{8,9},{9,8},{10,11... | collective-permute-start | bytes 49160 | tf_op jit(solution)/shard_map/ppermute | solution.py:401
  16.5 1.4 %collective-permute-done.7.b_ref = bf16[1,16,512]{2,1,0:T(8,128)(2,1)S(1)} collective-permute-done((bf16[1,16,512]{2,1,0:T(8,128)(2,1)S(1)}, bf16[1,16,512]{2,1,0:T(8,128)(2,1)S(1)}, u32[]{:S(2)}, u32[]{:S(2)}) %collective-permute-start.7) | collective-permute-done | bytes 16416 | tf_op jit(solution)/shard_map/ppermute | solution.py:394
  17.9 0.5 %collective-permute-start.9 = (bf16[2,16,512]{2,1,0:T(8,128)(2,1)S(1)}, bf16[2,16,512]{2,1,0:T(8,128)(2,1)S(1)}, u32[]{:S(2)}, u32[]{:S(2)}) collective-permute-start(bf16[2,16,512]{2,1,0:T(8,128)(2,1)S(1)} %join.4.refs_0_), channel_id=1, source_target_pairs={{0,12},{4,8},{8,4},{12,0},{16,28},{20,24},{24,20},{28,16},{1,13},{... | collective-permute-start | bytes 98312 | tf_op jit(solution)/shard_map/ppermute | solution.py:394
  18.4 0.6 %collective-permute-done.6.b_ref = bf16[16,512]{1,0:T(8,128)(2,1)S(1)} collective-permute-done((bf16[16,512]{1,0:T(8,128)(2,1)S(1)}, bf16[16,512]{1,0:T(8,128)(2,1)S(1)}, u32[]{:S(2)}, u32[]{:S(2)}) %collective-permute-start.6) | collective-permute-done | bytes 16416 | tf_op jit(solution)/shard_map/ppermute | solution.py:401
  19.0 1.8 %collective-permute-start.8 = (bf16[32,512]{1,0:T(8,128)(2,1)S(1)}, bf16[32,512]{1,0:T(8,128)(2,1)S(1)}, u32[]{:S(2)}, u32[]{:S(2)}) collective-permute-start(bf16[32,512]{1,0:T(8,128)(2,1)S(1)} %join.5.near_ref), channel_id=1, source_target_pairs={{0,2},{1,3},{2,0},{3,1},{4,5},{5,4},{6,7},{7,6},{8,10},{9,11},{10,... | collective-permute-start | bytes 98312 | tf_op jit(solution)/shard_map/ppermute | solution.py:401
  20.8 0.1 collective-permute-start.10
  20.9 0.4 %collective-permute-done.9.refs_1_ = bf16[2,16,512]{2,1,0:T(8,128)(2,1)S(1)} collective-permute-done((bf16[2,16,512]{2,1,0:T(8,128)(2,1)S(1)}, bf16[2,16,512]{2,1,0:T(8,128)(2,1)S(1)}, u32[]{:S(2)}, u32[]{:S(2)}) %collective-permute-start.9) | collective-permute-done | bytes 32800 | tf_op jit(solution)/shard_map/ppermute | solution.py:394
  21.3 0.3 %collective-permute-start.11 = (bf16[2,16,512]{2,1,0:T(8,128)(2,1)S(1)}, bf16[2,16,512]{2,1,0:T(8,128)(2,1)S(1)}, u32[]{:S(2)}, u32[]{:S(2)}) collective-permute-start(bf16[2,16,512]{2,1,0:T(8,128)(2,1)S(1)} %collective-permute-done.9.refs_1_), channel_id=1, source_target_pairs={{0,4},{4,0},{8,12},{12,8},{16,20},{20,16},{24,28},{28,24},{1,5},{5... | collective-permute-start | bytes 98312 | tf_op jit(solution)/shard_map/ppermute | solution.py:390
  21.6 0.2 own_part.1.own_ref
  21.8 1.1 %collective-permute-done.8.far_ref = bf16[32,512]{1,0:T(8,128)(2,1)S(1)} collective-permute-done((bf16[32,512]{1,0:T(8,128)(2,1)S(1)}, bf16[32,512]{1,0:T(8,128)(2,1)S(1)}, u32[]{:S(2)}, u32[]{:S(2)}) %collective-permute-start.8) | collective-permute-done | bytes 32800 | tf_op jit(solution)/shard_map/ppermute | solution.py:401
  22.9 0.2 mean_two.1.mean_two_ref
  23.1 1.0 %outputs.1 = (bf16[1,1,16,512]{3,2,1,0:T(8,128)(2,1)}, f32[1,128,512]{2,1,0:T(8,128)}, f32[1,128,512]{2,1,0:T(8,128)}) custom-call(bf16[16,512]{1,0:T(8,128)(2,1)S(1)} %mean_two.1.mean_two_ref, f32[16,512]{1,0:T(8,128)S(1)} %own_part.1.own_ref, bf16[512,512]{1,0:T(8,128)(2,1)S(1)} %get-tuple-element.29.w2n_ref, bf16[2,16,512]{2,1,0:T(8,128)(2,1)S(1)} %join.4.refs_0_, ...), custom_call_target="tpu_custom_call" | custom-call | tf_op jit(solution)/shard_map/outputs/pallas_call | solution.py:378
  (12 shorter events, 0.1 us)
Async XLA Ops:
  2.2 3.1 %collective-permute-start = (f32[4,16,512]{2,1,0:T(8,128)S(1)}, f32[4,16,512]{2,1,0:T(8,128)S(1)}, u32[]{:S(2)}, u32[]{:S(2)}) collective-permute-start(f32[4,16,512]{2,1,0:T(8,128)S(1)} %get-tuple-element.21), channel_id=1, source_target_pairs={{0,4},{4,0},{8,12},{12,8},{16,20},{20,16},{24,28},{28,24},{1,5},{5... | collective-permute-start | bytes 393224 | tf_op jit(solution)/shard_map/ppermute | solution.py:390
  2.7 6.5 %collective-permute-start.4 = (bf16[16,640]{1,0:T(8,128)(2,1)S(1)}, bf16[16,640]{1,0:T(8,128)(2,1)S(1)}, u32[]{:S(2)}, u32[]{:S(2)}) collective-permute-start(bf16[16,640]{1,0:T(8,128)(2,1)S(1)} %get-tuple-element.26.a_ref), channel_id=1, source_target_pairs={{0,1},{1,0},{2,3},{3,2},{4,6},{5,7},{6,4},{7,5},{8,9},{9,8},{10,11... | collective-permute-start | bytes 61448 | tf_op jit(solution)/shard_map/ppermute | solution.py:401
  5.3 7.1 %collective-permute-start.1 = (f32[16,512]{1,0:T(8,128)S(1)}, f32[16,512]{1,0:T(8,128)S(1)}, u32[]{:S(2)}, u32[]{:S(2)}) collective-permute-start(f32[16,512]{1,0:T(8,128)S(1)} %get-tuple-element.23), channel_id=1, source_target_pairs={{0,20},{4,16},{8,28},{12,24},{16,4},{20,0},{24,12},{28,8},{1,21},{... | collective-permute-start | bytes 98312 | tf_op jit(solution)/shard_map/ppermute | solution.py:394
  7.7 5.3 %collective-permute-start.2 = (f32[16,512]{1,0:T(8,128)S(1)}, f32[16,512]{1,0:T(8,128)S(1)}, u32[]{:S(2)}, u32[]{:S(2)}) collective-permute-start(f32[16,512]{1,0:T(8,128)S(1)} %get-tuple-element.24), channel_id=1, source_target_pairs={{0,28},{4,24},{8,20},{12,16},{16,12},{20,8},{24,4},{28,0},{1,29},{... | collective-permute-start | bytes 98312 | tf_op jit(solution)/shard_map/ppermute | solution.py:394
  9.0 4.0 %collective-permute-start.3 = (f32[16,512]{1,0:T(8,128)S(1)}, f32[16,512]{1,0:T(8,128)S(1)}, u32[]{:S(2)}, u32[]{:S(2)}) collective-permute-start(f32[16,512]{1,0:T(8,128)S(1)} %get-tuple-element.25), channel_id=1, source_target_pairs={{0,12},{4,8},{8,4},{12,0},{16,28},{20,24},{24,20},{28,16},{1,13},{... | collective-permute-start | bytes 98312 | tf_op jit(solution)/shard_map/ppermute | solution.py:394
  9.3 4.1 %collective-permute-start.5 = (bf16[32,640]{1,0:T(8,128)(2,1)S(1)}, bf16[32,640]{1,0:T(8,128)(2,1)S(1)}, u32[]{:S(2)}, u32[]{:S(2)}) collective-permute-start(bf16[32,640]{1,0:T(8,128)(2,1)S(1)} %join.3.near_ref), channel_id=1, source_target_pairs={{0,2},{1,3},{2,0},{3,1},{4,5},{5,4},{6,7},{7,6},{8,10},{9,11},{10,... | collective-permute-start | bytes 122888 | tf_op jit(solution)/shard_map/ppermute | solution.py:401
  13.8 4.1 %collective-permute-start.7 = (bf16[1,16,512]{2,1,0:T(8,128)(2,1)S(1)}, bf16[1,16,512]{2,1,0:T(8,128)(2,1)S(1)}, u32[]{:S(2)}, u32[]{:S(2)}) collective-permute-start(bf16[1,16,512]{2,1,0:T(8,128)(2,1)S(1)} %get-tuple-element.32.a_ref), channel_id=1, source_target_pairs={{0,20},{4,16},{8,28},{12,24},{16,4},{20,0},{24,12},{28,8},{1,21},{... | collective-permute-start | bytes 49160 | tf_op jit(solution)/shard_map/ppermute | solution.py:394
  15.2 3.7 %collective-permute-start.6 = (bf16[16,512]{1,0:T(8,128)(2,1)S(1)}, bf16[16,512]{1,0:T(8,128)(2,1)S(1)}, u32[]{:S(2)}, u32[]{:S(2)}) collective-permute-start(bf16[16,512]{1,0:T(8,128)(2,1)S(1)} %get-tuple-element.31.a_ref.hidden_ref), channel_id=1, source_target_pairs={{0,1},{1,0},{2,3},{3,2},{4,6},{5,7},{6,4},{7,5},{8,9},{9,8},{10,11... | collective-permute-start | bytes 49160 | tf_op jit(solution)/shard_map/ppermute | solution.py:401
  17.9 3.3 %collective-permute-start.9 = (bf16[2,16,512]{2,1,0:T(8,128)(2,1)S(1)}, bf16[2,16,512]{2,1,0:T(8,128)(2,1)S(1)}, u32[]{:S(2)}, u32[]{:S(2)}) collective-permute-start(bf16[2,16,512]{2,1,0:T(8,128)(2,1)S(1)} %join.4.refs_0_), channel_id=1, source_target_pairs={{0,12},{4,8},{8,4},{12,0},{16,28},{20,24},{24,20},{28,16},{1,13},{... | collective-permute-start | bytes 98312 | tf_op jit(solution)/shard_map/ppermute | solution.py:394
  19.0 3.9 %collective-permute-start.8 = (bf16[32,512]{1,0:T(8,128)(2,1)S(1)}, bf16[32,512]{1,0:T(8,128)(2,1)S(1)}, u32[]{:S(2)}, u32[]{:S(2)}) collective-permute-start(bf16[32,512]{1,0:T(8,128)(2,1)S(1)} %join.5.near_ref), channel_id=1, source_target_pairs={{0,2},{1,3},{2,0},{3,1},{4,5},{5,4},{6,7},{7,6},{8,10},{9,11},{10,... | collective-permute-start | bytes 98312 | tf_op jit(solution)/shard_map/ppermute | solution.py:401
  20.8 2.3 %collective-permute-start.10 = (bf16[2,16,512]{2,1,0:T(8,128)(2,1)S(1)}, bf16[2,16,512]{2,1,0:T(8,128)(2,1)S(1)}, u32[]{:S(2)}, u32[]{:S(2)}) collective-permute-start(bf16[2,16,512]{2,1,0:T(8,128)(2,1)S(1)} %join.4.refs_0_), channel_id=1, source_target_pairs={{0,4},{4,0},{8,12},{12,8},{16,20},{20,16},{24,28},{28,24},{1,5},{5... | collective-permute-start | bytes 98312 | tf_op jit(solution)/shard_map/ppermute | solution.py:390
  21.3 1.8 %collective-permute-start.11 = (bf16[2,16,512]{2,1,0:T(8,128)(2,1)S(1)}, bf16[2,16,512]{2,1,0:T(8,128)(2,1)S(1)}, u32[]{:S(2)}, u32[]{:S(2)}) collective-permute-start(bf16[2,16,512]{2,1,0:T(8,128)(2,1)S(1)} %collective-permute-done.9.refs_1_), channel_id=1, source_target_pairs={{0,4},{4,0},{8,12},{12,8},{16,20},{20,16},{24,28},{28,24},{1,5},{5... | collective-permute-start | bytes 98312 | tf_op jit(solution)/shard_map/ppermute | solution.py:390

commit v5 on v3

--- a/solution.py
+++ b/solution.py
@@ -168,7 +168,7 @@
 
 
 def code_of(n, levels, core):
-    return jnp.where(core == 0, n, reverse(n, levels))
+    return jnp.where(core == 1, n, reverse(n, levels))
 
 
 def levels_of(count):
@@ -387,7 +387,7 @@
 
 def swap_peers(x, level):
     feats, peers = lax.axis_size("feat"), lax.axis_size("dp")
-    bits = 1 << level, 1 << (levels_of(peers) - 1 - level)
+    bits = 1 << (levels_of(peers) - 1 - level), 1 << level
     pairs = [(f * peers + d, f * peers + (d ^ bits[f % 2])) for f in range(feats) for d in range(peers)]
     return lax.ppermute(x, ("feat", "dp"), pairs)
 

time: 24.3 us -> 24.3 us (level)
  no operation moved by 1% of the time
where the time goes in v5:
time: 24.3 us; the launch traced here: 24 us
  starting transfers between devices  14.5 us (60%)
  Pallas kernels  4.83 us (20%)
  waiting for transfers between devices  4.06 us (17%)
  between operations  0.69 us (3%)
    ppermute x4, starting transfers between devices, swap_peers(): return lax.ppermute(x, ('feat', 'dp'), pairs)  7.22 us
    ppermute x5, starting transfers between devices, swap_chips(): lax.ppermute(x, 'feat', [(i, i ^ 2 * bits + 1) for i in range(lax.axis_si...  5.87 us
    ppermute x5, waiting for transfers between devices, swap_chips(): lax.ppermute(x, 'feat', [(i, i ^ 2 * bits + 1) for i in range(lax.axis_si...  2.47 us
    pallas_call x1, Pallas kernels, backward_near(): pl.pallas_call(near_kernel, in_specs=[VMEM, hbm, hbm], out_specs=[VMEM] *...  1.57 us
    pallas_call x1, Pallas kernels, first_layer(): pl.pallas_call(functools.partial(first_layer_kernel, group // tile), grid...  1.56 us
    ppermute x4, starting transfers between devices, swap_cores(): lax.ppermute(x, 'feat', [(i, i ^ 1) for i in range(lax.axis_size('feat'))])  1.37 us
    pallas_call x1, Pallas kernels, outputs(): pl.pallas_call(functools.partial(outputs_kernel, codes), in_specs=[VMEM]...  1.05 us
    ppermute x4, waiting for transfers between devices, swap_peers(): return lax.ppermute(x, ('feat', 'dp'), pairs)  0.91 us
  transfers between devices with their start and end apart: 13, of which 7 were waited for; matrix products, arithmetic and copies ran while one was open for 0% of the time, Pallas kernels for 7%

profile of v5, /device:TPU:0, one launch (start us, length us, event | category | flops | bytes accessed | tf_op | source)
XLA Modules:
  0.0 24.0 jit_solution(5951801813464630653)
XLA Ops:
  0.6 1.6 %first_layer.1 = (f32[4,16,512]{2,1,0:T(8,128)S(1)}, f32[4,16,512]{2,1,0:T(8,128)S(1)}, bf16[256,128]{1,0:T(8,128)(2,1)S(1)}, bf16[16,640]{1,0:T(8,128)(2,1)S(1)}) custom-call(bf16[1,128,256]{2,1,0:T(8,128)(2,1)} %feat_hbm.1, s32[10,1,128]{2,1,0:T(1,128)} %bitcast.1, bf16[128,512]{1,0:T(8,128)(2,1)} %w1s_hbm.1, bf16[128,512]{1,0:T(8,128)(2,1)} %w1n_hbm.1, ...), custom_call_target="tpu_custom_call" | custom-call | tf_op jit(solution)/shard_map/first_layer/pallas_call | solution.py:134
  2.2 0.5 %collective-permute-start = (f32[4,16,512]{2,1,0:T(8,128)S(1)}, f32[4,16,512]{2,1,0:T(8,128)S(1)}, u32[]{:S(2)}, u32[]{:S(2)}) collective-permute-start(f32[4,16,512]{2,1,0:T(8,128)S(1)} %get-tuple-element.21), channel_id=1, source_target_pairs={{0,4},{4,0},{8,12},{12,8},{16,20},{20,16},{24,28},{28,24},{1,5},{5... | collective-permute-start | bytes 393224 | tf_op jit(solution)/shard_map/ppermute | solution.py:381
  2.7 2.6 %collective-permute-start.4 = (bf16[16,640]{1,0:T(8,128)(2,1)S(1)}, bf16[16,640]{1,0:T(8,128)(2,1)S(1)}, u32[]{:S(2)}, u32[]{:S(2)}) collective-permute-start(bf16[16,640]{1,0:T(8,128)(2,1)S(1)} %get-tuple-element.26.a_ref), channel_id=1, source_target_pairs={{0,2},{1,3},{2,0},{3,1},{4,5},{5,4},{6,7},{7,6},{8,10},{9,11},{10,... | collective-permute-start | bytes 61448 | tf_op jit(solution)/shard_map/ppermute | solution.py:392
  5.3 2.4 %collective-permute-start.1 = (f32[16,512]{1,0:T(8,128)S(1)}, f32[16,512]{1,0:T(8,128)S(1)}, u32[]{:S(2)}, u32[]{:S(2)}) collective-permute-start(f32[16,512]{1,0:T(8,128)S(1)} %get-tuple-element.23), channel_id=1, source_target_pairs={{0,20},{4,16},{8,28},{12,24},{16,4},{20,0},{24,12},{28,8},{1,21},{... | collective-permute-start | bytes 98312 | tf_op jit(solution)/shard_map/ppermute | solution.py:385
  7.7 1.3 %collective-permute-start.2 = (f32[16,512]{1,0:T(8,128)S(1)}, f32[16,512]{1,0:T(8,128)S(1)}, u32[]{:S(2)}, u32[]{:S(2)}) collective-permute-start(f32[16,512]{1,0:T(8,128)S(1)} %get-tuple-element.24), channel_id=1, source_target_pairs={{0,28},{4,24},{8,20},{12,16},{16,12},{20,8},{24,4},{28,0},{1,29},{... | collective-permute-start | bytes 98312 | tf_op jit(solution)/shard_map/ppermute | solution.py:385
  9.1 0.2 collective-permute-start.3
  9.3 1.6 %collective-permute-start.5 = (bf16[32,640]{1,0:T(8,128)(2,1)S(1)}, bf16[32,640]{1,0:T(8,128)(2,1)S(1)}, u32[]{:S(2)}, u32[]{:S(2)}) collective-permute-start(bf16[32,640]{1,0:T(8,128)(2,1)S(1)} %join.3.near_ref), channel_id=1, source_target_pairs={{0,1},{1,0},{2,3},{3,2},{4,6},{5,7},{6,4},{7,5},{8,9},{9,8},{10,11... | collective-permute-start | bytes 122888 | tf_op jit(solution)/shard_map/ppermute | solution.py:392
  10.8 1.6 %backward_near.1 = (f32[16,512]{1,0:T(8,128)S(1)}, f32[32,512]{1,0:T(8,128)S(1)}, bf16[512,512]{1,0:T(8,128)(2,1)S(1)}, bf16[512,512]{1,0:T(8,128)(2,1)S(1)}) custom-call(bf16[32,640]{1,0:T(8,128)(2,1)S(1)} %join.3.near_ref, bf16[512,512]{1,0:T(8,128)(2,1)} %w2s_hbm.1, bf16[512,512]{1,0:T(8,128)(2,1)} %w2n_hbm.1), custom_call_target="tpu_custom_call" | custom-call | tf_op jit(solution)/shard_map/backward_near/pallas_call | solution.py:224
  12.4 0.6 %collective-permute-done.2.refs_2_ = f32[16,512]{1,0:T(8,128)S(1)} collective-permute-done((f32[16,512]{1,0:T(8,128)S(1)}, f32[16,512]{1,0:T(8,128)S(1)}, u32[]{:S(2)}, u32[]{:S(2)}) %collective-permute-start.2) | collective-permute-done | bytes 32800 | tf_op jit(solution)/shard_map/ppermute | solution.py:385
  13.0 0.3 %collective-permute-done.5.far_ref = bf16[32,640]{1,0:T(8,128)(2,1)S(1)} collective-permute-done((bf16[32,640]{1,0:T(8,128)(2,1)S(1)}, bf16[32,640]{1,0:T(8,128)(2,1)S(1)}, u32[]{:S(2)}, u32[]{:S(2)}) %collective-permute-start.5) | collective-permute-done | bytes 40992 | tf_op jit(solution)/shard_map/ppermute | solution.py:392
  13.4 0.4 %second_backward.1 = (bf16[16,512]{1,0:T(8,128)(2,1)S(1)}, bf16[16,64]{1,0:T(8,128)(2,1)S(1)}, f32[16,128]{1,0:T(8,128)S(1)}) custom-call(bf16[32,640]{1,0:T(8,128)(2,1)S(1)} %join.3.near_ref, bf16[32,640]{1,0:T(8,128)(2,1)S(1)} %collective-permute-done.5.far_ref, f32[16,512]{1,0:T(8,128)S(1)} %get-tuple-element.27.self_ref, ...), custom_call_target="tpu_custom_call" | custom-call | tf_op jit(solution)/shard_map/second_backward/pallas_call | solution.py:298
  13.8 1.4 %collective-permute-start.7 = (bf16[1,16,512]{2,1,0:T(8,128)(2,1)S(1)}, bf16[1,16,512]{2,1,0:T(8,128)(2,1)S(1)}, u32[]{:S(2)}, u32[]{:S(2)}) collective-permute-start(bf16[1,16,512]{2,1,0:T(8,128)(2,1)S(1)} %get-tuple-element.32.a_ref.refs_0_), channel_id=1, source_target_pairs={{0,20},{4,16},{8,28},{12,24},{16,4},{20,0},{24,12},{28,8},{1,21},{... | collective-permute-start | bytes 49160 | tf_op jit(solution)/shard_map/ppermute | solution.py:385
  15.3 1.3 %collective-permute-start.6 = (bf16[16,512]{1,0:T(8,128)(2,1)S(1)}, bf16[16,512]{1,0:T(8,128)(2,1)S(1)}, u32[]{:S(2)}, u32[]{:S(2)}) collective-permute-start(bf16[16,512]{1,0:T(8,128)(2,1)S(1)} %get-tuple-element.31.a_ref.hidden_ref), channel_id=1, source_target_pairs={{0,2},{1,3},{2,0},{3,1},{4,5},{5,4},{6,7},{7,6},{8,10},{9,11},{10,... | collective-permute-start | bytes 49160 | tf_op jit(solution)/shard_map/ppermute | solution.py:392
  16.5 1.4 %collective-permute-done.7.b_ref.refs_1_ = bf16[1,16,512]{2,1,0:T(8,128)(2,1)S(1)} collective-permute-done((bf16[1,16,512]{2,1,0:T(8,128)(2,1)S(1)}, bf16[1,16,512]{2,1,0:T(8,128)(2,1)S(1)}, u32[]{:S(2)}, u32[]{:S(2)}) %collective-permute-start.7) | collective-permute-done | bytes 16416 | tf_op jit(solution)/shard_map/ppermute | solution.py:385
  17.9 0.5 %collective-permute-start.9 = (bf16[2,16,512]{2,1,0:T(8,128)(2,1)S(1)}, bf16[2,16,512]{2,1,0:T(8,128)(2,1)S(1)}, u32[]{:S(2)}, u32[]{:S(2)}) collective-permute-start(bf16[2,16,512]{2,1,0:T(8,128)(2,1)S(1)} %join.4.refs_0_), channel_id=1, source_target_pairs={{0,12},{4,8},{8,4},{12,0},{16,28},{20,24},{24,20},{28,16},{1,13},{... | collective-permute-start | bytes 98312 | tf_op jit(solution)/shard_map/ppermute | solution.py:385
  18.4 0.6 %collective-permute-done.6.b_ref = bf16[16,512]{1,0:T(8,128)(2,1)S(1)} collective-permute-done((bf16[16,512]{1,0:T(8,128)(2,1)S(1)}, bf16[16,512]{1,0:T(8,128)(2,1)S(1)}, u32[]{:S(2)}, u32[]{:S(2)}) %collective-permute-start.6) | collective-permute-done | bytes 16416 | tf_op jit(solution)/shard_map/ppermute | solution.py:392
  19.0 1.8 %collective-permute-start.8 = (bf16[32,512]{1,0:T(8,128)(2,1)S(1)}, bf16[32,512]{1,0:T(8,128)(2,1)S(1)}, u32[]{:S(2)}, u32[]{:S(2)}) collective-permute-start(bf16[32,512]{1,0:T(8,128)(2,1)S(1)} %join.5.near_ref), channel_id=1, source_target_pairs={{0,1},{1,0},{2,3},{3,2},{4,6},{5,7},{6,4},{7,5},{8,9},{9,8},{10,11... | collective-permute-start | bytes 98312 | tf_op jit(solution)/shard_map/ppermute | solution.py:392
  20.8 0.5 %collective-permute-done.9.refs_2_ = bf16[2,16,512]{2,1,0:T(8,128)(2,1)S(1)} collective-permute-done((bf16[2,16,512]{2,1,0:T(8,128)(2,1)S(1)}, bf16[2,16,512]{2,1,0:T(8,128)(2,1)S(1)}, u32[]{:S(2)}, u32[]{:S(2)}) %collective-permute-start.9) | collective-permute-done | bytes 32800 | tf_op jit(solution)/shard_map/ppermute | solution.py:385
  21.3 0.3 %collective-permute-start.12 = (bf16[2,16,512]{2,1,0:T(8,128)(2,1)S(1)}, bf16[2,16,512]{2,1,0:T(8,128)(2,1)S(1)}, u32[]{:S(2)}, u32[]{:S(2)}) collective-permute-start(bf16[2,16,512]{2,1,0:T(8,128)(2,1)S(1)} %collective-permute-done.9.refs_2_), channel_id=1, source_target_pairs={{0,4},{4,0},{8,12},{12,8},{16,20},{20,16},{24,28},{28,24},{1,5},{5... | collective-permute-start | bytes 98312 | tf_op jit(solution)/shard_map/ppermute | solution.py:381
  21.6 0.2 collective-permute-start.10
  21.8 0.3 %collective-permute-start.11 = (bf16[1,16,512]{2,1,0:T(8,128)(2,1)S(1)}, bf16[1,16,512]{2,1,0:T(8,128)(2,1)S(1)}, u32[]{:S(2)}, u32[]{:S(2)}) collective-permute-start(bf16[1,16,512]{2,1,0:T(8,128)(2,1)S(1)} %collective-permute-done.7.b_ref.refs_1_), channel_id=1, source_target_pairs={{0,4},{4,0},{8,12},{12,8},{16,20},{20,16},{24,28},{28,24},{1,5},{5... | collective-permute-start | bytes 49160 | tf_op jit(solution)/shard_map/ppermute | solution.py:381
  22.3 0.5 %collective-permute-done.10.refs_3_ = bf16[1,16,512]{2,1,0:T(8,128)(2,1)S(1)} collective-permute-done((bf16[1,16,512]{2,1,0:T(8,128)(2,1)S(1)}, bf16[1,16,512]{2,1,0:T(8,128)(2,1)S(1)}, u32[]{:S(2)}, u32[]{:S(2)}) %collective-permute-start.10) | collective-permute-done | bytes 16416 | tf_op jit(solution)/shard_map/ppermute | solution.py:381
  22.8 0.2 collective-permute-done.11.refs_4_
  23.0 1.1 %outputs.1 = (bf16[1,1,16,512]{3,2,1,0:T(8,128)(2,1)}, f32[1,128,512]{2,1,0:T(8,128)}, f32[1,128,512]{2,1,0:T(8,128)}) custom-call(bf16[32,512]{1,0:T(8,128)(2,1)S(1)} %join.5.near_ref, bf16[32,512]{1,0:T(8,128)(2,1)S(1)} %collective-permute-done.8.far_ref, bf16[16,64]{1,0:T(8,128)(2,1)S(1)} %get-tuple-element.33.table_ref, ...), custom_call_target="tpu_custom_call" | custom-call | tf_op jit(solution)/shard_map/outputs/pallas_call | solution.py:369
  (13 shorter events, 0.2 us)
Async XLA Ops:
  2.2 3.1 %collective-permute-start = (f32[4,16,512]{2,1,0:T(8,128)S(1)}, f32[4,16,512]{2,1,0:T(8,128)S(1)}, u32[]{:S(2)}, u32[]{:S(2)}) collective-permute-start(f32[4,16,512]{2,1,0:T(8,128)S(1)} %get-tuple-element.21), channel_id=1, source_target_pairs={{0,4},{4,0},{8,12},{12,8},{16,20},{20,16},{24,28},{28,24},{1,5},{5... | collective-permute-start | bytes 393224 | tf_op jit(solution)/shard_map/ppermute | solution.py:381
  2.7 6.6 %collective-permute-start.4 = (bf16[16,640]{1,0:T(8,128)(2,1)S(1)}, bf16[16,640]{1,0:T(8,128)(2,1)S(1)}, u32[]{:S(2)}, u32[]{:S(2)}) collective-permute-start(bf16[16,640]{1,0:T(8,128)(2,1)S(1)} %get-tuple-element.26.a_ref), channel_id=1, source_target_pairs={{0,2},{1,3},{2,0},{3,1},{4,5},{5,4},{6,7},{7,6},{8,10},{9,11},{10,... | collective-permute-start | bytes 61448 | tf_op jit(solution)/shard_map/ppermute | solution.py:392
  5.3 7.1 %collective-permute-start.1 = (f32[16,512]{1,0:T(8,128)S(1)}, f32[16,512]{1,0:T(8,128)S(1)}, u32[]{:S(2)}, u32[]{:S(2)}) collective-permute-start(f32[16,512]{1,0:T(8,128)S(1)} %get-tuple-element.23), channel_id=1, source_target_pairs={{0,20},{4,16},{8,28},{12,24},{16,4},{20,0},{24,12},{28,8},{1,21},{... | collective-permute-start | bytes 98312 | tf_op jit(solution)/shard_map/ppermute | solution.py:385
  7.7 5.3 %collective-permute-start.2 = (f32[16,512]{1,0:T(8,128)S(1)}, f32[16,512]{1,0:T(8,128)S(1)}, u32[]{:S(2)}, u32[]{:S(2)}) collective-permute-start(f32[16,512]{1,0:T(8,128)S(1)} %get-tuple-element.24), channel_id=1, source_target_pairs={{0,28},{4,24},{8,20},{12,16},{16,12},{20,8},{24,4},{28,0},{1,29},{... | collective-permute-start | bytes 98312 | tf_op jit(solution)/shard_map/ppermute | solution.py:385
  9.1 4.0 %collective-permute-start.3 = (f32[16,512]{1,0:T(8,128)S(1)}, f32[16,512]{1,0:T(8,128)S(1)}, u32[]{:S(2)}, u32[]{:S(2)}) collective-permute-start(f32[16,512]{1,0:T(8,128)S(1)} %get-tuple-element.25), channel_id=1, source_target_pairs={{0,12},{4,8},{8,4},{12,0},{16,28},{20,24},{24,20},{28,16},{1,13},{... | collective-permute-start | bytes 98312 | tf_op jit(solution)/shard_map/ppermute | solution.py:385
  9.3 4.1 %collective-permute-start.5 = (bf16[32,640]{1,0:T(8,128)(2,1)S(1)}, bf16[32,640]{1,0:T(8,128)(2,1)S(1)}, u32[]{:S(2)}, u32[]{:S(2)}) collective-permute-start(bf16[32,640]{1,0:T(8,128)(2,1)S(1)} %join.3.near_ref), channel_id=1, source_target_pairs={{0,1},{1,0},{2,3},{3,2},{4,6},{5,7},{6,4},{7,5},{8,9},{9,8},{10,11... | collective-permute-start | bytes 122888 | tf_op jit(solution)/shard_map/ppermute | solution.py:392
  13.8 4.1 %collective-permute-start.7 = (bf16[1,16,512]{2,1,0:T(8,128)(2,1)S(1)}, bf16[1,16,512]{2,1,0:T(8,128)(2,1)S(1)}, u32[]{:S(2)}, u32[]{:S(2)}) collective-permute-start(bf16[1,16,512]{2,1,0:T(8,128)(2,1)S(1)} %get-tuple-element.32.a_ref.refs_0_), channel_id=1, source_target_pairs={{0,20},{4,16},{8,28},{12,24},{16,4},{20,0},{24,12},{28,8},{1,21},{... | collective-permute-start | bytes 49160 | tf_op jit(solution)/shard_map/ppermute | solution.py:385
  15.3 3.7 %collective-permute-start.6 = (bf16[16,512]{1,0:T(8,128)(2,1)S(1)}, bf16[16,512]{1,0:T(8,128)(2,1)S(1)}, u32[]{:S(2)}, u32[]{:S(2)}) collective-permute-start(bf16[16,512]{1,0:T(8,128)(2,1)S(1)} %get-tuple-element.31.a_ref.hidden_ref), channel_id=1, source_target_pairs={{0,2},{1,3},{2,0},{3,1},{4,5},{5,4},{6,7},{7,6},{8,10},{9,11},{10,... | collective-permute-start | bytes 49160 | tf_op jit(solution)/shard_map/ppermute | solution.py:392
  17.9 3.3 %collective-permute-start.9 = (bf16[2,16,512]{2,1,0:T(8,128)(2,1)S(1)}, bf16[2,16,512]{2,1,0:T(8,128)(2,1)S(1)}, u32[]{:S(2)}, u32[]{:S(2)}) collective-permute-start(bf16[2,16,512]{2,1,0:T(8,128)(2,1)S(1)} %join.4.refs_0_), channel_id=1, source_target_pairs={{0,12},{4,8},{8,4},{12,0},{16,28},{20,24},{24,20},{28,16},{1,13},{... | collective-permute-start | bytes 98312 | tf_op jit(solution)/shard_map/ppermute | solution.py:385
  19.0 4.0 %collective-permute-start.8 = (bf16[32,512]{1,0:T(8,128)(2,1)S(1)}, bf16[32,512]{1,0:T(8,128)(2,1)S(1)}, u32[]{:S(2)}, u32[]{:S(2)}) collective-permute-start(bf16[32,512]{1,0:T(8,128)(2,1)S(1)} %join.5.near_ref), channel_id=1, source_target_pairs={{0,1},{1,0},{2,3},{3,2},{4,6},{5,7},{6,4},{7,5},{8,9},{9,8},{10,11... | collective-permute-start | bytes 98312 | tf_op jit(solution)/shard_map/ppermute | solution.py:392
  21.3 1.7 %collective-permute-start.12 = (bf16[2,16,512]{2,1,0:T(8,128)(2,1)S(1)}, bf16[2,16,512]{2,1,0:T(8,128)(2,1)S(1)}, u32[]{:S(2)}, u32[]{:S(2)}) collective-permute-start(bf16[2,16,512]{2,1,0:T(8,128)(2,1)S(1)} %collective-permute-done.9.refs_2_), channel_id=1, source_target_pairs={{0,4},{4,0},{8,12},{12,8},{16,20},{20,16},{24,28},{28,24},{1,5},{5... | collective-permute-start | bytes 98312 | tf_op jit(solution)/shard_map/ppermute | solution.py:381
  21.6 1.2 %collective-permute-start.10 = (bf16[1,16,512]{2,1,0:T(8,128)(2,1)S(1)}, bf16[1,16,512]{2,1,0:T(8,128)(2,1)S(1)}, u32[]{:S(2)}, u32[]{:S(2)}) collective-permute-start(bf16[1,16,512]{2,1,0:T(8,128)(2,1)S(1)} %get-tuple-element.32.a_ref.refs_0_), channel_id=1, source_target_pairs={{0,4},{4,0},{8,12},{12,8},{16,20},{20,16},{24,28},{28,24},{1,5},{5... | collective-permute-start | bytes 49160 | tf_op jit(solution)/shard_map/ppermute | solution.py:381
  21.8 1.2 %collective-permute-start.11 = (bf16[1,16,512]{2,1,0:T(8,128)(2,1)S(1)}, bf16[1,16,512]{2,1,0:T(8,128)(2,1)S(1)}, u32[]{:S(2)}, u32[]{:S(2)}) collective-permute-start(bf16[1,16,512]{2,1,0:T(8,128)(2,1)S(1)} %collective-permute-done.7.b_ref.refs_1_), channel_id=1, source_target_pairs={{0,4},{4,0},{8,12},{12,8},{16,20},{20,16},{24,28},{28,24},{1,5},{5... | collective-permute-start | bytes 49160 | tf_op jit(solution)/shard_map/ppermute | solution.py:381

commit v6 on v3

--- a/solution.py
+++ b/solution.py
@@ -333,7 +333,7 @@
     grad_refs, (both_ref, out_hbm, self_hbm, neigh_hbm) = refs[:-9], refs[-9:-5]
     out_ref, self_ref, neigh_ref, grad_scratch, sems = refs[-5:]
     depth = both_ref.shape[0] // 2
-    half = depth // 2 if depth % 32 == 0 else depth
+    half = depth
     pieces = [(ref, hbm, n, at) for n, (ref, hbm) in enumerate(((self_ref, self_hbm), (neigh_ref, neigh_hbm)))
               for at in range(0, depth, half)]
     pairs = [(ref.at[0, pl.ds(at, half)], hbm.at[0, pl.ds(at, half)]) for ref, hbm, _, at in pieces]
@@ -345,12 +345,6 @@
         for n, code in enumerate(code_list):
             to = pl.multiple_of(lax.bitwise_xor(me, code) * rows, rows)
             grad_scratch[pl.ds(to, rows), :] = ref[n]
-    grad_pre = grad_scratch[...]
-    for (ref, _, n, at), copy in zip(pieces, copies):
-        columns = both_ref[n * depth + at : n * depth + at + half, :]
-        ref[0, at : at + half] = jnp.dot(columns, grad_pre, preferred_element_type=F32)
-        copy.start()
-
     count = near_ref.shape[0]
     neigh_sum = jnp.dot(table_ref[:, :count], near_ref[...], preferred_element_type=F32)
     neigh_sum = neigh_sum + jnp.dot(table_ref[:, count:], far_ref[...], preferred_element_type=F32)
@@ -358,6 +352,11 @@
     out = own_ref[...] + jnp.dot(mean_two, w2n_ref[...], preferred_element_type=F32)
     out_ref[0, 0] = out.astype(BF16)
     copies[-1].start()
+    grad_pre = grad_scratch[...]
+    for (ref, _, n, at), copy in zip(pieces, copies):
+        columns = both_ref[n * depth + at : n * depth + at + half, :]
+        ref[0, at : at + half] = jnp.dot(columns, grad_pre, preferred_element_type=F32)
+        copy.start()
     for copy in copies:
         copy.wait()
 

time: 24.3 us -> 24.5 us (level)
  no operation moved by 1% of the time
where the time goes in v6:
time: 24.5 us; the launch traced here: 24.2 us
  starting transfers between devices  14.4 us (59%)
  Pallas kernels  5.01 us (20%)
  waiting for transfers between devices  4.04 us (16%)
  between operations  0.69 us (3%)
    ppermute x4, starting transfers between devices, swap_peers(): return lax.ppermute(x, ('feat', 'dp'), pairs)  7.22 us
    ppermute x5, starting transfers between devices, swap_chips(): lax.ppermute(x, 'feat', [(i, i ^ 2 * bits + 1) for i in range(lax.axis_si...  5.86 us
    ppermute x5, waiting for transfers between devices, swap_chips(): lax.ppermute(x, 'feat', [(i, i ^ 2 * bits + 1) for i in range(lax.axis_si...  2.47 us
    pallas_call x1, Pallas kernels, backward_near(): pl.pallas_call(near_kernel, in_specs=[VMEM, hbm, hbm], out_specs=[VMEM] *...  1.57 us
    pallas_call x1, Pallas kernels, first_layer(): pl.pallas_call(functools.partial(first_layer_kernel, group // tile), grid...  1.56 us
    ppermute x4, starting transfers between devices, swap_cores(): lax.ppermute(x, 'feat', [(i, i ^ 1) for i in range(lax.axis_size('feat'))])  1.36 us
    pallas_call x1, Pallas kernels, outputs(): pl.pallas_call(functools.partial(outputs_kernel, codes), in_specs=[VMEM]...  1.23 us
    ppermute x4, waiting for transfers between devices, swap_peers(): return lax.ppermute(x, ('feat', 'dp'), pairs)  0.89 us
  transfers between devices with their start and end apart: 13, of which 7 were waited for; matrix products, arithmetic and copies ran while one was open for 0% of the time, Pallas kernels for 7%

profile of v6, /device:TPU:0, one launch (start us, length us, event | category | flops | bytes accessed | tf_op | source)
XLA Modules:
  0.0 24.2 jit_solution(10052077417668657866)
XLA Ops:
  0.6 1.6 %first_layer.1 = (f32[4,16,512]{2,1,0:T(8,128)S(1)}, f32[4,16,512]{2,1,0:T(8,128)S(1)}, bf16[256,128]{1,0:T(8,128)(2,1)S(1)}, bf16[16,640]{1,0:T(8,128)(2,1)S(1)}) custom-call(bf16[1,128,256]{2,1,0:T(8,128)(2,1)} %feat_hbm.1, s32[10,1,128]{2,1,0:T(1,128)} %bitcast.1, bf16[128,512]{1,0:T(8,128)(2,1)} %w1s_hbm.1, bf16[128,512]{1,0:T(8,128)(2,1)} %w1n_hbm.1, ...), custom_call_target="tpu_custom_call" | custom-call | tf_op jit(solution)/shard_map/first_layer/pallas_call | solution.py:134
  2.2 0.5 %collective-permute-start = (f32[4,16,512]{2,1,0:T(8,128)S(1)}, f32[4,16,512]{2,1,0:T(8,128)S(1)}, u32[]{:S(2)}, u32[]{:S(2)}) collective-permute-start(f32[4,16,512]{2,1,0:T(8,128)S(1)} %get-tuple-element.21), channel_id=1, source_target_pairs={{0,4},{4,0},{8,12},{12,8},{16,20},{20,16},{24,28},{28,24},{1,5},{5... | collective-permute-start | bytes 393224 | tf_op jit(solution)/shard_map/ppermute | solution.py:380
  2.7 2.6 %collective-permute-start.4 = (bf16[16,640]{1,0:T(8,128)(2,1)S(1)}, bf16[16,640]{1,0:T(8,128)(2,1)S(1)}, u32[]{:S(2)}, u32[]{:S(2)}) collective-permute-start(bf16[16,640]{1,0:T(8,128)(2,1)S(1)} %get-tuple-element.26.a_ref), channel_id=1, source_target_pairs={{0,1},{1,0},{2,3},{3,2},{4,6},{5,7},{6,4},{7,5},{8,9},{9,8},{10,11... | collective-permute-start | bytes 61448 | tf_op jit(solution)/shard_map/ppermute | solution.py:391
  5.3 2.4 %collective-permute-start.1 = (f32[16,512]{1,0:T(8,128)S(1)}, f32[16,512]{1,0:T(8,128)S(1)}, u32[]{:S(2)}, u32[]{:S(2)}) collective-permute-start(f32[16,512]{1,0:T(8,128)S(1)} %get-tuple-element.23), channel_id=1, source_target_pairs={{0,20},{4,16},{8,28},{12,24},{16,4},{20,0},{24,12},{28,8},{1,21},{... | collective-permute-start | bytes 98312 | tf_op jit(solution)/shard_map/ppermute | solution.py:384
  7.7 1.3 %collective-permute-start.2 = (f32[16,512]{1,0:T(8,128)S(1)}, f32[16,512]{1,0:T(8,128)S(1)}, u32[]{:S(2)}, u32[]{:S(2)}) collective-permute-start(f32[16,512]{1,0:T(8,128)S(1)} %get-tuple-element.24), channel_id=1, source_target_pairs={{0,28},{4,24},{8,20},{12,16},{16,12},{20,8},{24,4},{28,0},{1,29},{... | collective-permute-start | bytes 98312 | tf_op jit(solution)/shard_map/ppermute | solution.py:384
  9.0 0.2 collective-permute-start.3
  9.3 1.6 %collective-permute-start.5 = (bf16[32,640]{1,0:T(8,128)(2,1)S(1)}, bf16[32,640]{1,0:T(8,128)(2,1)S(1)}, u32[]{:S(2)}, u32[]{:S(2)}) collective-permute-start(bf16[32,640]{1,0:T(8,128)(2,1)S(1)} %join.3.near_ref), channel_id=1, source_target_pairs={{0,2},{1,3},{2,0},{3,1},{4,5},{5,4},{6,7},{7,6},{8,10},{9,11},{10,... | collective-permute-start | bytes 122888 | tf_op jit(solution)/shard_map/ppermute | solution.py:391
  10.8 1.6 %backward_near.1 = (f32[16,512]{1,0:T(8,128)S(1)}, f32[32,512]{1,0:T(8,128)S(1)}, bf16[512,512]{1,0:T(8,128)(2,1)S(1)}, bf16[512,512]{1,0:T(8,128)(2,1)S(1)}) custom-call(bf16[32,640]{1,0:T(8,128)(2,1)S(1)} %join.3.near_ref, bf16[512,512]{1,0:T(8,128)(2,1)} %w2s_hbm.1, bf16[512,512]{1,0:T(8,128)(2,1)} %w2n_hbm.1), custom_call_target="tpu_custom_call" | custom-call | tf_op jit(solution)/shard_map/backward_near/pallas_call | solution.py:224
  12.4 0.6 %collective-permute-done.2.refs_2_ = f32[16,512]{1,0:T(8,128)S(1)} collective-permute-done((f32[16,512]{1,0:T(8,128)S(1)}, f32[16,512]{1,0:T(8,128)S(1)}, u32[]{:S(2)}, u32[]{:S(2)}) %collective-permute-start.2) | collective-permute-done | bytes 32800 | tf_op jit(solution)/shard_map/ppermute | solution.py:384
  13.0 0.3 %collective-permute-done.5.far_ref = bf16[32,640]{1,0:T(8,128)(2,1)S(1)} collective-permute-done((bf16[32,640]{1,0:T(8,128)(2,1)S(1)}, bf16[32,640]{1,0:T(8,128)(2,1)S(1)}, u32[]{:S(2)}, u32[]{:S(2)}) %collective-permute-start.5) | collective-permute-done | bytes 40992 | tf_op jit(solution)/shard_map/ppermute | solution.py:391
  13.3 0.4 %second_backward.1 = (bf16[16,512]{1,0:T(8,128)(2,1)S(1)}, bf16[16,64]{1,0:T(8,128)(2,1)S(1)}, f32[16,128]{1,0:T(8,128)S(1)}) custom-call(bf16[32,640]{1,0:T(8,128)(2,1)S(1)} %join.3.near_ref, bf16[32,640]{1,0:T(8,128)(2,1)S(1)} %collective-permute-done.5.far_ref, f32[16,512]{1,0:T(8,128)S(1)} %get-tuple-element.27.self_ref, ...), custom_call_target="tpu_custom_call" | custom-call | tf_op jit(solution)/shard_map/second_backward/pallas_call | solution.py:298
  13.8 1.4 %collective-permute-start.7 = (bf16[1,16,512]{2,1,0:T(8,128)(2,1)S(1)}, bf16[1,16,512]{2,1,0:T(8,128)(2,1)S(1)}, u32[]{:S(2)}, u32[]{:S(2)}) collective-permute-start(bf16[1,16,512]{2,1,0:T(8,128)(2,1)S(1)} %get-tuple-element.32.a_ref.refs_0_), channel_id=1, source_target_pairs={{0,20},{4,16},{8,28},{12,24},{16,4},{20,0},{24,12},{28,8},{1,21},{... | collective-permute-start | bytes 49160 | tf_op jit(solution)/shard_map/ppermute | solution.py:384
  15.2 1.3 %collective-permute-start.6 = (bf16[16,512]{1,0:T(8,128)(2,1)S(1)}, bf16[16,512]{1,0:T(8,128)(2,1)S(1)}, u32[]{:S(2)}, u32[]{:S(2)}) collective-permute-start(bf16[16,512]{1,0:T(8,128)(2,1)S(1)} %get-tuple-element.31.a_ref.hidden_ref), channel_id=1, source_target_pairs={{0,1},{1,0},{2,3},{3,2},{4,6},{5,7},{6,4},{7,5},{8,9},{9,8},{10,11... | collective-permute-start | bytes 49160 | tf_op jit(solution)/shard_map/ppermute | solution.py:391
  16.5 1.4 %collective-permute-done.7.b_ref.refs_1_ = bf16[1,16,512]{2,1,0:T(8,128)(2,1)S(1)} collective-permute-done((bf16[1,16,512]{2,1,0:T(8,128)(2,1)S(1)}, bf16[1,16,512]{2,1,0:T(8,128)(2,1)S(1)}, u32[]{:S(2)}, u32[]{:S(2)}) %collective-permute-start.7) | collective-permute-done | bytes 16416 | tf_op jit(solution)/shard_map/ppermute | solution.py:384
  17.9 0.5 %collective-permute-start.9 = (bf16[2,16,512]{2,1,0:T(8,128)(2,1)S(1)}, bf16[2,16,512]{2,1,0:T(8,128)(2,1)S(1)}, u32[]{:S(2)}, u32[]{:S(2)}) collective-permute-start(bf16[2,16,512]{2,1,0:T(8,128)(2,1)S(1)} %join.4.refs_0_), channel_id=1, source_target_pairs={{0,12},{4,8},{8,4},{12,0},{16,28},{20,24},{24,20},{28,16},{1,13},{... | collective-permute-start | bytes 98312 | tf_op jit(solution)/shard_map/ppermute | solution.py:384
  18.4 0.6 %collective-permute-done.6.b_ref = bf16[16,512]{1,0:T(8,128)(2,1)S(1)} collective-permute-done((bf16[16,512]{1,0:T(8,128)(2,1)S(1)}, bf16[16,512]{1,0:T(8,128)(2,1)S(1)}, u32[]{:S(2)}, u32[]{:S(2)}) %collective-permute-start.6) | collective-permute-done | bytes 16416 | tf_op jit(solution)/shard_map/ppermute | solution.py:391
  19.0 1.8 %collective-permute-start.8 = (bf16[32,512]{1,0:T(8,128)(2,1)S(1)}, bf16[32,512]{1,0:T(8,128)(2,1)S(1)}, u32[]{:S(2)}, u32[]{:S(2)}) collective-permute-start(bf16[32,512]{1,0:T(8,128)(2,1)S(1)} %join.5.near_ref), channel_id=1, source_target_pairs={{0,2},{1,3},{2,0},{3,1},{4,5},{5,4},{6,7},{7,6},{8,10},{9,11},{10,... | collective-permute-start | bytes 98312 | tf_op jit(solution)/shard_map/ppermute | solution.py:391
  20.8 0.5 %collective-permute-done.9.refs_2_ = bf16[2,16,512]{2,1,0:T(8,128)(2,1)S(1)} collective-permute-done((bf16[2,16,512]{2,1,0:T(8,128)(2,1)S(1)}, bf16[2,16,512]{2,1,0:T(8,128)(2,1)S(1)}, u32[]{:S(2)}, u32[]{:S(2)}) %collective-permute-start.9) | collective-permute-done | bytes 32800 | tf_op jit(solution)/shard_map/ppermute | solution.py:384
  21.3 0.3 %collective-permute-start.12 = (bf16[2,16,512]{2,1,0:T(8,128)(2,1)S(1)}, bf16[2,16,512]{2,1,0:T(8,128)(2,1)S(1)}, u32[]{:S(2)}, u32[]{:S(2)}) collective-permute-start(bf16[2,16,512]{2,1,0:T(8,128)(2,1)S(1)} %collective-permute-done.9.refs_2_), channel_id=1, source_target_pairs={{0,4},{4,0},{8,12},{12,8},{16,20},{20,16},{24,28},{28,24},{1,5},{5... | collective-permute-start | bytes 98312 | tf_op jit(solution)/shard_map/ppermute | solution.py:380
  21.6 0.2 collective-permute-start.10
  21.8 0.3 %collective-permute-start.11 = (bf16[1,16,512]{2,1,0:T(8,128)(2,1)S(1)}, bf16[1,16,512]{2,1,0:T(8,128)(2,1)S(1)}, u32[]{:S(2)}, u32[]{:S(2)}) collective-permute-start(bf16[1,16,512]{2,1,0:T(8,128)(2,1)S(1)} %collective-permute-done.7.b_ref.refs_1_), channel_id=1, source_target_pairs={{0,4},{4,0},{8,12},{12,8},{16,20},{20,16},{24,28},{28,24},{1,5},{5... | collective-permute-start | bytes 49160 | tf_op jit(solution)/shard_map/ppermute | solution.py:380
  22.3 0.5 %collective-permute-done.10.refs_3_ = bf16[1,16,512]{2,1,0:T(8,128)(2,1)S(1)} collective-permute-done((bf16[1,16,512]{2,1,0:T(8,128)(2,1)S(1)}, bf16[1,16,512]{2,1,0:T(8,128)(2,1)S(1)}, u32[]{:S(2)}, u32[]{:S(2)}) %collective-permute-start.10) | collective-permute-done | bytes 16416 | tf_op jit(solution)/shard_map/ppermute | solution.py:380
  22.8 0.2 collective-permute-done.11.refs_4_
  23.0 1.2 %outputs.1 = (bf16[1,1,16,512]{3,2,1,0:T(8,128)(2,1)}, f32[1,128,512]{2,1,0:T(8,128)}, f32[1,128,512]{2,1,0:T(8,128)}) custom-call(bf16[32,512]{1,0:T(8,128)(2,1)S(1)} %join.5.near_ref, bf16[32,512]{1,0:T(8,128)(2,1)S(1)} %collective-permute-done.8.far_ref, bf16[16,64]{1,0:T(8,128)(2,1)S(1)} %get-tuple-element.33.table_ref, ...), custom_call_target="tpu_custom_call" | custom-call | tf_op jit(solution)/shard_map/outputs/pallas_call | solution.py:368
  (13 shorter events, 0.2 us)
Async XLA Ops:
  2.2 3.1 %collective-permute-start = (f32[4,16,512]{2,1,0:T(8,128)S(1)}, f32[4,16,512]{2,1,0:T(8,128)S(1)}, u32[]{:S(2)}, u32[]{:S(2)}) collective-permute-start(f32[4,16,512]{2,1,0:T(8,128)S(1)} %get-tuple-element.21), channel_id=1, source_target_pairs={{0,4},{4,0},{8,12},{12,8},{16,20},{20,16},{24,28},{28,24},{1,5},{5... | collective-permute-start | bytes 393224 | tf_op jit(solution)/shard_map/ppermute | solution.py:380
  2.7 6.5 %collective-permute-start.4 = (bf16[16,640]{1,0:T(8,128)(2,1)S(1)}, bf16[16,640]{1,0:T(8,128)(2,1)S(1)}, u32[]{:S(2)}, u32[]{:S(2)}) collective-permute-start(bf16[16,640]{1,0:T(8,128)(2,1)S(1)} %get-tuple-element.26.a_ref), channel_id=1, source_target_pairs={{0,1},{1,0},{2,3},{3,2},{4,6},{5,7},{6,4},{7,5},{8,9},{9,8},{10,11... | collective-permute-start | bytes 61448 | tf_op jit(solution)/shard_map/ppermute | solution.py:391
  5.3 7.1 %collective-permute-start.1 = (f32[16,512]{1,0:T(8,128)S(1)}, f32[16,512]{1,0:T(8,128)S(1)}, u32[]{:S(2)}, u32[]{:S(2)}) collective-permute-start(f32[16,512]{1,0:T(8,128)S(1)} %get-tuple-element.23), channel_id=1, source_target_pairs={{0,20},{4,16},{8,28},{12,24},{16,4},{20,0},{24,12},{28,8},{1,21},{... | collective-permute-start | bytes 98312 | tf_op jit(solution)/shard_map/ppermute | solution.py:384
  7.7 5.3 %collective-permute-start.2 = (f32[16,512]{1,0:T(8,128)S(1)}, f32[16,512]{1,0:T(8,128)S(1)}, u32[]{:S(2)}, u32[]{:S(2)}) collective-permute-start(f32[16,512]{1,0:T(8,128)S(1)} %get-tuple-element.24), channel_id=1, source_target_pairs={{0,28},{4,24},{8,20},{12,16},{16,12},{20,8},{24,4},{28,0},{1,29},{... | collective-permute-start | bytes 98312 | tf_op jit(solution)/shard_map/ppermute | solution.py:384
  9.0 4.0 %collective-permute-start.3 = (f32[16,512]{1,0:T(8,128)S(1)}, f32[16,512]{1,0:T(8,128)S(1)}, u32[]{:S(2)}, u32[]{:S(2)}) collective-permute-start(f32[16,512]{1,0:T(8,128)S(1)} %get-tuple-element.25), channel_id=1, source_target_pairs={{0,12},{4,8},{8,4},{12,0},{16,28},{20,24},{24,20},{28,16},{1,13},{... | collective-permute-start | bytes 98312 | tf_op jit(solution)/shard_map/ppermute | solution.py:384
  9.3 4.1 %collective-permute-start.5 = (bf16[32,640]{1,0:T(8,128)(2,1)S(1)}, bf16[32,640]{1,0:T(8,128)(2,1)S(1)}, u32[]{:S(2)}, u32[]{:S(2)}) collective-permute-start(bf16[32,640]{1,0:T(8,128)(2,1)S(1)} %join.3.near_ref), channel_id=1, source_target_pairs={{0,2},{1,3},{2,0},{3,1},{4,5},{5,4},{6,7},{7,6},{8,10},{9,11},{10,... | collective-permute-start | bytes 122888 | tf_op jit(solution)/shard_map/ppermute | solution.py:391
  13.8 4.1 %collective-permute-start.7 = (bf16[1,16,512]{2,1,0:T(8,128)(2,1)S(1)}, bf16[1,16,512]{2,1,0:T(8,128)(2,1)S(1)}, u32[]{:S(2)}, u32[]{:S(2)}) collective-permute-start(bf16[1,16,512]{2,1,0:T(8,128)(2,1)S(1)} %get-tuple-element.32.a_ref.refs_0_), channel_id=1, source_target_pairs={{0,20},{4,16},{8,28},{12,24},{16,4},{20,0},{24,12},{28,8},{1,21},{... | collective-permute-start | bytes 49160 | tf_op jit(solution)/shard_map/ppermute | solution.py:384
  15.2 3.7 %collective-permute-start.6 = (bf16[16,512]{1,0:T(8,128)(2,1)S(1)}, bf16[16,512]{1,0:T(8,128)(2,1)S(1)}, u32[]{:S(2)}, u32[]{:S(2)}) collective-permute-start(bf16[16,512]{1,0:T(8,128)(2,1)S(1)} %get-tuple-element.31.a_ref.hidden_ref), channel_id=1, source_target_pairs={{0,1},{1,0},{2,3},{3,2},{4,6},{5,7},{6,4},{7,5},{8,9},{9,8},{10,11... | collective-permute-start | bytes 49160 | tf_op jit(solution)/shard_map/ppermute | solution.py:391
  17.9 3.3 %collective-permute-start.9 = (bf16[2,16,512]{2,1,0:T(8,128)(2,1)S(1)}, bf16[2,16,512]{2,1,0:T(8,128)(2,1)S(1)}, u32[]{:S(2)}, u32[]{:S(2)}) collective-permute-start(bf16[2,16,512]{2,1,0:T(8,128)(2,1)S(1)} %join.4.refs_0_), channel_id=1, source_target_pairs={{0,12},{4,8},{8,4},{12,0},{16,28},{20,24},{24,20},{28,16},{1,13},{... | collective-permute-start | bytes 98312 | tf_op jit(solution)/shard_map/ppermute | solution.py:384
  19.0 4.0 %collective-permute-start.8 = (bf16[32,512]{1,0:T(8,128)(2,1)S(1)}, bf16[32,512]{1,0:T(8,128)(2,1)S(1)}, u32[]{:S(2)}, u32[]{:S(2)}) collective-permute-start(bf16[32,512]{1,0:T(8,128)(2,1)S(1)} %join.5.near_ref), channel_id=1, source_target_pairs={{0,2},{1,3},{2,0},{3,1},{4,5},{5,4},{6,7},{7,6},{8,10},{9,11},{10,... | collective-permute-start | bytes 98312 | tf_op jit(solution)/shard_map/ppermute | solution.py:391
  21.3 1.7 %collective-permute-start.12 = (bf16[2,16,512]{2,1,0:T(8,128)(2,1)S(1)}, bf16[2,16,512]{2,1,0:T(8,128)(2,1)S(1)}, u32[]{:S(2)}, u32[]{:S(2)}) collective-permute-start(bf16[2,16,512]{2,1,0:T(8,128)(2,1)S(1)} %collective-permute-done.9.refs_2_), channel_id=1, source_target_pairs={{0,4},{4,0},{8,12},{12,8},{16,20},{20,16},{24,28},{28,24},{1,5},{5... | collective-permute-start | bytes 98312 | tf_op jit(solution)/shard_map/ppermute | solution.py:380
  21.6 1.2 %collective-permute-start.10 = (bf16[1,16,512]{2,1,0:T(8,128)(2,1)S(1)}, bf16[1,16,512]{2,1,0:T(8,128)(2,1)S(1)}, u32[]{:S(2)}, u32[]{:S(2)}) collective-permute-start(bf16[1,16,512]{2,1,0:T(8,128)(2,1)S(1)} %get-tuple-element.32.a_ref.refs_0_), channel_id=1, source_target_pairs={{0,4},{4,0},{8,12},{12,8},{16,20},{20,16},{24,28},{28,24},{1,5},{5... | collective-permute-start | bytes 49160 | tf_op jit(solution)/shard_map/ppermute | solution.py:380
  21.8 1.2 %collective-permute-start.11 = (bf16[1,16,512]{2,1,0:T(8,128)(2,1)S(1)}, bf16[1,16,512]{2,1,0:T(8,128)(2,1)S(1)}, u32[]{:S(2)}, u32[]{:S(2)}) collective-permute-start(bf16[1,16,512]{2,1,0:T(8,128)(2,1)S(1)} %collective-permute-done.7.b_ref.refs_1_), channel_id=1, source_target_pairs={{0,4},{4,0},{8,12},{12,8},{16,20},{20,16},{24,28},{28,24},{1,5},{5... | collective-permute-start | bytes 49160 | tf_op jit(solution)/shard_map/ppermute | solution.py:380
